TPU v7x, 32 devices: a whole 2x2x4 slice. The times are simulated.
32 devices in a mesh: seq: 8 (over y, x, core), fsdp: 4 (over z).
Axes of the slice: x: 2, y: 2, z: 4, core: 2. Of those that a mesh axis runs over, the one named last changes fastest.
Arguments:
- tokens: bfloat16 [8, 1024, 2048], P('fsdp', 'seq'), may hold values from -6 to 6
- doc_starts: int32 [8, 4], P('fsdp'), may hold values from 0 to 1023, as said below
- w_query: bfloat16 [2048, 2048], P(('seq', 'fsdp')), may hold values from -0.1875 to 0.1875
- w_kv: bfloat16 [2048, 256], P(('seq', 'fsdp')), may hold values from -0.125 to 0.125
- w_out: bfloat16 [2048, 2048], P(('seq', 'fsdp')), may hold values from -1.5 to 1.5
- w_fc: bfloat16 [2048, 8192], P(('seq', 'fsdp')), may hold values from -0.125 to 0.125
- w_proj: bfloat16 [8192, 2048], P(('seq', 'fsdp')), may hold values from -0.0625 to 0.0625
- ln1_gain: float32 [2048], replicated, may hold values from 0.5 to 1.5
- ln1_bias: float32 [2048], replicated, may hold values from -1.2 to 1.2
- b_query: float32 [2048], replicated, may hold values from -3 to 3
- b_value: float32 [128], replicated, may hold values from -0.12 to 0.12
- b_out: float32 [2048], replicated, may hold values from -1.2 to 1.2
- ln2_gain: float32 [2048], replicated, may hold values from 0.5 to 1.5
- ln2_bias: float32 [2048], replicated, may hold values from -1.2 to 1.2
- b_fc: float32 [8192], replicated, may hold values from -3 to 3
- b_proj: float32 [2048], replicated, may hold values from -1.2 to 1.2
- cotangent: bfloat16 [8, 1024, 2048], P('fsdp', 'seq'), may hold values from -6 to 6
Outputs:
- output: float32 [8, 1024, 2048], P('fsdp', 'seq')
- input_grad: float32 [8, 1024, 2048], P('fsdp', 'seq')
- grad_w_query: float32 [2048, 2048], P(('seq', 'fsdp'))
- grad_w_kv: float32 [2048, 256], P(('seq', 'fsdp'))
- grad_w_out: float32 [2048, 2048], P(('seq', 'fsdp'))
- grad_w_fc: float32 [2048, 8192], P(('seq', 'fsdp'))
- grad_w_proj: float32 [8192, 2048], P(('seq', 'fsdp'))
- grad_ln1_gain: float32 [2048], replicated
- grad_ln1_bias: float32 [2048], replicated
- grad_b_query: float32 [2048], replicated
- grad_b_value: float32 [128], replicated
- grad_b_out: float32 [2048], replicated
- grad_ln2_gain: float32 [2048], replicated
- grad_ln2_bias: float32 [2048], replicated
- grad_b_fc: float32 [8192], replicated
- grad_b_proj: float32 [2048], replicated
Inputs may be any that keep to these rules, and one draw needn't show every extreme that they name: `doc_starts`: positions at which documents of a stream start, in any order, repeats allowed; position 0 and position 1023 are always listed. Token t of stream b belongs to the document begun by the latest listed start at or before t.
All inputs are finite; a program needn't handle non-finite values.
Results may differ from a plain program's by a relative error of at most 0.02.
Values may be sent and summed in bfloat16 or wider, within the bound.
A program may use at most 384 MiB of HBM per device.

v0:
```python
import jax
import jax.numpy as jnp
from jax import lax
from jax.sharding import PartitionSpec as P

HEADS = 16
HD = 128


root_two_pi = 0.7978845608028654
cubic_coef = 0.044715
epsilon = 1e-05


def normalize(values, gain_row, shift_row):
    center = values - jnp.mean(values, axis=-1, keepdims=True)
    inverse = lax.rsqrt(jnp.mean(center * center, axis=-1, keepdims=True) + epsilon)
    normed = center * inverse
    return (normed * gain_row + shift_row, normed, inverse)


def normalize_back(grad_out, normed, inverse, gain_row):
    scaled = grad_out * gain_row
    grad_in = inverse * (
        scaled
        - jnp.mean(scaled, axis=-1, keepdims=True)
        - normed * jnp.mean(scaled * normed, axis=-1, keepdims=True)
    )
    return (grad_in, jnp.sum(grad_out * normed, axis=0), jnp.sum(grad_out, axis=0))


def gelu_pair(inputs):
    tangent = jnp.tanh(root_two_pi * (inputs + cubic_coef * inputs * inputs * inputs))
    activated = 0.5 * inputs * (1.0 + tangent)
    gradient_slope = 0.5 * (1.0 + tangent) + 0.5 * inputs * (
        1.0 - tangent * tangent
    ) * root_two_pi * (1.0 + 3.0 * cubic_coef * inputs * inputs)
    return (activated, gradient_slope)


def shards(
    tokens,
    doc_starts,
    w_query,
    w_kv,
    w_out,
    w_fc,
    w_proj,
    ln1_gain,
    ln1_bias,
    b_query,
    b_value,
    b_out,
    ln2_gain,
    ln2_bias,
    b_fc,
    b_proj,
    cotangent,
):
    part_query, part_kv, part_out, part_fc, part_proj = (
        lax.all_gather(w_query, "fsdp", axis=0, tiled=True),
        lax.all_gather(w_kv, "fsdp", axis=0, tiled=True),
        lax.all_gather(w_out, "fsdp", axis=0, tiled=True),
        lax.all_gather(w_fc, "fsdp", axis=0, tiled=True),
        lax.all_gather(w_proj, "fsdp", axis=0, tiled=True),
    )
    full_query, full_kv, full_out, full_fc, full_proj = (
        lax.all_gather(part_query, "seq", axis=0, tiled=True),
        lax.all_gather(part_kv, "seq", axis=0, tiled=True),
        lax.all_gather(part_out, "seq", axis=0, tiled=True),
        lax.all_gather(part_fc, "seq", axis=0, tiled=True),
        lax.all_gather(part_proj, "seq", axis=0, tiled=True),
    )
    local_streams = tokens.shape[0]
    local_rows = tokens.shape[1]
    width = tokens.shape[2]
    groups = lax.axis_size("seq")
    local_heads = HEADS // groups
    length = groups * local_rows
    block_rows = min(512, length)
    block_count = length // block_rows
    score_scale = HD ** (-0.5)
    position = jnp.arange(length, dtype=jnp.int32)
    segments = jnp.sum(
        (doc_starts[:, None, :] <= position[None, :, None]).astype(jnp.int32), axis=2
    )
    inputs = tokens.reshape(local_streams * local_rows, width).astype(jnp.float32)
    shifted1, normed1, inverse1 = normalize(inputs, ln1_gain, ln1_bias)
    hidden1 = shifted1.astype(jnp.bfloat16)
    queries = (jnp.dot(hidden1, full_query, preferred_element_type=jnp.float32) + b_query).astype(
        jnp.bfloat16
    )
    value_shift = jnp.concatenate([jnp.zeros((HD,), jnp.float32), b_value])
    keyval = (jnp.dot(hidden1, full_kv, preferred_element_type=jnp.float32) + value_shift).astype(
        jnp.bfloat16
    )
    head_queries = lax.all_to_all(
        queries.reshape(local_streams, local_rows, HEADS, HD),
        "seq",
        split_axis=2,
        concat_axis=1,
        tiled=True,
    )
    keyval_all = lax.all_gather(
        keyval.reshape(local_streams, local_rows, 2 * HD), "seq", axis=1, tiled=True
    )

    def block_scores(query_block, key_rows, segment, row_start):
        raw_scores = (
            jnp.einsum("thd,ud->htu", query_block, key_rows, preferred_element_type=jnp.float32)
            * score_scale
        )
        query_pos = row_start + jnp.arange(block_rows, dtype=jnp.int32)
        query_seg = lax.dynamic_slice_in_dim(segment, row_start, block_rows, 0)
        allowed = (position[None, :] <= query_pos[:, None]) & (
            segment[None, :] == query_seg[:, None]
        )
        return jnp.where(allowed[None], raw_scores, -1e30)

    mixed_list = []
    total_list = []
    for stream in range(local_streams):
        forward_stream_queries = head_queries[stream]
        forward_stream_kv = keyval_all[stream]
        forward_segment = segments[stream]
        forward_key_rows = forward_stream_kv[:, :HD]
        forward_value_rows = forward_stream_kv[:, HD:]

        def attend(block_index):
            row_start = block_index * block_rows
            query_block = lax.dynamic_slice_in_dim(forward_stream_queries, row_start, block_rows, 0)
            scores = block_scores(query_block, forward_key_rows, forward_segment, row_start)
            row_max = jnp.max(scores, axis=-1, keepdims=True)
            log_total = row_max + jnp.log(
                jnp.sum(jnp.exp(scores - row_max), axis=-1, keepdims=True)
            )
            attention = jnp.exp(scores - log_total).astype(jnp.bfloat16)
            mixed_block = jnp.einsum(
                "htu,ud->thd", attention, forward_value_rows, preferred_element_type=jnp.float32
            )
            return (mixed_block.astype(jnp.bfloat16), log_total[..., 0])

        forward_block_ids = jnp.arange(block_count, dtype=jnp.int32)
        mixed_blocks, forward_log_totals = lax.map(attend, forward_block_ids)
        mixed_one = mixed_blocks.reshape(length, local_heads, HD)
        mixed_list.append(mixed_one)
        total_list.append(forward_log_totals)
    mixed_heads = jnp.stack(mixed_list)
    mixed = lax.all_to_all(mixed_heads, "seq", split_axis=1, concat_axis=2, tiled=True).reshape(
        local_streams * local_rows, HEADS * HD
    )
    residual = inputs + jnp.dot(mixed, full_out, preferred_element_type=jnp.float32) + b_out
    shifted2, normed2, inverse2 = normalize(residual, ln2_gain, ln2_bias)
    hidden2 = shifted2.astype(jnp.bfloat16)
    pre_act = jnp.dot(hidden2, full_fc, preferred_element_type=jnp.float32) + b_fc
    activated, gradient_slope = gelu_pair(pre_act)
    act_low = activated.astype(jnp.bfloat16)
    output = residual + jnp.dot(act_low, full_proj, preferred_element_type=jnp.float32) + b_proj
    cot_low = cotangent.reshape(local_streams * local_rows, width)
    cot_full = cot_low.astype(jnp.float32)
    grad_b_proj = jnp.sum(cot_full, axis=0)
    grad_w_proj = jnp.einsum("tf,td->fd", act_low, cot_low, preferred_element_type=jnp.float32)
    grad_act = jnp.einsum("td,fd->tf", cot_low, full_proj, preferred_element_type=jnp.float32)
    grad_pre = (grad_act * gradient_slope).astype(jnp.bfloat16)
    grad_b_fc = jnp.sum(grad_pre.astype(jnp.float32), axis=0)
    grad_w_fc = jnp.einsum("td,tf->df", hidden2, grad_pre, preferred_element_type=jnp.float32)
    grad_hidden2 = jnp.einsum("tf,df->td", grad_pre, full_fc, preferred_element_type=jnp.float32)
    back_second, grad_ln2_gain, grad_ln2_bias = normalize_back(
        grad_hidden2, normed2, inverse2, ln2_gain
    )
    grad_residual = cot_full + back_second
    grad_attn = grad_residual.astype(jnp.bfloat16)
    grad_b_out = jnp.sum(grad_attn.astype(jnp.float32), axis=0)
    grad_w_out = jnp.einsum("td,te->de", mixed, grad_attn, preferred_element_type=jnp.float32)
    grad_mixed = jnp.einsum(
        "te,de->td", grad_attn, full_out, preferred_element_type=jnp.float32
    ).astype(jnp.bfloat16)
    grad_heads = lax.all_to_all(
        grad_mixed.reshape(local_streams, local_rows, HEADS, HD),
        "seq",
        split_axis=2,
        concat_axis=1,
        tiled=True,
    )
    kv_grad_list = []
    query_grad_list = []
    for stream in range(local_streams):
        stream_queries = head_queries[stream]
        stream_grads = grad_heads[stream]
        stream_kv = keyval_all[stream]
        backward_segment = segments[stream]
        backward_key_rows = stream_kv[:, :HD]
        value_rows = stream_kv[:, HD:]

        def attend_back(grad_pair, block_item):
            block_index, log_total = block_item
            grad_key_rows, grad_value_rows = grad_pair
            row_start = block_index * block_rows
            query_block = lax.dynamic_slice_in_dim(stream_queries, row_start, block_rows, 0)
            grad_block = lax.dynamic_slice_in_dim(stream_grads, row_start, block_rows, 0)
            scores = block_scores(query_block, backward_key_rows, backward_segment, row_start)
            probs = jnp.exp(scores - log_total[..., None])
            probs_low = probs.astype(jnp.bfloat16)
            grad_probs = jnp.einsum(
                "thd,ud->htu", grad_block, value_rows, preferred_element_type=jnp.float32
            )
            delta = jnp.sum(probs * grad_probs, axis=-1, keepdims=True)
            grad_scores = (probs * (grad_probs - delta)).astype(jnp.bfloat16)
            grad_query_block = (
                jnp.einsum(
                    "htu,ud->thd",
                    grad_scores,
                    backward_key_rows,
                    preferred_element_type=jnp.float32,
                )
                * score_scale
            ).astype(jnp.bfloat16)
            grad_key_rows = (
                grad_key_rows
                + jnp.einsum(
                    "htu,thd->ud", grad_scores, query_block, preferred_element_type=jnp.float32
                )
                * score_scale
            )
            grad_value_rows = grad_value_rows + jnp.einsum(
                "htu,thd->ud", probs_low, grad_block, preferred_element_type=jnp.float32
            )
            return ((grad_key_rows, grad_value_rows), grad_query_block)

        block_ids = jnp.arange(block_count, dtype=jnp.int32)
        zero_rows = jnp.zeros((length, HD), jnp.float32)
        (grad_key_rows, grad_value_rows), grad_query_blocks = lax.scan(
            attend_back, (zero_rows, zero_rows), (block_ids, total_list[stream])
        )
        kv_one = jnp.concatenate([grad_key_rows, grad_value_rows], axis=1)
        query_one = grad_query_blocks.reshape(length, local_heads, HD)
        kv_grad_list.append(kv_one)
        query_grad_list.append(query_one)
    grad_query_heads = jnp.stack(query_grad_list)
    grad_queries = lax.all_to_all(
        grad_query_heads, "seq", split_axis=1, concat_axis=2, tiled=True
    ).reshape(local_streams * local_rows, HEADS * HD)
    grad_keyval_sum = lax.psum_scatter(
        jnp.stack(kv_grad_list).astype(jnp.bfloat16), "seq", scatter_dimension=1, tiled=True
    ).astype(jnp.float32)
    grad_keyval = grad_keyval_sum.reshape(local_streams * local_rows, 2 * HD).astype(jnp.bfloat16)
    grad_b_query = jnp.sum(grad_queries.astype(jnp.float32), axis=0)
    grad_b_value = jnp.sum(grad_keyval[:, HD:].astype(jnp.float32), axis=0)
    grad_w_query = jnp.einsum(
        "td,te->de", hidden1, grad_queries, preferred_element_type=jnp.float32
    )
    grad_w_kv = jnp.einsum("td,te->de", hidden1, grad_keyval, preferred_element_type=jnp.float32)
    grad_hidden1 = jnp.einsum(
        "te,de->td", grad_queries, full_query, preferred_element_type=jnp.float32
    ) + jnp.einsum("te,de->td", grad_keyval, full_kv, preferred_element_type=jnp.float32)
    back_first, grad_ln1_gain, grad_ln1_bias = normalize_back(
        grad_hidden1, normed1, inverse1, ln1_gain
    )
    input_grad = grad_residual + back_first
    outer_query, outer_kv, outer_out, outer_fc, outer_proj = (
        lax.psum_scatter(
            grad_w_query.astype(jnp.bfloat16), "seq", scatter_dimension=0, tiled=True
        ).astype(jnp.float32),
        lax.psum_scatter(
            grad_w_kv.astype(jnp.bfloat16), "seq", scatter_dimension=0, tiled=True
        ).astype(jnp.float32),
        lax.psum_scatter(
            grad_w_out.astype(jnp.bfloat16), "seq", scatter_dimension=0, tiled=True
        ).astype(jnp.float32),
        lax.psum_scatter(
            grad_w_fc.astype(jnp.bfloat16), "seq", scatter_dimension=0, tiled=True
        ).astype(jnp.float32),
        lax.psum_scatter(
            grad_w_proj.astype(jnp.bfloat16), "seq", scatter_dimension=0, tiled=True
        ).astype(jnp.float32),
    )
    shard_query, shard_kv, shard_out, shard_fc, shard_proj = (
        lax.psum_scatter(
            outer_query.astype(jnp.bfloat16), "fsdp", scatter_dimension=0, tiled=True
        ).astype(jnp.float32),
        lax.psum_scatter(
            outer_kv.astype(jnp.bfloat16), "fsdp", scatter_dimension=0, tiled=True
        ).astype(jnp.float32),
        lax.psum_scatter(
            outer_out.astype(jnp.bfloat16), "fsdp", scatter_dimension=0, tiled=True
        ).astype(jnp.float32),
        lax.psum_scatter(
            outer_fc.astype(jnp.bfloat16), "fsdp", scatter_dimension=0, tiled=True
        ).astype(jnp.float32),
        lax.psum_scatter(
            outer_proj.astype(jnp.bfloat16), "fsdp", scatter_dimension=0, tiled=True
        ).astype(jnp.float32),
    )
    vector_sums = lax.psum(
        (
            grad_ln1_gain,
            grad_ln1_bias,
            grad_b_query,
            grad_b_value,
            grad_b_out,
            grad_ln2_gain,
            grad_ln2_bias,
            grad_b_fc,
            grad_b_proj,
        ),
        ("seq", "fsdp"),
    )
    return (
        output.reshape(local_streams, local_rows, width),
        input_grad.reshape(local_streams, local_rows, width),
        shard_query,
        shard_kv,
        shard_out,
        shard_fc,
        shard_proj,
        vector_sums[0],
        vector_sums[1],
        vector_sums[2],
        vector_sums[3],
        vector_sums[4],
        vector_sums[5],
        vector_sums[6],
        vector_sums[7],
        vector_sums[8],
    )


def solution(mesh):
    return jax.shard_map(
        shards,
        mesh=mesh,
        in_specs=(
            P("fsdp", "seq", None),
            P("fsdp", None),
            P(("seq", "fsdp"), None),
            P(("seq", "fsdp"), None),
            P(("seq", "fsdp"), None),
            P(("seq", "fsdp"), None),
            P(("seq", "fsdp"), None),
            P(),
            P(),
            P(),
            P(),
            P(),
            P(),
            P(),
            P(),
            P(),
            P("fsdp", "seq", None),
        ),
        out_specs=(
            P("fsdp", "seq", None),
            P("fsdp", "seq", None),
            P(("seq", "fsdp"), None),
            P(("seq", "fsdp"), None),
            P(("seq", "fsdp"), None),
            P(("seq", "fsdp"), None),
            P(("seq", "fsdp"), None),
            P(),
            P(),
            P(),
            P(),
            P(),
            P(),
            P(),
            P(),
            P(),
        ),
        check_vma=False,
    )
```

profile of v0, /device:TPU:0, one launch (start us, length us, event | category | flops | bytes accessed | tf_op | source)
XLA Modules:
  0.0 1910.3 jit_solution(10148773197887487337)
XLA Ops:
  43.5 22.0 %all-gather.15.cloned.1.call-done = bf16[2048,256]{1,0:T(8,128)(2,1)} async-done(((bf16[256,256]{1,0:T(8,128)(2,1)}), bf16[2048,256]{1,0:T(8,128)(2,1)}) %all-gather.15.cloned.1.call-update) | async-done | bytes 1048592 | tf_op jit(solution)/shard_map/all_gather | solution.py:69
  67.9 27.1 %all-gather.19.cloned.1.call-done = bf16[256,2048]{1,0:T(8,128)(2,1)} async-done(((bf16[64,2048]{1,0:T(8,128)(2,1)}), bf16[256,2048]{1,0:T(8,128)(2,1)}) %all-gather.19.cloned.1.call-update) | async-done | bytes 1048592 | tf_op jit(solution)/shard_map/all_gather | solution.py:63
  95.1 81.6 %all-gather.23.cloned.1.call-done = bf16[256,8192]{1,0:T(8,128)(2,1)} async-done(((bf16[64,8192]{1,0:T(8,128)(2,1)}), bf16[256,8192]{1,0:T(8,128)(2,1)}) %all-gather.23.cloned.1.call-update) | async-done | bytes 4194320 | tf_op jit(solution)/shard_map/all_gather | solution.py:64
  176.9 80.7 %all-gather.27.cloned.1.call-done = bf16[1024,2048]{1,0:T(8,128)(2,1)} async-done(((bf16[256,2048]{1,0:T(8,128)(2,1)}), bf16[1024,2048]{1,0:T(8,128)(2,1)}) %all-gather.27.cloned.1.call-update) | async-done | bytes 4194320 | tf_op jit(solution)/shard_map/all_gather | solution.py:65
  257.6 54.7 %all-gather.13.cloned.1.call-done = bf16[2048,2048]{1,0:T(8,128)(2,1)} async-done(((bf16[256,2048]{1,0:T(8,128)(2,1)}), bf16[2048,2048]{1,0:T(8,128)(2,1)}) %all-gather.13.cloned.1.call-update) | async-done | bytes 8388624 | tf_op jit(solution)/shard_map/all_gather | solution.py:68
  374.9 30.5 %all_to_all.60 = bf16[2,1024,2,128]{3,2,0,1:T(2,128)(2,1)S(1)} all-to-all(bf16[2,1024,2,128]{3,2,0,1:T(2,128)(2,1)S(1)} %copy.81), channel_id=1, replica_groups=mesh['seq'=8,'fsdp'=4] {'seq'}, dimensions={1} | all-to-all | bytes 2097152 | tf_op jit(solution)/shard_map/all_to_all | solution.py:149
  416.3 155.9 %all-gather.25.cloned.1.call-done = bf16[2048,8192]{1,0:T(8,128)(2,1)} async-done(((bf16[256,8192]{1,0:T(8,128)(2,1)}), bf16[2048,8192]{1,0:T(8,128)(2,1)}) %all-gather.25.cloned.1.call-update) | async-done | bytes 33554448 | tf_op jit(solution)/shard_map/all_gather | solution.py:71
  572.2 20.4 %convolution_add_fusion = f32[256,8192]{1,0:T(8,128)} fusion(bf16[2048,8192]{1,0:T(8,128)(2,1)} %all-gather.25.cloned.1.call-done, f32[8192]{0:T(1024)S(1)} %copy-done.44, f32[256,2048]{1,0:T(8,128)S(1)} %get-tuple-element.524, f32[2048]{0:T(1024)S(1)} %copy-done.29, f32[2048]{0:T(1024)S(1)} %copy-done.27, f32[256]{0:T(256)S(1)} %add_rsqrt_fusion, ...), kind=kOutput, calls=%fused_computation.135 | convolution fusion | flops 8594653184 | bytes 44091392 | tf_op jit(solution)/shard_map/dot_general | solution.py:155
  592.7 142.1 %all-gather.29.cloned.1.call-done = bf16[8192,2048]{1,0:T(8,128)(2,1)} async-done(((bf16[1024,2048]{1,0:T(8,128)(2,1)}), bf16[8192,2048]{1,0:T(8,128)(2,1)}) %all-gather.29.cloned.1.call-update) | async-done | bytes 33554448 | tf_op jit(solution)/shard_map/all_gather | solution.py:72
  734.8 21.4 %convert_reduce_fusion = (f32[8192]{0:T(1024)}, bf16[256,8192]{1,0:T(8,128)(2,1)}) fusion(f32[256,8192]{1,0:T(8,128)} %convolution_add_fusion, bf16[256,2048]{1,0:T(8,128)(2,1)S(1)} %bitcast.395, bf16[8192,2048]{1,0:T(8,128)(2,1)} %all-gather.29.cloned.1.call-done), kind=kOutput, calls=%fused_computation.142 | convolution fusion | flops 8633966592 | bytes 47218688 | tf_op jit(solution)/shard_map/td,fd->tf/dot_general | solution.py:163
  807.9 32.3 %while.59 = (s32[]{:T(128)}, f32[1024,128]{1,0:T(8,128)}, f32[1024,128]{1,0:T(8,128)}, bf16[2,512,2,128]{3,1,0,2:T(8,128)(2,1)}, s32[2]{0:T(128)S(1)}, /*index=5...) while((s32[]{:T(128)}, f32[1024,128]{1,0:T(8,128)}, ...), condition=%wide.region_20.21_spmd.clone, body=%wide.region_18.20_spmd.clone.sunk | while | flops 1360395776 | bytes 79735216 | solution.py:232
  843.0 28.9 %while.58 = (s32[]{:T(128)}, f32[1024,128]{1,0:T(8,128)S(1)}, f32[1024,128]{1,0:T(8,128)}, bf16[2,512,2,128]{3,1,0,2:T(8,128)(2,1)}, s32[2]{0:T(128)S(1)}, /*ind...) while((s32[]{:T(128)}, f32[1024,128]{1,0:T(8,128)S(1)}, ...), condition=%wide.region_17.18_spmd.clone, body=%wide.region_15.17_spmd.clone.sunk | while | flops 1360395776 | bytes 80783824 | solution.py:232
  877.0 34.7 %reduce-scatter.12.cloned.1.call-done = bf16[2,128,256]{2,1,0:T(8,128)(2,1)} async-done(((bf16[2,1024,256]{2,1,0:T(8,128)(2,1)}), bf16[2,128,256]{2,1,0:T(8,128)(2,1)}) %reduce-scatter.12.cloned.1.call-update) | async-done | bytes 131088 | tf_op jit(solution)/shard_map/reduce_scatter | solution.py:243
  924.2 21.1 %all_to_all.61 = bf16[2,1024,2,128]{3,2,0,1:T(2,128)(2,1)S(1)} all-to-all(bf16[2,1024,2,128]{3,2,0,1:T(2,128)(2,1)S(1)} %copy.88), channel_id=1, replica_groups=mesh['seq'=8,'fsdp'=4] {'seq'}, dimensions={1} | all-to-all | bytes 2097152 | tf_op jit(solution)/shard_map/all_to_all | solution.py:240
  979.7 21.3 %convolution_convert_fusion = bf16[8192,2048]{1,0:T(8,128)(2,1)} fusion(bf16[256,2048]{1,0:T(8,128)(2,1)S(1)} %bitcast.396, f32[256,8192]{1,0:T(8,128)} %convolution_add_fusion), kind=kOutput, calls=%fused_computation.130 | convolution fusion | flops 8625586176 | bytes 42991616 | tf_op jit(solution)/shard_map/tf,td->fd/dot_general | solution.py:162
  1001.6 28.5 %reduce-scatter.22.cloned.1.call-done = bf16[256,2048]{1,0:T(8,128)(2,1)} async-done(((bf16[2048,2048]{1,0:T(8,128)(2,1)}), bf16[256,2048]{1,0:T(8,128)(2,1)}) %reduce-scatter.22.cloned.1.call-update) | async-done | bytes 1048592 | tf_op jit(solution)/shard_map/reduce_scatter | solution.py:267
  1030.2 75.0 %reduce-scatter.14.cloned.1.call-done = bf16[256,2048]{1,0:T(8,128)(2,1)} async-done(((bf16[2048,2048]{1,0:T(8,128)(2,1)}), bf16[256,2048]{1,0:T(8,128)(2,1)}) %reduce-scatter.14.cloned.1.call-update) | async-done | bytes 1048592 | tf_op jit(solution)/shard_map/reduce_scatter | solution.py:261
  1105.2 208.6 %reduce-scatter.26.cloned.1.call-done = bf16[256,8192]{1,0:T(8,128)(2,1)} async-done(((bf16[2048,8192]{1,0:T(8,128)(2,1)}), bf16[256,8192]{1,0:T(8,128)(2,1)}) %reduce-scatter.26.cloned.1.call-update) | async-done | bytes 4194320 | tf_op jit(solution)/shard_map/reduce_scatter | solution.py:270
  1313.9 209.1 %reduce-scatter.30.cloned.1.call-done = bf16[1024,2048]{1,0:T(8,128)(2,1)} async-done(((bf16[8192,2048]{1,0:T(8,128)(2,1)}), bf16[1024,2048]{1,0:T(8,128)(2,1)}) %reduce-scatter.30.cloned.1.call-update) | async-done | bytes 4194320 | tf_op jit(solution)/shard_map/reduce_scatter | solution.py:273
  1523.8 20.3 %fusion.132 = f32[256,2048]{1,0:T(8,128)} fusion(f32[256,2048]{1,0:T(8,128)} %copy-done.6, bf16[8192,2048]{1,0:T(8,128)(2,1)} %all-gather.29.cloned.1.call-done, f32[2048]{0:T(1024)S(1)} %copy-done.47, f32[256,8192]{1,0:T(8,128)} %convolution_add_fusion), kind=kOutput, calls=%fused_computation.149 | convolution fusion | flops 8609857536 | bytes 46145536 | tf_op jit(solution)/shard_map/dot_general | solution.py:158
  1573.7 26.3 %reduce-scatter.16.cloned.1.call-done = bf16[64,2048]{1,0:T(8,128)(2,1)} async-done(((bf16[256,2048]{1,0:T(8,128)(2,1)}), bf16[64,2048]{1,0:T(8,128)(2,1)}) %reduce-scatter.16.cloned.1.call-update) | async-done | bytes 262160 | tf_op jit(solution)/shard_map/reduce_scatter | solution.py:278
  1601.8 75.9 %reduce-scatter.28.cloned.1.call-done = bf16[64,8192]{1,0:T(8,128)(2,1)} async-done(((bf16[256,8192]{1,0:T(8,128)(2,1)}), bf16[64,8192]{1,0:T(8,128)(2,1)}) %reduce-scatter.28.cloned.1.call-update) | async-done | bytes 1048592 | tf_op jit(solution)/shard_map/reduce_scatter | solution.py:287
  1680.4 77.0 %reduce-scatter.32.cloned.1.call-done = bf16[256,2048]{1,0:T(8,128)(2,1)} async-done(((bf16[1024,2048]{1,0:T(8,128)(2,1)}), bf16[256,2048]{1,0:T(8,128)(2,1)}) %reduce-scatter.32.cloned.1.call-update) | async-done | bytes 1048592 | tf_op jit(solution)/shard_map/reduce_scatter | solution.py:290
  1760.1 131.6 %all-reduce.4.cloned.1.call-done = (f32[2048]{0:T(1024)}, f32[2048]{0:T(1024)}, f32[2048]{0:T(1024)}, f32[128]{0:T(128)}, f32[2048]{0:T(1024)}, /*index=5*/f32[2...) async-done(((f32[2048]{0:T(1024)}, f32[2048]{0:T(1024)}, f32[2048]{0:T(1024)}, f32[128]{0:T(128)}, f32[2048]{0:T(1024)}, /*index=5*/f32[2048]{0:T(1024)}, ...) | async-done | bytes 90640 | tf_op jit(solution)/shard_map/psum | solution.py:294
  (342 shorter events, 349.4 us)
Async XLA Ops:
  7.2 33.3 %all-gather.11.cloned.1.call-start = ((), (), s32[]{:S(2)}) async-start(), calls=%async_computation.15 | async-start | bytes 1310720 | tf_op jit(solution)/shard_map/all_gather | solution.py:61
  8.0 57.6 %all-gather.15.cloned.1.call-start = ((), (), s32[]{:S(2)}) async-start(), calls=%async_computation.17 | async-start | bytes 1179648 | tf_op jit(solution)/shard_map/all_gather | solution.py:69
  25.4 69.6 %all-gather.19.cloned.1.call-start = ((), (), s32[]{:S(2)}) async-start(), calls=%async_computation.19 | async-start | bytes 1310720 | tf_op jit(solution)/shard_map/all_gather | solution.py:63
  26.2 150.6 %all-gather.23.cloned.1.call-start = ((), (), s32[]{:S(2)}) async-start(), calls=%async_computation.21 | async-start | bytes 5242880 | tf_op jit(solution)/shard_map/all_gather | solution.py:64
  26.8 230.8 %all-gather.27.cloned.1.call-start = ((), (), s32[]{:S(2)}) async-start(), calls=%async_computation.23 | async-start | bytes 5242880 | tf_op jit(solution)/shard_map/all_gather | solution.py:65
  27.3 284.9 %all-gather.13.cloned.1.call-start = ((), (), s32[]{:S(2)}) async-start(), calls=%async_computation.16 | async-start | bytes 9437184 | tf_op jit(solution)/shard_map/all_gather | solution.py:68
  40.5 300.6 %all-gather.17.cloned.1.call-start = ((), (), s32[]{:S(2)}) async-start(), calls=%async_computation.18 | async-start | bytes 1179648 | tf_op jit(solution)/shard_map/all_gather | solution.py:104
  67.9 341.8 %all-gather.21.cloned.1.call-start = ((), (), s32[]{:S(2)}) async-start(), calls=%async_computation.20 | async-start | bytes 9437184 | tf_op jit(solution)/shard_map/all_gather | solution.py:70
  95.1 477.1 %all-gather.25.cloned.1.call-start = ((), (), s32[]{:S(2)}) async-start(), calls=%async_computation.22 | async-start | bytes 37748736 | tf_op jit(solution)/shard_map/all_gather | solution.py:71
  176.8 558.0 %all-gather.29.cloned.1.call-start = ((), (), s32[]{:S(2)}) async-start(), calls=%async_computation.24 | async-start | bytes 37748736 | tf_op jit(solution)/shard_map/all_gather | solution.py:72
  319.5 23.9 %all-to-all-start = ((bf16[2,128,16,128]{3,1,0,2:T(8,128)(2,1)}), bf16[2,128,16,128]{3,1,0,2:T(8,128)(2,1)S(1)}, u32[]{:S(2)}, u32[]{:S(2)}) async-start(bf16[2,128,16,128]{3,1,0,2:T(8,128)(2,1)} %copy.76), calls=%async_computation | async-start | bytes 2097152 | tf_op jit(solution)/shard_map/all_to_all | solution.py:97
  786.4 18.9 all-to-all-start.2
  789.9 121.8 %reduce-scatter.12.cloned.1.call-start = ((), (), s32[]{:S(2)}) async-start(), calls=%async_computation.25 | async-start | bytes 1179648 | tf_op jit(solution)/shard_map/reduce_scatter | solution.py:243
  876.5 124.6 %reduce-scatter.18.cloned.1.call-start = ((), (), s32[]{:S(2)}) async-start(), calls=%async_computation.28 | async-start | bytes 1179648 | tf_op jit(solution)/shard_map/reduce_scatter | solution.py:264
  914.2 115.9 %reduce-scatter.22.cloned.1.call-start = ((), (), s32[]{:S(2)}) async-start(), calls=%async_computation.30 | async-start | bytes 9437184 | tf_op jit(solution)/shard_map/reduce_scatter | solution.py:267
  921.8 183.3 %reduce-scatter.14.cloned.1.call-start = ((), (), s32[]{:S(2)}) async-start(), calls=%async_computation.26 | async-start | bytes 9437184 | tf_op jit(solution)/shard_map/reduce_scatter | solution.py:261
  957.5 356.3 %reduce-scatter.26.cloned.1.call-start = ((), (), s32[]{:S(2)}) async-start(), calls=%async_computation.32 | async-start | bytes 37748736 | tf_op jit(solution)/shard_map/reduce_scatter | solution.py:270
  978.5 544.5 %reduce-scatter.30.cloned.1.call-start = ((), (), s32[]{:S(2)}) async-start(), calls=%async_computation.34 | async-start | bytes 37748736 | tf_op jit(solution)/shard_map/reduce_scatter | solution.py:273
  1001.0 558.6 %reduce-scatter.20.cloned.1.call-start = ((), (), s32[]{:S(2)}) async-start(), calls=%async_computation.29 | async-start | bytes 163840 | tf_op jit(solution)/shard_map/reduce_scatter | solution.py:281
  1001.6 570.3 %reduce-scatter.24.cloned.1.call-start = ((), (), s32[]{:S(2)}) async-start(), calls=%async_computation.31 | async-start | bytes 1310720 | tf_op jit(solution)/shard_map/reduce_scatter | solution.py:284
  1030.1 569.9 %reduce-scatter.16.cloned.1.call-start = ((), (), s32[]{:S(2)}) async-start(), calls=%async_computation.27 | async-start | bytes 1310720 | tf_op jit(solution)/shard_map/reduce_scatter | solution.py:278
  1105.2 572.5 %reduce-scatter.28.cloned.1.call-start = ((), (), s32[]{:S(2)}) async-start(), calls=%async_computation.33 | async-start | bytes 5242880 | tf_op jit(solution)/shard_map/reduce_scatter | solution.py:287
  1313.9 443.5 %reduce-scatter.32.cloned.1.call-start = ((), (), s32[]{:S(2)}) async-start(), calls=%async_computation.35 | async-start | bytes 5242880 | tf_op jit(solution)/shard_map/reduce_scatter | solution.py:290
  1523.0 368.7 %all-reduce.4.cloned.1.call-start = ((), (), s32[]{:S(2)}) async-start(), calls=%async_computation.36 | async-start | bytes 181248 | tf_op jit(solution)/shard_map/psum | solution.py:294
  (61 other events, 1872.2 us)
Sparse Core Ops, SparseCore 0:
  9.6 30.8 all-gather.10
  42.4 23.1 all-gather.14
  67.1 27.9 all-gather.18
  96.5 80.2 all-gather.22
  178.2 79.2 all-gather.26
  259.3 52.9 all-gather.12
  314.7 26.3 all-gather.16
  343.0 66.4 all-gather.20
  411.4 160.7 all-gather.24
  574.0 160.7 all-gather.28
  876.6 35.1 reduce-scatter.11
  915.4 39.9 reduce-scatter.17
  958.8 71.2 reduce-scatter.21
  1033.8 71.2 reduce-scatter.13
  1108.5 205.2 reduce-scatter.25
  1317.7 205.2 reduce-scatter.29
  1525.1 19.1 reduce-scatter.19
  1546.5 25.3 reduce-scatter.23
  1574.2 25.7 reduce-scatter.15
  1602.3 75.4 reduce-scatter.27
  1680.0 77.2 reduce-scatter.31
  1766.0 125.5 all-reduce.3
where the time goes:
time: 1920 us; the launch traced here: 1910 us
  waiting for transfers between devices  1490 us (78%)
  matrix products  226 us (12%)
  blocking collectives  69 us (4%)
  local copies, waits for them, and re-layouts  51.5 us (3%)
  other arithmetic  43.9 us (2%)
    reduce_scatter x1, waiting for transfers between devices, shards(): lax.psum_scatter(grad_w_proj.astype(jnp.bfloat16), 'seq', scatter_dimensi...  209 us
    reduce_scatter x1, waiting for transfers between devices, shards(): lax.psum_scatter(grad_w_fc.astype(jnp.bfloat16), 'seq', scatter_dimension...  209 us
    all_gather x1, waiting for transfers between devices, shards(): lax.all_gather(part_fc, 'seq', axis=0, tiled=True)  156 us
    all_gather x1, waiting for transfers between devices, shards(): lax.all_gather(part_proj, 'seq', axis=0, tiled=True)  142 us
    psum x1, waiting for transfers between devices, shards(): lax.psum((grad_ln1_gain, grad_ln1_bias, grad_b_query, grad_b_value, grad_...  132 us
    all_gather x1, waiting for transfers between devices, shards(): lax.all_gather(w_fc, 'fsdp', axis=0, tiled=True)  81.6 us
    all_gather x1, waiting for transfers between devices, shards(): lax.all_gather(w_proj, 'fsdp', axis=0, tiled=True)  80.7 us
    reduce_scatter x1, waiting for transfers between devices, shards(): lax.psum_scatter(outer_proj.astype(jnp.bfloat16), 'fsdp', scatter_dimensi...  77 us
  transfers between devices with their start and end apart: 24, of which 20 were waited for; matrix products, arithmetic and copies ran while one was open for 10% of the time, Pallas kernels for 0%

commit v1 on v0

v1 whole, which is shorter than its diff:
```python
import jax
import jax.numpy as jnp
from jax import lax
from jax.sharding import PartitionSpec as P

HEADS = 16
HD = 128

root_two_pi = 0.7978845608028654
cubic_coef = 0.044715
epsilon = 1e-05
f32 = jnp.float32
bf16 = jnp.bfloat16


def normalize(values, gain_row, shift_row):
    center = values - jnp.mean(values, axis=-1, keepdims=True)
    inverse = lax.rsqrt(jnp.mean(center * center, axis=-1, keepdims=True) + epsilon)
    normed = center * inverse
    return (normed * gain_row + shift_row, normed, inverse)


def normalize_back(grad_out, normed, inverse, gain_row):
    scaled = grad_out * gain_row
    grad_in = inverse * (
        scaled
        - jnp.mean(scaled, axis=-1, keepdims=True)
        - normed * jnp.mean(scaled * normed, axis=-1, keepdims=True)
    )
    return (grad_in, jnp.sum(grad_out * normed, axis=0), jnp.sum(grad_out, axis=0))


def gelu_pair(inputs):
    tangent = jnp.tanh(root_two_pi * (inputs + cubic_coef * inputs * inputs * inputs))
    activated = 0.5 * inputs * (1.0 + tangent)
    gradient_slope = 0.5 * (1.0 + tangent) + 0.5 * inputs * (
        1.0 - tangent * tangent
    ) * root_two_pi * (1.0 + 3.0 * cubic_coef * inputs * inputs)
    return (activated, gradient_slope)


def dot(a, b):
    return jnp.dot(a, b, preferred_element_type=f32)


def dot_nt(a, b):
    return lax.dot_general(a, b, (((1,), (1,)), ((), ())), preferred_element_type=f32)


def dot_tn(a, b):
    return lax.dot_general(a, b, (((0,), (0,)), ((), ())), preferred_element_type=f32)


def gather_seq(block):
    return lax.all_gather(block, "seq", axis=0, tiled=True)


def scatter_seq(partial):
    return lax.psum_scatter(partial.astype(bf16), "seq", scatter_dimension=0, tiled=True).astype(f32)


def columns_to_rows(part, groups):
    rows = part.shape[0]
    spread = part.reshape(rows, groups, part.shape[1] // groups).transpose(1, 0, 2)
    return lax.all_to_all(spread, "seq", split_axis=0, concat_axis=0, tiled=True)


def column_weight(shard, groups):
    pieces = columns_to_rows(shard, groups)
    full = lax.all_gather(pieces, "fsdp", axis=1, tiled=True)
    return full.reshape(-1, full.shape[2])


def column_weight_grad(grad, groups):
    rows, cols = grad.shape
    kept = lax.psum_scatter(
        grad.astype(bf16).reshape(groups, rows // groups, cols), "fsdp", scatter_dimension=1, tiled=True
    )
    moved = lax.all_to_all(kept, "seq", split_axis=0, concat_axis=0, tiled=True)
    return moved.transpose(1, 0, 2).reshape(moved.shape[1], groups * cols).astype(f32)


def row_weight_grad(grad):
    return lax.psum_scatter(grad.astype(bf16), "fsdp", scatter_dimension=0, tiled=True).astype(f32)


def attend(queries, keyval, starts, groups, streams, rows, heads):
    length = groups * rows
    scale = HD ** (-0.5)
    position = jnp.arange(length, dtype=jnp.int32)
    mixed_list, lse_list = [], []
    for stream in range(streams):
        q = queries[:, stream].reshape(length, heads, HD)
        k = keyval[:, stream, :, :HD].reshape(length, HD)
        v = keyval[:, stream, :, HD:].reshape(length, HD)
        segment = jnp.sum((starts[stream][None, :] <= position[:, None]).astype(jnp.int32), axis=1)
        allowed = (position[None, :] <= position[:, None]) & (segment[None, :] == segment[:, None])
        scores = jnp.einsum("thd,ud->htu", q, k, preferred_element_type=f32) * scale
        scores = jnp.where(allowed[None], scores, -1e30)
        top = jnp.max(scores, axis=-1, keepdims=True)
        lse = top + jnp.log(jnp.sum(jnp.exp(scores - top), axis=-1, keepdims=True))
        probs = jnp.exp(scores - lse).astype(bf16)
        mixed = jnp.einsum("htu,ud->thd", probs, v, preferred_element_type=f32)
        mixed_list.append(mixed.astype(bf16).reshape(groups, rows, heads * HD))
        lse_list.append(lse)
    return jnp.stack(mixed_list, axis=1), lse_list


def attend_back(queries, keyval, grads, lse_list, starts, groups, streams, rows, heads):
    length = groups * rows
    scale = HD ** (-0.5)
    position = jnp.arange(length, dtype=jnp.int32)
    gq_list, gkv_list = [], []
    for stream in range(streams):
        q = queries[:, stream].reshape(length, heads, HD)
        g = grads[:, stream].reshape(length, heads, HD)
        k = keyval[:, stream, :, :HD].reshape(length, HD)
        v = keyval[:, stream, :, HD:].reshape(length, HD)
        segment = jnp.sum((starts[stream][None, :] <= position[:, None]).astype(jnp.int32), axis=1)
        allowed = (position[None, :] <= position[:, None]) & (segment[None, :] == segment[:, None])
        scores = jnp.einsum("thd,ud->htu", q, k, preferred_element_type=f32) * scale
        probs = jnp.exp(jnp.where(allowed[None], scores, -1e30) - lse_list[stream])
        grad_probs = jnp.einsum("thd,ud->htu", g, v, preferred_element_type=f32)
        delta = jnp.sum(probs * grad_probs, axis=-1, keepdims=True)
        gs = (probs * (grad_probs - delta)).astype(bf16)
        gq = jnp.einsum("htu,ud->thd", gs, k, preferred_element_type=f32) * scale
        gk = jnp.einsum("htu,thd->ud", gs, q, preferred_element_type=f32) * scale
        gv = jnp.einsum("htu,thd->ud", probs.astype(bf16), g, preferred_element_type=f32)
        gq_list.append(gq.astype(bf16).reshape(groups, rows, heads * HD))
        gkv_list.append(jnp.concatenate([gk, gv], axis=1).reshape(groups, rows, 2 * HD))
    return jnp.stack(gq_list, axis=1), jnp.stack(gkv_list, axis=1)


def shards(
    tokens,
    doc_starts,
    w_query,
    w_kv,
    w_out,
    w_fc,
    w_proj,
    ln1_gain,
    ln1_bias,
    b_query,
    b_value,
    b_out,
    ln2_gain,
    ln2_bias,
    b_fc,
    b_proj,
    cotangent,
):
    groups = lax.axis_size("seq")
    me = lax.axis_index("seq")
    streams, rows, width = tokens.shape
    own = streams * rows
    heads = HEADS // groups
    hidden = b_fc.shape[0]
    my_cols = heads * HD
    my_hidden = hidden // groups

    wq = column_weight(w_query, groups)
    w_kv_all = gather_seq(lax.all_gather(w_kv, "fsdp", axis=0, tiled=True))
    wo = lax.all_gather(w_out, "fsdp", axis=0, tiled=True)
    wf = column_weight(w_fc, groups)
    wp = lax.all_gather(w_proj, "fsdp", axis=0, tiled=True)
    my_bq = lax.dynamic_slice_in_dim(b_query, me * my_cols, my_cols, 0)
    my_bf = lax.dynamic_slice_in_dim(b_fc, me * my_hidden, my_hidden, 0)

    inputs = tokens.reshape(own, width).astype(f32)
    cot_low = cotangent.reshape(own, width)
    cot_full = cot_low.astype(f32)
    shifted1, normed1, inverse1 = normalize(inputs, ln1_gain, ln1_bias)
    hidden1 = gather_seq(shifted1.astype(bf16))
    queries = (dot(hidden1, wq) + my_bq).astype(bf16).reshape(groups, streams, rows, my_cols)
    value_shift = jnp.concatenate([jnp.zeros((HD,), f32), b_value])
    keyval = (dot(hidden1, w_kv_all) + value_shift).astype(bf16).reshape(groups, streams, rows, 2 * HD)
    mixed, lse = attend(queries, keyval, doc_starts, groups, streams, rows, heads)
    mixed_rows = mixed.reshape(groups * own, my_cols)
    residual = inputs + scatter_seq(dot(mixed_rows, wo)) + b_out
    shifted2, normed2, inverse2 = normalize(residual, ln2_gain, ln2_bias)
    hidden2 = gather_seq(shifted2.astype(bf16))
    cot_all = gather_seq(cot_low)
    pre_act = dot(hidden2, wf) + my_bf
    activated, slope = gelu_pair(pre_act)
    act_low = activated.astype(bf16)
    output = residual + scatter_seq(dot(act_low, wp)) + b_proj

    grad_b_proj = jnp.sum(cot_full, axis=0)
    shard_proj = row_weight_grad(dot_tn(act_low, cot_all))
    grad_pre = (dot_nt(cot_all, wp) * slope).astype(bf16)
    my_grad_b_fc = jnp.sum(grad_pre.astype(f32), axis=0)
    shard_fc = column_weight_grad(dot_tn(hidden2, grad_pre), groups)
    grad_hidden2 = scatter_seq(dot_nt(grad_pre, wf))
    back_second, grad_ln2_gain, grad_ln2_bias = normalize_back(
        grad_hidden2, normed2, inverse2, ln2_gain
    )
    grad_residual = cot_full + back_second
    grad_attn = grad_residual.astype(bf16)
    grad_b_out = jnp.sum(grad_attn.astype(f32), axis=0)
    grad_attn_all = gather_seq(grad_attn)
    shard_out = row_weight_grad(dot_tn(mixed_rows, grad_attn_all))
    grad_mixed = dot_nt(grad_attn_all, wo).astype(bf16).reshape(groups, streams, rows, my_cols)
    gq, gkv = attend_back(
        queries, keyval, grad_mixed, lse, doc_starts, groups, streams, rows, heads
    )
    gq_rows = gq.reshape(groups * own, my_cols)
    gkv_rows = gkv.reshape(groups * own, 2 * HD)
    my_grad_b_query = jnp.sum(gq_rows.astype(f32), axis=0)
    grad_b_value = jnp.sum(gkv_rows[:, HD:], axis=0)
    gkv_low = gkv_rows.astype(bf16)
    shard_query = column_weight_grad(dot_tn(hidden1, gq_rows), groups)
    shard_kv = row_weight_grad(scatter_seq(dot_tn(hidden1, gkv_low)))
    grad_hidden1 = scatter_seq(dot_nt(gq_rows, wq) + dot_nt(gkv_low, w_kv_all))
    back_first, grad_ln1_gain, grad_ln1_bias = normalize_back(
        grad_hidden1, normed1, inverse1, ln1_gain
    )
    input_grad = grad_residual + back_first

    zero = jnp.zeros_like
    grad_b_query = lax.dynamic_update_slice_in_dim(zero(b_query), my_grad_b_query, me * my_cols, 0)
    grad_b_fc = lax.dynamic_update_slice_in_dim(zero(b_fc), my_grad_b_fc, me * my_hidden, 0)
    vectors = (
        grad_ln1_gain,
        grad_ln1_bias,
        grad_b_query,
        grad_b_value,
        grad_b_out,
        grad_ln2_gain,
        grad_ln2_bias,
        grad_b_fc,
        grad_b_proj,
    )
    sums = lax.psum(vectors, ("seq", "fsdp"))
    return (
        output.reshape(streams, rows, width),
        input_grad.reshape(streams, rows, width),
        shard_query,
        shard_kv,
        shard_out,
        shard_fc,
        shard_proj,
        *sums,
    )


def solution(mesh):
    acts = P("fsdp", "seq", None)
    weight = P(("seq", "fsdp"), None)
    return jax.shard_map(
        shards,
        mesh=mesh,
        in_specs=(acts, P("fsdp", None)) + (weight,) * 5 + (P(),) * 9 + (acts,),
        out_specs=(acts, acts) + (weight,) * 5 + (P(),) * 9,
        check_vma=False,
    )
```

time: 1920 us -> 1340 us (0.70)
  waiting for transfers between devices: 1490 us -> 936 us
  blocking collectives: 69 us -> 47.1 us
    reduce_scatter x11 -> x10, waiting for transfers between devices: 746 us -> 425 us  [the longest x5 248 us: scatter_seq(): lax.psum_scatter(partial.astype(bf16), 'seq', scatter_dimension=0, tiled=...]
    all_gather x10 -> x9, waiting for transfers between devices: 595 us -> 382 us  [the longest x5 229 us: gather_seq(): return lax.all_gather(block, 'seq', axis=0, tiled=True)]
    all_to_all x2, blocking collectives: 51.6 us -> 30.7 us  [columns_to_rows(): lax.all_to_all(spread, 'seq', split_axis=0, concat_axis=0, tiled=True)]
    dot_general x43 -> x27, matrix products: 226 us -> 207 us  [the longest x5 58.8 us: dot_nt(): lax.dot_general(a, b, (((1,), (1,)), ((), ())), preferred_element_type=f32)]
  transfers between devices with their start and end apart: 24 -> 22, of which waited for: 20 -> 19; matrix products, arithmetic and copies ran while one was open for 10% -> 14% of each run, Pallas kernels for 0% -> 0%
where the time goes in v1:
time: 1340 us; the launch traced here: 1330 us
  waiting for transfers between devices  936 us (70%)
  matrix products  207 us (15%)
  other arithmetic  57.8 us (4%)
  local copies, waits for them, and re-layouts  56.8 us (4%)
  blocking collectives  47.1 us (4%)
  between operations  15.5 us (1%)
    reduce_scatter x5, waiting for transfers between devices, scatter_seq(): lax.psum_scatter(partial.astype(bf16), 'seq', scatter_dimension=0, tiled=...  248 us
    all_gather x5, waiting for transfers between devices, gather_seq(): return lax.all_gather(block, 'seq', axis=0, tiled=True)  229 us
    psum x1, waiting for transfers between devices, shards(): sums = lax.psum(vectors, ('seq', 'fsdp'))  127 us
    reduce_scatter x3, waiting for transfers between devices, row_weight_grad(): lax.psum_scatter(grad.astype(bf16), 'fsdp', scatter_dimension=0, tiled=True)  110 us
    all_gather x2, waiting for transfers between devices, column_weight(): full = lax.all_gather(pieces, 'fsdp', axis=1, tiled=True)  77.8 us
    all_gather x1, waiting for transfers between devices, shards(): wp = lax.all_gather(w_proj, 'fsdp', axis=0, tiled=True)  67.8 us
    reduce_scatter x2, waiting for transfers between devices, column_weight_grad(): lax.psum_scatter(grad.astype(bf16).reshape(groups, rows // groups, cols),...  67.2 us
    dot_general x5, matrix products, dot_nt(): lax.dot_general(a, b, (((1,), (1,)), ((), ())), preferred_element_type=f32)  58.8 us
  transfers between devices with their start and end apart: 22, of which 19 were waited for; matrix products, arithmetic and copies ran while one was open for 14% of the time, Pallas kernels for 0%

profile of v1, /device:TPU:0, one launch (start us, length us, event | category | flops | bytes accessed | tf_op | source)
XLA Modules:
  0.0 1328.8 jit_solution(12546922136152499672)
XLA Ops:
  8.3 11.9 all_to_all.20
  27.0 16.4 %all_gather.31 = bf16[256,256]{1,0:T(8,128)(2,1)} all-gather(bf16[64,256]{1,0:T(8,128)(2,1)} %param.20), channel_id=1, replica_groups=mesh['seq'=8,'fsdp'=4] {'fsdp'}, dimensions={0}, use_global_device_ids=true | all-gather | bytes 163840 | tf_op jit(solution)/shard_map/all_gather | solution.py:163
  51.9 54.9 %all-gather.10.cloned.1.call-done = bf16[2048,2048]{1,0:T(8,128)(2,1)} async-done(((bf16[256,2048]{1,0:T(8,128)(2,1)}), bf16[2048,2048]{1,0:T(8,128)(2,1)}) %all-gather.10.cloned.1.call-update) | async-done | bytes 8388624 | tf_op jit(solution)/shard_map/all_gather | solution.py:55
  117.2 15.1 %all-gather.12.cloned.1.call-done = bf16[2048,256]{1,0:T(8,128)(2,1)} async-done(((bf16[256,256]{1,0:T(8,128)(2,1)}), bf16[2048,256]{1,0:T(8,128)(2,1)}) %all-gather.12.cloned.1.call-update) | async-done | bytes 1048592 | tf_op jit(solution)/shard_map/all_gather | solution.py:55
  169.8 18.8 %all_to_all.21 = bf16[8,64,1024]{2,1,0:T(8,128)(2,1)S(1)} all-to-all(bf16[8,64,1024]{2,1,0:T(8,128)(2,1)S(1)} %copy.164), channel_id=1, replica_groups=mesh['seq'=8,'fsdp'=4] {'seq'}, dimensions={0} | all-to-all | bytes 2097152 | tf_op jit(solution)/shard_map/all_to_all | solution.py:65
  190.3 49.2 %reduce-scatter.11.cloned.1.call-done = bf16[256,2048]{1,0:T(8,128)(2,1)} async-done(((bf16[2048,2048]{1,0:T(8,128)(2,1)}), bf16[256,2048]{1,0:T(8,128)(2,1)}) %reduce-scatter.11.cloned.1.call-update) | async-done | bytes 1048592 | tf_op jit(solution)/shard_map/reduce_scatter | solution.py:59
  248.1 74.3 %all-gather.20.cloned.1.call-done = bf16[8,256,1024]{2,0,1:T(8,128)(2,1)} async-done(((bf16[8,64,1024]{2,0,1:T(8,128)(2,1)}), bf16[8,256,1024]{2,0,1:T(8,128)(2,1)}) %all-gather.20.cloned.1.call-update) | async-done | bytes 4194320 | tf_op jit(solution)/shard_map/all_gather | solution.py:70
  328.8 49.1 %all-gather.18.cloned.1.call-done = bf16[2048,2048]{1,0:T(8,128)(2,1)} async-done(((bf16[256,2048]{1,0:T(8,128)(2,1)}), bf16[2048,2048]{1,0:T(8,128)(2,1)}) %all-gather.18.cloned.1.call-update) | async-done | bytes 8388624 | tf_op jit(solution)/shard_map/all_gather | solution.py:55
  377.9 14.6 %fusion.61 = f32[2048,1024]{1,0:T(8,128)} fusion(bf16[2048,2048]{1,0:T(8,128)(2,1)} %all-gather.18.cloned.1.call-done, bf16[2048,1024]{1,0:T(8,128)(2,1)} %bitcast.254), kind=kOutput, calls=%fused_computation.132 | convolution fusion | flops 8589934592 | bytes 20971520 | tf_op jit(solution)/shard_map/dot_general | solution.py:43
  392.5 67.8 %all-gather.22.cloned.1.call-done = bf16[1024,2048]{1,0:T(8,128)(2,1)} async-done(((bf16[256,2048]{1,0:T(8,128)(2,1)}), bf16[1024,2048]{1,0:T(8,128)(2,1)}) %all-gather.22.cloned.1.call-update) | async-done | bytes 4194320 | tf_op jit(solution)/shard_map/all_gather | solution.py:166
  460.3 55.0 %all-gather.24.cloned.1.call-done = bf16[2048,2048]{1,0:T(8,128)(2,1)} async-done(((bf16[256,2048]{1,0:T(8,128)(2,1)}), bf16[2048,2048]{1,0:T(8,128)(2,1)}) %all-gather.24.cloned.1.call-update) | async-done | bytes 8388624 | tf_op jit(solution)/shard_map/all_gather | solution.py:55
  515.3 20.3 %convert_reduce_fusion = (f32[1024]{0:T(1024)}, bf16[2048,1024]{1,0:T(8,128)(2,1)S(1)}) fusion(f32[2048,1024]{1,0:T(8,128)} %fusion.61, f32[1024]{0:T(1024)S(1)} %dynamic_slice.7, bf16[2048,2048]{1,0:T(8,128)(2,1)} %all-gather.24.cloned.1.call-done, bf16[1024,2048]{1,0:T(8,128)(2,1)} %all-gather.22.cloned.1.call-done), kind=kOutput, calls=%fused_computation.22 | convolution fusion | flops 8636070912 | bytes 25174016 | tf_op jit(solution)/shard_map/dot_general | solution.py:47
  548.9 15.4 %convolution_convert_fusion.1 = bf16[2048,2048]{1,0:T(8,128)(2,1)} fusion(bf16[1024,2048]{1,0:T(8,128)(2,1)} %all-gather.22.cloned.1.call-done, f32[2048,1024]{1,0:T(8,128)} %fusion.61, f32[1024]{0:T(1024)S(1)} %dynamic_slice.7), kind=kOutput, calls=%fused_computation.29 | convolution fusion | flops 8615100416 | bytes 20975616 | tf_op jit(solution)/shard_map/dot_general | solution.py:43
  564.4 55.9 %reduce-scatter.15.cloned.1.call-done = bf16[256,2048]{1,0:T(8,128)(2,1)} async-done(((bf16[2048,2048]{1,0:T(8,128)(2,1)}), bf16[256,2048]{1,0:T(8,128)(2,1)}) %reduce-scatter.15.cloned.1.call-update) | async-done | bytes 1048592 | tf_op jit(solution)/shard_map/reduce_scatter | solution.py:59
  623.4 71.7 %reduce-scatter.13.cloned.1.call-done = bf16[256,2048]{1,0:T(8,128)(2,1)} async-done(((bf16[2048,2048]{1,0:T(8,128)(2,1)}), bf16[256,2048]{1,0:T(8,128)(2,1)}) %reduce-scatter.13.cloned.1.call-update) | async-done | bytes 1048592 | tf_op jit(solution)/shard_map/reduce_scatter | solution.py:59
  701.6 54.5 %all-gather.26.cloned.1.call-done = bf16[2048,2048]{1,0:T(8,128)(2,1)} async-done(((bf16[256,2048]{1,0:T(8,128)(2,1)}), bf16[2048,2048]{1,0:T(8,128)(2,1)}) %all-gather.26.cloned.1.call-update) | async-done | bytes 8388624 | tf_op jit(solution)/shard_map/all_gather | solution.py:55
  830.8 14.0 %convolution_convert_fusion.4 = bf16[2048,1024]{1,0:T(8,128)(2,1)} fusion(bf16[2048,2048]{1,0:T(8,128)(2,1)} %all-gather.18.cloned.1.call-done, bf16[2048,1024]{1,0:T(8,128)(2,1)} %copy-done.46), kind=kOutput, calls=%fused_computation.39 | convolution fusion | flops 8592031744 | bytes 16777216 | tf_op jit(solution)/shard_map/dot_general | solution.py:51
  844.9 16.7 %convolution_convert_fusion.3 = bf16[1024,2048]{1,0:T(8,128)(2,1)} fusion(bf16[2048,2048]{1,0:T(8,128)(2,1)} %all-gather.24.cloned.1.call-done, f32[2048,1024]{1,0:T(8,128)} %fusion.61, f32[1024]{0:T(1024)S(1)} %dynamic_slice.7), kind=kOutput, calls=%fused_computation.38 | convolution fusion | flops 8613003264 | bytes 20975616 | tf_op jit(solution)/shard_map/dot_general | solution.py:51
  906.0 40.0 %reduce-scatter.27.cloned.1.call-done = bf16[8,64,1024]{2,1,0:T(8,128)(2,1)} async-done(((bf16[8,256,1024]{2,1,0:T(8,128)(2,1)}), bf16[8,64,1024]{2,1,0:T(8,128)(2,1)}) %reduce-scatter.27.cloned.1.call-update) | async-done | bytes 1048592 | tf_op jit(solution)/shard_map/reduce_scatter | solution.py:76
  952.5 72.9 %reduce-scatter.29.cloned.1.call-done = bf16[256,2048]{1,0:T(8,128)(2,1)} async-done(((bf16[1024,2048]{1,0:T(8,128)(2,1)}), bf16[256,2048]{1,0:T(8,128)(2,1)}) %reduce-scatter.29.cloned.1.call-update) | async-done | bytes 1048592 | tf_op jit(solution)/shard_map/reduce_scatter | solution.py:84
  1028.2 27.1 %reduce-scatter.19.cloned.1.call-done = bf16[8,64,256]{2,1,0:T(8,128)(2,1)} async-done(((bf16[8,256,256]{2,1,0:T(8,128)(2,1)}), bf16[8,64,256]{2,1,0:T(8,128)(2,1)}) %reduce-scatter.19.cloned.1.call-update) | async-done | bytes 262160 | tf_op jit(solution)/shard_map/reduce_scatter | solution.py:76
  1076.7 26.2 %reduce-scatter.25.cloned.1.call-done = bf16[64,2048]{1,0:T(8,128)(2,1)} async-done(((bf16[256,2048]{1,0:T(8,128)(2,1)}), bf16[64,2048]{1,0:T(8,128)(2,1)}) %reduce-scatter.25.cloned.1.call-update) | async-done | bytes 262160 | tf_op jit(solution)/shard_map/reduce_scatter | solution.py:84
  1105.5 70.8 %reduce-scatter.17.cloned.1.call-done = bf16[256,2048]{1,0:T(8,128)(2,1)} async-done(((bf16[2048,2048]{1,0:T(8,128)(2,1)}), bf16[256,2048]{1,0:T(8,128)(2,1)}) %reduce-scatter.17.cloned.1.call-update) | async-done | bytes 1048592 | tf_op jit(solution)/shard_map/reduce_scatter | solution.py:59
  1183.2 126.8 %all-reduce.4.cloned.1.call-done = (f32[2048]{0:T(1024)}, f32[2048]{0:T(1024)}, f32[2048]{0:T(1024)}, f32[128]{0:T(128)}, f32[2048]{0:T(1024)}, /*index=5*/f32[2...) async-done(((f32[2048]{0:T(1024)}, f32[2048]{0:T(1024)}, f32[2048]{0:T(1024)}, f32[128]{0:T(128)}, f32[2048]{0:T(1024)}, /*index=5*/f32[2048]{0:T(1024)}, ...) | async-done | bytes 90640 | tf_op jit(solution)/shard_map/psum | solution.py:234
  (262 shorter events, 273.8 us)
Async XLA Ops:
  7.2 43.3 %all-gather.14.cloned.1.call-start = ((), (), s32[]{:S(2)}) async-start(), calls=%async_computation.16 | async-start | bytes 1310720 | tf_op jit(solution)/shard_map/all_gather | solution.py:70
  21.1 85.8 %all-gather.10.cloned.1.call-start = ((), (), s32[]{:S(2)}) async-start(), calls=%async_computation.14 | async-start | bytes 9437184 | tf_op jit(solution)/shard_map/all_gather | solution.py:55
  27.0 105.3 %all-gather.12.cloned.1.call-start = ((), (), s32[]{:S(2)}) async-start(), calls=%async_computation.15 | async-start | bytes 1179648 | tf_op jit(solution)/shard_map/all_gather | solution.py:55
  43.5 118.2 %all-gather.16.cloned.1.call-start = ((), (), s32[]{:S(2)}) async-start(), calls=%async_computation.17 | async-start | bytes 1310720 | tf_op jit(solution)/shard_map/all_gather | solution.py:164
  44.0 195.4 %reduce-scatter.11.cloned.1.call-start = ((), (), s32[]{:S(2)}) async-start(), calls=%async_computation.18 | async-start | bytes 9437184 | tf_op jit(solution)/shard_map/reduce_scatter | solution.py:59
  168.6 153.7 %all-gather.20.cloned.1.call-start = ((), (), s32[]{:S(2)}) async-start(), calls=%async_computation.20 | async-start | bytes 5242880 | tf_op jit(solution)/shard_map/all_gather | solution.py:70
  190.2 187.7 %all-gather.18.cloned.1.call-start = ((), (), s32[]{:S(2)}) async-start(), calls=%async_computation.19 | async-start | bytes 9437184 | tf_op jit(solution)/shard_map/all_gather | solution.py:55
  245.8 214.5 %all-gather.22.cloned.1.call-start = ((), (), s32[]{:S(2)}) async-start(), calls=%async_computation.21 | async-start | bytes 5242880 | tf_op jit(solution)/shard_map/all_gather | solution.py:166
  246.6 268.8 %all-gather.24.cloned.1.call-start = ((), (), s32[]{:S(2)}) async-start(), calls=%async_computation.23 | async-start | bytes 9437184 | tf_op jit(solution)/shard_map/all_gather | solution.py:55
  247.3 373.0 %reduce-scatter.15.cloned.1.call-start = ((), (), s32[]{:S(2)}) async-start(), calls=%async_computation.24 | async-start | bytes 9437184 | tf_op jit(solution)/shard_map/reduce_scatter | solution.py:59
  548.8 146.3 %reduce-scatter.13.cloned.1.call-start = ((), (), s32[]{:S(2)}) async-start(), calls=%async_computation.22 | async-start | bytes 9437184 | tf_op jit(solution)/shard_map/reduce_scatter | solution.py:59
  564.3 191.7 %all-gather.26.cloned.1.call-start = ((), (), s32[]{:S(2)}) async-start(), calls=%async_computation.25 | async-start | bytes 9437184 | tf_op jit(solution)/shard_map/all_gather | solution.py:55
  701.5 175.4 %reduce-scatter.21.cloned.1.call-start = ((), (), s32[]{:S(2)}) async-start(), calls=%async_computation.28 | async-start | bytes 1179648 | tf_op jit(solution)/shard_map/reduce_scatter | solution.py:59
  830.7 115.2 %reduce-scatter.27.cloned.1.call-start = ((), (), s32[]{:S(2)}) async-start(), calls=%async_computation.31 | async-start | bytes 5242880 | tf_op jit(solution)/shard_map/reduce_scatter | solution.py:76
  844.8 180.6 %reduce-scatter.29.cloned.1.call-start = ((), (), s32[]{:S(2)}) async-start(), calls=%async_computation.32 | async-start | bytes 5242880 | tf_op jit(solution)/shard_map/reduce_scatter | solution.py:84
  861.6 193.7 %reduce-scatter.19.cloned.1.call-start = ((), (), s32[]{:S(2)}) async-start(), calls=%async_computation.27 | async-start | bytes 1310720 | tf_op jit(solution)/shard_map/reduce_scatter | solution.py:76
  876.9 198.4 %reduce-scatter.23.cloned.1.call-start = ((), (), s32[]{:S(2)}) async-start(), calls=%async_computation.29 | async-start | bytes 163840 | tf_op jit(solution)/shard_map/reduce_scatter | solution.py:84
  877.4 225.4 %reduce-scatter.25.cloned.1.call-start = ((), (), s32[]{:S(2)}) async-start(), calls=%async_computation.30 | async-start | bytes 1310720 | tf_op jit(solution)/shard_map/reduce_scatter | solution.py:84
  884.2 292.0 %reduce-scatter.17.cloned.1.call-start = ((), (), s32[]{:S(2)}) async-start(), calls=%async_computation.26 | async-start | bytes 9437184 | tf_op jit(solution)/shard_map/reduce_scatter | solution.py:59
  946.0 82.2 %all-to-all-start.3 = ((bf16[8,64,1024]{2,1,0:T(8,128)(2,1)}), bf16[8,64,1024]{2,1,0:T(8,128)(2,1)}, u32[]{:S(2)}, u32[]{:S(2)}) async-start(bf16[8,64,1024]{2,1,0:T(8,128)(2,1)} %reduce-scatter.27.cloned.1.call-done), calls=%async_computation.12 | async-start | bytes 2097152 | tf_op jit(solution)/shard_map/all_to_all | solution.py:79
  950.2 226.1 %copy-start.36 = (f32[2048]{0:T(1024)S(1)}, f32[2048]{0:T(1024)}, u32[]{:S(2)}) copy-start(f32[2048]{0:T(1024)} %param.24) | copy-start | bytes 24580
  952.5 226.7 %copy-start.34 = (f32[8192]{0:T(1024)}, f32[8192]{0:T(1024)S(1)}, u32[]{:S(2)}) copy-start(f32[8192]{0:T(1024)S(1)} %dynamic_update_slice.7) | copy-start | bytes 98308
  1055.3 49.3 %all-to-all-start.2 = ((bf16[8,64,256]{2,1,0:T(8,128)(2,1)}), bf16[8,64,256]{2,1,0:T(8,128)(2,1)S(1)}, u32[]{:S(2)}, u32[]{:S(2)}) async-start(bf16[8,64,256]{2,1,0:T(8,128)(2,1)} %reduce-scatter.19.cloned.1.call-done), calls=%async_computation.7 | async-start | bytes 524288 | tf_op jit(solution)/shard_map/all_to_all | solution.py:79
  1059.0 251.0 %all-reduce.4.cloned.1.call-start = ((), (), s32[]{:S(2)}) async-start(), calls=%async_computation.33 | async-start | bytes 181248 | tf_op jit(solution)/shard_map/psum | solution.py:234
  (49 other events, 1655.8 us)
Sparse Core Ops, SparseCore 0:
  21.2 29.2 all-gather.13
  52.9 53.8 all-gather.9
  108.7 23.4 all-gather.11
  133.7 27.9 all-gather.15
  168.7 70.7 reduce-scatter.10
  241.5 80.7 all-gather.19
  324.9 52.9 all-gather.17
  379.5 80.7 all-gather.21
  462.4 52.9 all-gather.23
  548.9 71.3 reduce-scatter.14
  623.7 71.2 reduce-scatter.12
  701.6 54.3 all-gather.25
  830.9 36.0 reduce-scatter.20
  869.2 76.7 reduce-scatter.26
  948.1 77.2 reduce-scatter.28
  1027.7 27.6 reduce-scatter.18
  1057.4 17.7 reduce-scatter.22
  1077.5 25.3 reduce-scatter.24
  1106.3 69.9 reduce-scatter.16
  1184.8 125.0 all-reduce.3

commit v2 on v1

v2 whole, which is shorter than its diff:
```python
import functools

import jax
import jax.numpy as jnp
from jax import lax
from jax.experimental import pallas as pl
from jax.experimental.pallas import tpu as pltpu
from jax.sharding import PartitionSpec as P

HEADS = 16
HD = 128

root_two_pi = 0.7978845608028654
cubic_coef = 0.044715
epsilon = 1e-05
f32 = jnp.float32
bf16 = jnp.bfloat16
MESH = pl.DeviceIdType.MESH
ANY = pl.BlockSpec(memory_space=pl.ANY)
WHOLE = pl.BlockSpec(memory_space=pltpu.VMEM)
VMEM_LIMIT = 56 * 1024 * 1024
PLANE = 8


def normalize(values, gain_row, shift_row):
    center = values - jnp.mean(values, axis=-1, keepdims=True)
    inverse = lax.rsqrt(jnp.mean(center * center, axis=-1, keepdims=True) + epsilon)
    normed = center * inverse
    return (normed * gain_row + shift_row, normed, inverse)


def normalize_back(grad_out, normed, inverse, gain_row):
    scaled = grad_out * gain_row
    grad_in = inverse * (
        scaled
        - jnp.mean(scaled, axis=-1, keepdims=True)
        - normed * jnp.mean(scaled * normed, axis=-1, keepdims=True)
    )
    return (grad_in, jnp.sum(grad_out * normed, axis=0), jnp.sum(grad_out, axis=0))


def gelu_pair(inputs):
    tangent = jnp.tanh(root_two_pi * (inputs + cubic_coef * inputs * inputs * inputs))
    activated = 0.5 * inputs * (1.0 + tangent)
    gradient_slope = 0.5 * (1.0 + tangent) + 0.5 * inputs * (
        1.0 - tangent * tangent
    ) * root_two_pi * (1.0 + 3.0 * cubic_coef * inputs * inputs)
    return (activated, gradient_slope)


def dot(a, b):
    return jnp.dot(a, b, preferred_element_type=f32)


def dot_nt(a, b):
    return lax.dot_general(a, b, (((1,), (1,)), ((), ())), preferred_element_type=f32)


def dot_tn(a, b):
    return lax.dot_general(a, b, (((0,), (0,)), ((), ())), preferred_element_type=f32)


def push(src, dst, send, recv, to):
    return pltpu.make_async_remote_copy(
        src_ref=src, dst_ref=dst, send_sem=send, recv_sem=recv, device_id=to, device_id_type=MESH
    )


class Place:
    def __init__(self):
        me = lax.axis_index("seq")
        self.me = me
        self.core = lax.rem(me, 2)
        x = lax.rem(lax.div(me, 2), 2)
        y = lax.div(me, 4)
        self.sib = me + 1 - 2 * self.core
        self.xn = me + 2 - 4 * x
        self.yn = me + 4 - 8 * y
        self.dg = me + 2 - 4 * x + 4 - 8 * y
        turn = 1 - 2 * self.core
        self.xs, self.ys, self.ds = self.xn + turn, self.yn + turn, self.dg + turn

    def greet(self):
        barrier = pltpu.get_barrier_semaphore()
        for other in (self.sib, self.xn, self.yn):
            pl.semaphore_signal(barrier, inc=1, device_id={"seq": other}, device_id_type=MESH)
        pl.semaphore_wait(barrier, 3)


class Gather:
    sends = 14

    def __init__(self, place, buf, rows, send, recv):
        self.p, self.buf, self.rows, self.half = place, buf, rows, rows // 2
        self.send_sem, self.recv_sem = send, recv
        self.copies = []

    def piece(self, dev, half):
        start = pl.multiple_of(dev * self.rows + half * self.half, self.half)
        return self.buf.at[pl.ds(start, self.half), :]

    def pair(self, dev):
        start = pl.multiple_of(lax.div(dev, 2) * (2 * self.rows), 2 * self.rows)
        return pl.ds(start, 2 * self.rows)

    def send(self, dev, half, to, src=None):
        k = len(self.copies)
        piece = self.piece(dev, half)
        copy = push(
            piece if src is None else src,
            piece,
            self.send_sem.at[k],
            self.recv_sem.at[dev, half],
            {"seq": to},
        )
        copy.start()
        self.copies.append(copy)

    def arrived(self, dev, half):
        piece = self.piece(dev, half)
        push(
            piece, piece, self.send_sem.at[0], self.recv_sem.at[dev, half], {"seq": self.p.sib}
        ).wait_recv()

    def start(self, own):
        p = self.p
        parts = [own.at[pl.ds(h * self.half, self.half), :] for h in range(2)]
        self.send(p.me, 0, p.yn, parts[0])
        self.send(p.me, 1, p.xn, parts[1])
        self.send(p.me, 1, p.yn, parts[1])
        self.send(p.me, 0, p.xn, parts[0])
        for h in range(2):
            self.send(p.me, h, p.sib, parts[h])

    def relay(self):
        p = self.p
        self.arrived(p.yn, 0)
        self.send(p.yn, 0, p.xn)
        self.arrived(p.xn, 1)
        self.send(p.xn, 1, p.yn)
        self.send(p.yn, 0, p.sib)
        self.send(p.xn, 1, p.sib)
        self.arrived(p.xn, 0)
        self.send(p.xn, 0, p.sib)
        self.arrived(p.yn, 1)
        self.send(p.yn, 1, p.sib)

    def have(self, dev):
        self.arrived(dev, 0)
        self.arrived(dev, 1)

    def relay_corner(self):
        p = self.p
        for h in range(2):
            self.arrived(p.dg, h)
            self.send(p.dg, h, p.sib)

    def finish(self):
        for copy in self.copies:
            copy.wait_send()


def gather_sems():
    return [pltpu.SemaphoreType.DMA((Gather.sends,)), pltpu.SemaphoreType.DMA((PLANE, 2))]


def gather_plane(blocks, number):
    count = len(blocks)

    def kernel(*refs):
        ins, outs = refs[:count], refs[count : 2 * count]
        sems = refs[2 * count :]
        p = Place()
        locals_ = []
        for i in range(count):
            rows = ins[i].shape[0]
            start = pl.multiple_of(p.me * rows, rows)
            copy = pltpu.make_async_copy(
                ins[i], outs[i].at[pl.ds(start, rows), :], sems[2 * count].at[i]
            )
            copy.start()
            locals_.append(copy)
        p.greet()
        gathers = [
            Gather(p, outs[i], ins[i].shape[0], sems[2 * i], sems[2 * i + 1]) for i in range(count)
        ]
        gathers[0].start(ins[0])
        for i in range(count):
            if i + 1 < count:
                gathers[i + 1].start(ins[i + 1])
            gathers[i].relay()
        for i in range(count):
            gathers[i].relay_corner()
        for i in range(count):
            for dev in (p.sib, p.xs, p.ys, p.ds):
                gathers[i].have(dev)
            gathers[i].finish()
            locals_[i].wait()

    scratch = []
    for _ in blocks:
        scratch += gather_sems()
    scratch.append(pltpu.SemaphoreType.DMA((count,)))
    return pl.pallas_call(
        kernel,
        out_shape=[
            jax.ShapeDtypeStruct((PLANE * b.shape[0], b.shape[1]), b.dtype) for b in blocks
        ],
        in_specs=[ANY] * count,
        out_specs=[ANY] * count,
        scratch_shapes=scratch,
        compiler_params=pltpu.CompilerParams(collective_id=number, has_side_effects=True),
        name="gather_plane",
    )(*blocks)


def gather_matmul(own, weight, extras, outs, epilogue, number, nt=False, name="gather_matmul"):
    rows, depth = own.shape
    wide = weight.shape[0] if nt else weight.shape[1]
    tile = 256
    n_ex, n_out = len(extras), len(outs)

    def kernel(own_ref, w_ref, *refs):
        ex = refs[:n_ex]
        all_ref = refs[n_ex]
        out_refs = refs[n_ex + 1 : n_ex + 1 + n_out]
        buf, w_buf = refs[n_ex + 1 + n_out : n_ex + 3 + n_out]
        stage = refs[n_ex + 3 + n_out : n_ex + 3 + 2 * n_out]
        send, recv, local = refs[n_ex + 3 + 2 * n_out :]
        p = Place()
        mine = pl.ds(pl.multiple_of(p.me * rows, rows), rows)
        load_own = pltpu.make_async_copy(own_ref, buf.at[mine, :], local.at[0])
        load_w = pltpu.make_async_copy(w_ref, w_buf, local.at[1])
        load_own.start()
        load_w.start()
        p.greet()
        g = Gather(p, buf, rows, send, recv)
        g.start(own_ref)
        stores = []

        def work(dev, k):
            block = g.pair(dev)
            copy = pltpu.make_async_copy(
                buf.at[block, :], all_ref.at[block, :], local.at[2 + k * (1 + n_out)]
            )
            copy.start()
            stores.append(copy)

            @pl.loop(0, wide // tile)
            def _(j):
                cols = pl.ds(pl.multiple_of(j * tile, tile), tile)
                if nt:
                    acc = dot_nt(buf[block, :], w_buf[cols, :])
                else:
                    acc = dot(buf[block, :], w_buf[:, cols])
                for ref, value in zip(stage, epilogue(acc, cols, ex)):
                    ref[block, cols] = value.astype(ref.dtype)

            for i in range(n_out):
                copy = pltpu.make_async_copy(
                    stage[i].at[block, :],
                    out_refs[i].at[block, :],
                    local.at[2 + k * (1 + n_out) + 1 + i],
                )
                copy.start()
                stores.append(copy)

        load_own.wait()
        load_w.wait()
        g.have(p.sib)
        work(p.me, 0)
        g.relay()
        g.have(p.xs)
        work(p.xn, 1)
        g.have(p.ys)
        work(p.yn, 2)
        g.relay_corner()
        g.have(p.ds)
        work(p.dg, 3)
        g.finish()
        for copy in stores:
            copy.wait()

    total = PLANE * rows
    return pl.pallas_call(
        kernel,
        out_shape=[jax.ShapeDtypeStruct((total, depth), own.dtype)]
        + [jax.ShapeDtypeStruct((total, wide), t) for t in outs],
        in_specs=[ANY, ANY] + [WHOLE] * n_ex,
        out_specs=[ANY] * (1 + n_out),
        scratch_shapes=[
            pltpu.VMEM((total, depth), own.dtype),
            pltpu.VMEM(weight.shape, weight.dtype),
        ]
        + [pltpu.VMEM((total, wide), t) for t in outs]
        + gather_sems()
        + [pltpu.SemaphoreType.DMA((2 + 4 * (1 + n_out),))],
        compiler_params=pltpu.CompilerParams(
            collective_id=number, has_side_effects=True, vmem_limit_bytes=VMEM_LIMIT
        ),
        cost_estimate=pl.CostEstimate(
            flops=2 * total * depth * wide, bytes_accessed=40 * 1024 * 1024, transcendentals=0
        ),
        name=name,
    )(own, weight, *extras)


def matmul_scatter(pairs, number, name="matmul_scatter"):
    count = len(pairs)
    total = pairs[0][0].shape[0]
    rows = total // PLANE
    half = rows // 2
    wide = pairs[0][1].shape[0] if pairs[0][2] else pairs[0][1].shape[1]
    tile = 512
    lines = 32

    def kernel(*refs):
        a_refs, w_refs = refs[:count], refs[count : 2 * count]
        out_ref = refs[2 * count]
        a_bufs = refs[2 * count + 1 : 3 * count + 1]
        w_bufs = refs[3 * count + 1 : 4 * count + 1]
        part, sib_out, sib_in, out_d, out_x, out_y, in_d, in_x, in_y = refs[
            4 * count + 1 : 4 * count + 10
        ]
        sib_send, sib_recv, send, recv, local = refs[4 * count + 10 :]
        p = Place()
        loads = []
        for i in range(count):
            for k, (src, dst) in enumerate(((a_refs[i], a_bufs[i]), (w_refs[i], w_bufs[i]))):
                copy = pltpu.make_async_copy(src, dst, local.at[2 * i + k])
                copy.start()
                loads.append(copy)
        p.greet()
        for copy in loads:
            copy.wait()
        copies = []

        def product(role, dev):
            chip = lax.div(dev, 2) * (2 * rows)
            theirs = pl.ds(pl.multiple_of(chip + (1 - p.core) * rows, rows), rows)
            ours = pl.ds(pl.multiple_of(chip + p.core * rows, rows), rows)

            @pl.loop(0, wide // tile)
            def _(j):
                cols = pl.ds(pl.multiple_of(j * tile, tile), tile)

                def sum_of(where):
                    acc = None
                    for i in range(count):
                        if pairs[i][2]:
                            term = dot_nt(a_bufs[i][where, :], w_bufs[i][cols, :])
                        else:
                            term = dot(a_bufs[i][where, :], w_bufs[i][:, cols])
                        acc = term if acc is None else acc + term
                    return acc

                sib_out[role, :, cols] = sum_of(theirs).astype(bf16)
                part[role, :, cols] = sum_of(ours)

            copy = push(
                sib_out.at[role],
                sib_in.at[role],
                sib_send.at[role],
                sib_recv.at[role],
                {"seq": p.sib},
            )
            copy.start()
            copies.append(copy)
            return copy

        def add_into(dst, role, first, size, more=()):
            @pl.loop(0, size // lines)
            def _(i):
                line = pl.ds(pl.multiple_of(first + i * lines, lines), lines)
                value = part[role, line, :] + sib_in[role, line, :].astype(f32)
                for ref in more:
                    value = value + ref[line, :].astype(f32)
                dst[line, :] = value.astype(dst.dtype)

        def ship(src, dst, h, k, to):
            part_rows = pl.ds(h * half, half)
            copy = push(
                src.at[part_rows, :], dst.at[part_rows, :], send.at[k], recv.at[k], {"seq": to}
            )
            copy.start()
            copies.append(copy)
            return copy

        to_d = product(0, p.dg)
        to_x = product(1, p.xn)
        to_d.wait_recv()
        add_into(out_d, 0, 0, rows)
        dx = ship(out_d, in_d, 0, 0, p.xn)
        dy = ship(out_d, in_d, 1, 1, p.yn)
        to_y = product(2, p.yn)
        to_x.wait_recv()
        add_into(out_x, 1, 0, half)
        x0 = ship(out_x, in_x, 0, 2, p.xn)
        to_y.wait_recv()
        add_into(out_y, 2, half, half)
        y1 = ship(out_y, in_y, 1, 3, p.yn)
        to_me = product(3, p.me)
        dy.wait_recv()
        add_into(out_x, 1, half, half, (in_d,))
        x1 = ship(out_x, in_x, 1, 4, p.xn)
        dx.wait_recv()
        add_into(out_y, 2, 0, half, (in_d,))
        y0 = ship(out_y, in_y, 0, 5, p.yn)
        to_me.wait_recv()
        x0.wait_recv()
        y0.wait_recv()
        add_into(out_ref, 3, 0, half, (in_x, in_y))
        y1.wait_recv()
        x1.wait_recv()
        add_into(out_ref, 3, half, half, (in_x, in_y))
        for copy in copies:
            copy.wait_send()

    flops = sum(2 * total * a.shape[1] * wide for a, _, _ in pairs)
    return pl.pallas_call(
        kernel,
        out_shape=jax.ShapeDtypeStruct((rows, wide), f32),
        in_specs=[ANY] * (2 * count),
        out_specs=WHOLE,
        scratch_shapes=[pltpu.VMEM(a.shape, a.dtype) for a, _, _ in pairs]
        + [pltpu.VMEM(w.shape, w.dtype) for _, w, _ in pairs]
        + [pltpu.VMEM((4, rows, wide), f32)]
        + [pltpu.VMEM((4, rows, wide), bf16)] * 2
        + [pltpu.VMEM((rows, wide), bf16)] * 6
        + [pltpu.SemaphoreType.DMA((4,))] * 2
        + [pltpu.SemaphoreType.DMA((6,))] * 2
        + [pltpu.SemaphoreType.DMA((2 * count,))],
        compiler_params=pltpu.CompilerParams(
            collective_id=number, has_side_effects=True, vmem_limit_bytes=VMEM_LIMIT
        ),
        cost_estimate=pl.CostEstimate(
            flops=flops, bytes_accessed=40 * 1024 * 1024, transcendentals=0
        ),
        name=name,
    )(*[a for a, _, _ in pairs], *[w for _, w, _ in pairs])


def greet_all(groups, layers):
    me, layer = lax.axis_index("seq"), lax.axis_index("fsdp")
    barrier = pltpu.get_barrier_semaphore()
    for step in range(1, groups):
        other = lax.rem(me + step, groups)
        pl.semaphore_signal(barrier, inc=1, device_id={"seq": other}, device_id_type=MESH)
    for step in range(1, layers):
        other = lax.rem(layer + step, layers)
        pl.semaphore_signal(barrier, inc=1, device_id={"fsdp": other}, device_id_type=MESH)
    pl.semaphore_wait(barrier, groups - 1 + layers - 1)


def split_columns(arrays, groups, number):
    count = len(arrays)

    def kernel(*refs):
        ins, outs = refs[:count], refs[count : 2 * count]
        send, recv, local = refs[2 * count :]
        me = lax.axis_index("seq")
        greet_all(groups, 1)
        copies, own = [], []
        for i in range(count):
            cols = ins[i].shape[1] // groups

            def block(dev, i=i, cols=cols):
                return ins[i].at[:, pl.ds(pl.multiple_of(dev * cols, cols), cols)]

            copy = pltpu.make_async_copy(block(me), outs[i].at[me], local.at[i])
            copy.start()
            own.append(copy)
            for step in range(1, groups):
                to = lax.rem(me + step, groups)
                copy = push(
                    block(to), outs[i].at[me], send.at[i, step], recv.at[i, step], {"seq": to}
                )
                copy.start()
                copies.append(copy)
        for copy in own:
            copy.wait()
        for copy in copies:
            copy.wait()

    return pl.pallas_call(
        kernel,
        out_shape=[
            jax.ShapeDtypeStruct((groups, a.shape[0], a.shape[1] // groups), a.dtype)
            for a in arrays
        ],
        in_specs=[ANY] * count,
        out_specs=[ANY] * count,
        scratch_shapes=[
            pltpu.SemaphoreType.DMA((count, groups)),
            pltpu.SemaphoreType.DMA((count, groups)),
            pltpu.SemaphoreType.DMA((count,)),
        ],
        compiler_params=pltpu.CompilerParams(collective_id=number, has_side_effects=True),
        name="split_columns",
    )(*arrays)


def last_exchange(vector, arrays, groups, layers, number):
    count = len(arrays)
    lines = vector.shape[1]

    def kernel(vec, *refs):
        ins = refs[:count]
        vec_out = refs[count]
        outs = refs[count + 1 : 2 * count + 1]
        box, plane_sum, zbox, vsend, vrecv, zsend, zrecv, gsend, grecv, send, recv, local = refs[
            2 * count + 1 :
        ]
        me, layer = lax.axis_index("seq"), lax.axis_index("fsdp")
        greet_all(groups, layers)
        first, copies, own = [], [], []
        for step in range(1, groups):
            to = lax.rem(me + step, groups)
            copy = push(vec.at[to], box.at[step], vsend.at[step], vrecv.at[step], {"seq": to})
            copy.start()
            first.append(copy)
        for i in range(count):
            cols = ins[i].shape[2]
            place = pl.ds(pl.multiple_of(me * cols, cols), cols)
            copy = pltpu.make_async_copy(ins[i].at[me], outs[i].at[:, place], local.at[i])
            copy.start()
            own.append(copy)
            for step in range(1, groups):
                to = lax.rem(me + step, groups)
                copy = push(
                    ins[i].at[to],
                    outs[i].at[:, place],
                    send.at[i, step],
                    recv.at[i, step],
                    {"seq": to},
                )
                copy.start()
                copies.append(copy)
        total = vec[me]
        for step in range(1, groups):
            first[step - 1].wait_recv()
            total = total + box[step]
        plane_sum[...] = total
        across = []
        for step in range(1, layers):
            to = lax.rem(layer + step, layers)
            copy = push(plane_sum, zbox.at[step], zsend.at[step], zrecv.at[step], {"fsdp": to})
            copy.start()
            across.append(copy)
        for step in range(1, layers):
            across[step - 1].wait_recv()
        zbox[0] = total
        total = None
        for k in range(layers):
            term = zbox[lax.rem(k - layer + layers, layers)]
            total = term if total is None else total + term
        vec_out[me] = total
        for copy in across:
            copy.wait_send()
        last = []
        for step in range(1, groups):
            to = lax.rem(me + step, groups)
            copy = push(
                vec_out.at[me], vec_out.at[me], gsend.at[step], grecv.at[step], {"seq": to}
            )
            copy.start()
            last.append(copy)
        for copy in last:
            copy.wait()
        for copy in first:
            copy.wait_send()
        for copy in own + copies:
            copy.wait()

    sem = pltpu.SemaphoreType.DMA
    return pl.pallas_call(
        kernel,
        out_shape=[jax.ShapeDtypeStruct(vector.shape, f32)]
        + [
            jax.ShapeDtypeStruct((a.shape[1], groups * a.shape[2]), a.dtype) for a in arrays
        ],
        in_specs=[WHOLE] + [ANY] * count,
        out_specs=[WHOLE] + [ANY] * count,
        scratch_shapes=[
            pltpu.VMEM((groups, lines, 128), f32),
            pltpu.VMEM((lines, 128), f32),
            pltpu.VMEM((layers, lines, 128), f32),
            sem((groups,)),
            sem((groups,)),
            sem((layers,)),
            sem((layers,)),
            sem((groups,)),
            sem((groups,)),
            sem((max(count, 1), groups)),
            sem((max(count, 1), groups)),
            sem((max(count, 1),)),
        ],
        compiler_params=pltpu.CompilerParams(collective_id=number, has_side_effects=True),
        name="last_exchange",
    )(vector, *arrays)


def starts_of(docs, stream, positions):
    start = jnp.zeros_like(positions)
    for j in range(docs.shape[1]):
        here = docs[stream, j]
        start = jnp.maximum(start, jnp.where(here <= positions, here, 0))
    return start


def masked_scores(docs, stream, keys, q, first, limit):
    scores = dot_nt(keys, q) * (HD**-0.5)
    t = first + lax.broadcasted_iota(jnp.int32, (1, q.shape[0]), 1)
    u = lax.broadcasted_iota(jnp.int32, scores.shape, 0)
    return scores, (u >= starts_of(docs, stream, t)) & (u <= t)


QROWS = 256


def attention_forward(docs, queries, keyval, heads):
    groups, streams, rows, cols = queries.shape
    length = groups * rows
    block = min(QROWS, length)

    def kernel(docs_ref, q_ref, kv_ref, mixed_ref, lse_ref):
        stream = pl.program_id(0)
        kv = kv_ref[...].reshape(length, 2 * HD)
        keys = kv[:, :HD]
        values_t = kv[:, HD:].T
        per = block // rows
        for b in range(length // block):
            limit = (b + 1) * block
            q_rows = q_ref[b * per : (b + 1) * per].reshape(block, cols)
            for h in range(heads):
                q = q_rows[:, h * HD : (h + 1) * HD]
                scores, allowed = masked_scores(
                    docs_ref, stream, keys[:limit], q, b * block, limit
                )
                scores = jnp.where(allowed, scores, -1e30)
                top = jnp.max(scores, axis=0, keepdims=True)
                weights = jnp.exp(scores - top)
                total = jnp.sum(weights, axis=0, keepdims=True)
                mixed = dot(values_t[:, :limit], weights.astype(bf16)) / total
                mixed_ref[b * per : (b + 1) * per, :, h * HD : (h + 1) * HD] = (
                    mixed.T.astype(bf16).reshape(per, rows, HD)
                )
                lse_ref[h : h + 1, b * block : (b + 1) * block] = top + jnp.log(total)

    spec = pl.BlockSpec((groups, None, rows, cols), lambda s: (0, s, 0, 0))
    spec_kv = pl.BlockSpec((groups, None, rows, 2 * HD), lambda s: (0, s, 0, 0))
    return pl.pallas_call(
        kernel,
        grid=(streams,),
        out_shape=[
            jax.ShapeDtypeStruct(queries.shape, bf16),
            jax.ShapeDtypeStruct((streams, heads, length), f32),
        ],
        in_specs=[pl.BlockSpec(memory_space=pltpu.SMEM), spec, spec_kv],
        out_specs=[spec, pl.BlockSpec((None, heads, length), lambda s: (s, 0, 0))],
        compiler_params=pltpu.CompilerParams(vmem_limit_bytes=VMEM_LIMIT),
        cost_estimate=pl.CostEstimate(
            flops=4 * streams * heads * length * length * HD,
            bytes_accessed=8 * 1024 * 1024,
            transcendentals=streams * heads * length * length,
        ),
        name="attention_forward",
    )(docs, queries, keyval)


def attention_backward(docs, queries, keyval, grads, lse, heads):
    groups, streams, rows, cols = queries.shape
    length = groups * rows
    block = min(QROWS, length)

    def kernel(docs_ref, q_ref, kv_ref, g_ref, lse_ref, gq_ref, gkv_ref, gk, gv):
        stream = pl.program_id(0)
        kv = kv_ref[...].reshape(length, 2 * HD)
        keys, values = kv[:, :HD], kv[:, HD:]
        keys_t = keys.T
        per = block // rows
        gk[...] = jnp.zeros_like(gk)
        gv[...] = jnp.zeros_like(gv)
        for b in range(length // block):
            limit = (b + 1) * block
            q_rows = q_ref[b * per : (b + 1) * per].reshape(block, cols)
            g_rows = g_ref[b * per : (b + 1) * per].reshape(block, cols)
            for h in range(heads):
                q = q_rows[:, h * HD : (h + 1) * HD]
                g = g_rows[:, h * HD : (h + 1) * HD]
                scores, allowed = masked_scores(
                    docs_ref, stream, keys[:limit], q, b * block, limit
                )
                shift = lse_ref[h : h + 1, b * block : (b + 1) * block]
                probs = jnp.where(allowed, jnp.exp(scores - shift), 0.0)
                grad_probs = dot_nt(values[:limit], g)
                weighted = probs * grad_probs
                delta = jnp.sum(weighted, axis=0, keepdims=True)
                grad_scores = (weighted - probs * delta).astype(bf16)
                gq = dot(keys_t[:, :limit], grad_scores) * (HD**-0.5)
                gq_ref[b * per : (b + 1) * per, :, h * HD : (h + 1) * HD] = (
                    gq.T.astype(bf16).reshape(per, rows, HD)
                )
                gk[:limit, :] += dot(grad_scores, q)
                gv[:limit, :] += dot(probs.astype(bf16), g)
        gkv_ref[:, :, :HD] = (gk[...] * (HD**-0.5)).astype(bf16).reshape(groups, rows, HD)
        gkv_ref[:, :, HD:] = gv[...].astype(bf16).reshape(groups, rows, HD)

    spec = pl.BlockSpec((groups, None, rows, cols), lambda s: (0, s, 0, 0))
    spec_kv = pl.BlockSpec((groups, None, rows, 2 * HD), lambda s: (0, s, 0, 0))
    return pl.pallas_call(
        kernel,
        grid=(streams,),
        out_shape=[
            jax.ShapeDtypeStruct(queries.shape, bf16),
            jax.ShapeDtypeStruct(keyval.shape, bf16),
        ],
        in_specs=[
            pl.BlockSpec(memory_space=pltpu.SMEM),
            spec,
            spec_kv,
            spec,
            pl.BlockSpec((None, heads, length), lambda s: (s, 0, 0)),
        ],
        out_specs=[spec, spec_kv],
        scratch_shapes=[pltpu.VMEM((length, HD), f32)] * 2,
        compiler_params=pltpu.CompilerParams(vmem_limit_bytes=VMEM_LIMIT),
        cost_estimate=pl.CostEstimate(
            flops=10 * streams * heads * length * length * HD,
            bytes_accessed=8 * 1024 * 1024,
            transcendentals=streams * heads * length * length,
        ),
        name="attention_backward",
    )(docs, queries, keyval, grads, lse)


def columns_to_rows(part, groups):
    rows = part.shape[0]
    spread = part.reshape(rows, groups, part.shape[1] // groups).transpose(1, 0, 2)
    return lax.all_to_all(spread, "seq", split_axis=0, concat_axis=0, tiled=True)


def column_weight(pieces):
    full = lax.all_gather(pieces, "fsdp", axis=1, tiled=True)
    return full.reshape(-1, full.shape[2])


def column_weight_grad(grad, groups):
    rows, cols = grad.shape
    return lax.psum_scatter(
        grad.astype(bf16).reshape(groups, rows // groups, cols),
        "fsdp",
        scatter_dimension=1,
        tiled=True,
    )


def row_weight_grad(grad):
    return lax.psum_scatter(grad.astype(bf16), "fsdp", scatter_dimension=0, tiled=True).astype(f32)


def shards(
    tokens,
    doc_starts,
    w_query,
    w_kv,
    w_out,
    w_fc,
    w_proj,
    ln1_gain,
    ln1_bias,
    b_query,
    b_value,
    b_out,
    ln2_gain,
    ln2_bias,
    b_fc,
    b_proj,
    cotangent,
):
    groups = lax.axis_size("seq")
    layers = lax.axis_size("fsdp")
    me = lax.axis_index("seq")
    streams, rows, width = tokens.shape
    own = streams * rows
    heads = HEADS // groups
    hidden = b_fc.shape[0]
    my_cols = heads * HD
    my_hidden = hidden // groups
    kernels = groups == PLANE

    def gather(*blocks, number):
        if kernels:
            return gather_plane(blocks, number)
        return [lax.all_gather(b, "seq", axis=0, tiled=True) for b in blocks]

    def scatter(*pairs, number, name):
        if kernels:
            return matmul_scatter(pairs, number, name)
        total = sum((dot_nt if nt else dot)(a, w) for a, w, nt in pairs)
        return lax.psum_scatter(
            total.astype(bf16), "seq", scatter_dimension=0, tiled=True
        ).astype(f32)

    inputs = tokens.reshape(own, width).astype(f32)
    cot_low = cotangent.reshape(own, width)
    cot_full = cot_low.astype(f32)

    if kernels:
        wq_pieces, wf_pieces = split_columns((w_query, w_fc), groups, 1)
    else:
        wq_pieces, wf_pieces = columns_to_rows(w_query, groups), columns_to_rows(w_fc, groups)
    low_kv = lax.all_gather(w_kv, "fsdp", axis=0, tiled=True)
    wo = lax.all_gather(w_out, "fsdp", axis=0, tiled=True)
    wq = column_weight(wq_pieces)
    wf = column_weight(wf_pieces)
    wp = lax.all_gather(w_proj, "fsdp", axis=0, tiled=True)
    my_bq = lax.dynamic_slice_in_dim(b_query, me * my_cols, my_cols, 0)
    my_bf = lax.dynamic_slice_in_dim(b_fc, me * my_hidden, my_hidden, 0)

    shifted1, normed1, inverse1 = normalize(inputs, ln1_gain, ln1_bias)
    hidden1, cot_all, w_kv_all = gather(shifted1.astype(bf16), cot_low, low_kv, number=2)
    queries = (dot(hidden1, wq) + my_bq).astype(bf16).reshape(groups, streams, rows, my_cols)
    value_shift = jnp.concatenate([jnp.zeros((HD,), f32), b_value])
    keyval = (
        (dot(hidden1, w_kv_all) + value_shift).astype(bf16).reshape(groups, streams, rows, 2 * HD)
    )
    mixed, lse = attention_forward(doc_starts, queries, keyval, heads)
    mixed_rows = mixed.reshape(groups * own, my_cols)
    residual = inputs + scatter((mixed_rows, wo, False), number=3, name="scatter_attn") + b_out
    shifted2, normed2, inverse2 = normalize(residual, ln2_gain, ln2_bias)
    if kernels:
        hidden2, act_low, slope = gather_matmul(
            shifted2.astype(bf16),
            wf,
            [my_bf.reshape(1, my_hidden)],
            [bf16, bf16],
            lambda acc, cols, ex: gelu_pair(acc + ex[0][:, cols]),
            4,
            name="gather_fc",
        )
    else:
        (hidden2,) = gather(shifted2.astype(bf16), number=4)
        activated, slope = gelu_pair(dot(hidden2, wf) + my_bf)
        act_low = activated.astype(bf16)

    grad_b_proj = jnp.sum(cot_full, axis=0)
    shard_proj = row_weight_grad(dot_tn(act_low, cot_all))
    grad_pre = (dot_nt(cot_all, wp) * slope.astype(f32)).astype(bf16)
    my_grad_b_fc = jnp.sum(grad_pre.astype(f32), axis=0)
    fc_part = column_weight_grad(dot_tn(hidden2, grad_pre), groups)
    grad_hidden2 = scatter((grad_pre, wf, True), number=5, name="scatter_fc")
    output = residual + scatter((act_low, wp, False), number=6, name="scatter_proj") + b_proj
    back_second, grad_ln2_gain, grad_ln2_bias = normalize_back(
        grad_hidden2, normed2, inverse2, ln2_gain
    )
    grad_residual = cot_full + back_second
    grad_attn = grad_residual.astype(bf16)
    grad_b_out = jnp.sum(grad_attn.astype(f32), axis=0)
    if kernels:
        grad_attn_all, grad_mixed = gather_matmul(
            grad_attn, wo, [], [bf16], lambda acc, cols, ex: (acc,), 7, nt=True, name="gather_out"
        )
    else:
        (grad_attn_all,) = gather(grad_attn, number=7)
        grad_mixed = dot_nt(grad_attn_all, wo).astype(bf16)
    shard_out = row_weight_grad(dot_tn(mixed_rows, grad_attn_all))
    gq, gkv = attention_backward(
        doc_starts,
        queries,
        keyval,
        grad_mixed.reshape(groups, streams, rows, my_cols),
        lse,
        heads,
    )
    gq_rows = gq.reshape(groups * own, my_cols)
    gkv_rows = gkv.reshape(groups * own, 2 * HD)
    my_grad_b_query = jnp.sum(gq_rows.astype(f32), axis=0)
    grad_b_value = jnp.sum(gkv_rows[:, HD:].astype(f32), axis=0)
    query_part = column_weight_grad(dot_tn(hidden1, gq_rows), groups)
    shard_kv = row_weight_grad(
        lax.psum_scatter(
            dot_tn(hidden1, gkv_rows).astype(bf16), "seq", scatter_dimension=0, tiled=True
        )
    )
    grad_hidden1 = scatter(
        (gq_rows, wq, True), (gkv_rows, w_kv_all, True), number=8, name="scatter_query"
    )
    back_first, grad_ln1_gain, grad_ln1_bias = normalize_back(
        grad_hidden1, normed1, inverse1, ln1_gain
    )
    input_grad = grad_residual + back_first

    zero = jnp.zeros_like
    grad_b_query = lax.dynamic_update_slice_in_dim(zero(b_query), my_grad_b_query, me * my_cols, 0)
    grad_b_fc = lax.dynamic_update_slice_in_dim(zero(b_fc), my_grad_b_fc, me * my_hidden, 0)
    vectors = (
        grad_ln1_gain,
        grad_ln1_bias,
        grad_b_query,
        grad_b_value,
        grad_b_out,
        grad_ln2_gain,
        grad_ln2_bias,
        grad_b_fc,
        grad_b_proj,
    )
    if kernels:
        sizes = [v.shape[0] for v in vectors]
        lines = -(-sum(sizes) // (groups * 8 * 128)) * 8
        pad = groups * lines * 128 - sum(sizes)
        packed = jnp.concatenate(vectors + (jnp.zeros((pad,), f32),)).reshape(groups, lines, 128)
        packed, shard_fc, shard_query = last_exchange(
            packed, (fc_part, query_part), groups, layers, 9
        )
        flat = packed.reshape(-1)
        sums, at = [], 0
        for size in sizes:
            sums.append(flat[at : at + size])
            at += size
        shard_fc, shard_query = shard_fc.astype(f32), shard_query.astype(f32)
    else:
        sums = lax.psum(vectors, ("seq", "fsdp"))

        def side_by_side(part):
            moved = lax.all_to_all(part, "seq", split_axis=0, concat_axis=0, tiled=True)
            return moved.transpose(1, 0, 2).reshape(moved.shape[1], -1).astype(f32)

        shard_fc, shard_query = side_by_side(fc_part), side_by_side(query_part)
    return (
        output.reshape(streams, rows, width),
        input_grad.reshape(streams, rows, width),
        shard_query,
        shard_kv,
        shard_out,
        shard_fc,
        shard_proj,
        *sums,
    )


def solution(mesh):
    acts = P("fsdp", "seq", None)
    weight = P(("seq", "fsdp"), None)
    return jax.shard_map(
        shards,
        mesh=mesh,
        in_specs=(acts, P("fsdp", None)) + (weight,) * 5 + (P(),) * 9 + (acts,),
        out_specs=(acts, acts) + (weight,) * 5 + (P(),) * 9,
        check_vma=False,
    )
```

time: 1340 us -> 715 us (0.53)
  waiting for transfers between devices: 936 us -> 151 us
  Pallas kernels: 0 us -> 410 us
  matrix products: 207 us -> 79.1 us
  local copies, waits for them, and re-layouts: 56.8 us -> 7.55 us
  blocking collectives: 47.1 us -> 15.1 us
  other arithmetic: 57.8 us -> 30.1 us
    pallas_call x0 -> x11, Pallas kernels: none -> 410 us  [the longest x4 183 us: matmul_scatter(): pl.pallas_call(kernel, out_shape=jax.ShapeDtypeStruct((rows, wide), f32),...]
    all_gather x5 -> x0, waiting for transfers between devices: 229 us -> none  [gather_seq(): return lax.all_gather(block, 'seq', axis=0, tiled=True)]
    reduce_scatter x5 -> x1, waiting for transfers between devices: 248 us -> 35.7 us  [shards(): lax.psum_scatter(dot_tn(hidden1, gkv_rows).astype(bf16), 'seq', scatter_d...]
    psum x1 -> x0, waiting for transfers between devices: 127 us -> none  [shards(): sums = lax.psum(vectors, ('seq', 'fsdp'))]
    all_gather x2, waiting for transfers between devices: 77.8 us -> 0.01 us  [column_weight(): full = lax.all_gather(pieces, 'fsdp', axis=1, tiled=True)]
    reduce_scatter x3, waiting for transfers between devices: 110 us -> 49.6 us  [row_weight_grad(): lax.psum_scatter(grad.astype(bf16), 'fsdp', scatter_dimension=0, tiled=True)]
    all_gather x1, waiting for transfers between devices: 67.8 us -> 7.63 us  [shards(): wp = lax.all_gather(w_proj, 'fsdp', axis=0, tiled=True)]
    dot_general x12 -> x0, matrix products: 47.8 us -> none  [the longest x2 14.9 us: attend_back(): grad_probs = jnp.einsum('thd,ud->htu', g, v, preferred_element_type=f32)]
  transfers between devices with their start and end apart: 22 -> 10, of which waited for: 19 -> 4; matrix products, arithmetic and copies ran while one was open for 14% -> 12% of each run, Pallas kernels for 0% -> 34%
where the time goes in v2:
time: 715 us; the launch traced here: 709 us
  Pallas kernels  410 us (57%)
  waiting for transfers between devices  151 us (21%)
  matrix products  79.1 us (11%)
  other arithmetic  30.1 us (4%)
  blocking collectives  15.1 us (2%)
  between operations  15 us (2%)
  local copies, waits for them, and re-layouts  7.55 us (1%)
    pallas_call x4, Pallas kernels, matmul_scatter(): pl.pallas_call(kernel, out_shape=jax.ShapeDtypeStruct((rows, wide), f32),...  183 us
    pallas_call x2, Pallas kernels, gather_matmul(): pl.pallas_call(kernel, out_shape=[jax.ShapeDtypeStruct((total, depth), ow...  83.7 us
    pallas_call x1, Pallas kernels, gather_plane(): pl.pallas_call(kernel, out_shape=[jax.ShapeDtypeStruct((PLANE * b.shape[0...  76.9 us
    reduce_scatter x2, waiting for transfers between devices, column_weight_grad(): lax.psum_scatter(grad.astype(bf16).reshape(groups, rows // groups, cols),...  56 us
    reduce_scatter x3, waiting for transfers between devices, row_weight_grad(): lax.psum_scatter(grad.astype(bf16), 'fsdp', scatter_dimension=0, tiled=True)  49.6 us
    dot_general x5, matrix products, dot_tn(): lax.dot_general(a, b, (((0,), (0,)), ((), ())), preferred_element_type=f32)  49 us
    reduce_scatter x1, waiting for transfers between devices, shards(): lax.psum_scatter(dot_tn(hidden1, gkv_rows).astype(bf16), 'seq', scatter_d...  35.7 us
    pallas_call x1, Pallas kernels, last_exchange(): pl.pallas_call(kernel, out_shape=[jax.ShapeDtypeStruct(vector.shape, f32)...  23.8 us
  transfers between devices with their start and end apart: 10, of which 4 were waited for; matrix products, arithmetic and copies ran while one was open for 12% of the time, Pallas kernels for 34%

profile of v2, /device:TPU:0, one launch (start us, length us, event | category | flops | bytes accessed | tf_op | source)
XLA Modules:
  0.0 708.8 jit_solution(5334456172434220225)
XLA Ops:
  7.3 19.2 %split_columns.1 = (bf16[8,64,256]{2,1,0:T(8,128)(2,1)}, bf16[8,64,1024]{2,1,0:T(8,128)(2,1)}) custom-call(bf16[64,2048]{1,0:T(8,128)(2,1)} %refs_0_.1, bf16[64,8192]{1,0:T(8,128)(2,1)} %refs_1_.1), custom_call_target="tpu_custom_call" | custom-call | tf_op jit(solution)/shard_map/split_columns/pallas_call | solution.py:485
  30.6 15.1 %all_gather.15.refs_2_ = bf16[256,256]{1,0:T(8,128)(2,1)} all-gather(bf16[64,256]{1,0:T(8,128)(2,1)S(1)} %copy-done.13), channel_id=1, replica_groups=mesh['seq'=8,'fsdp'=4] {'fsdp'}, dimensions={0}, use_global_device_ids=true | all-gather | bytes 163840 | tf_op jit(solution)/shard_map/all_gather | solution.py:813
  47.8 76.9 %gather_plane.1 = (bf16[2048,2048]{1,0:T(8,128)(2,1)}, bf16[2048,2048]{1,0:T(8,128)(2,1)}, bf16[2048,256]{1,0:T(8,128)(2,1)}) custom-call(bf16[256,2048]{1,0:T(8,128)(2,1)} %fusion.10.refs_0_, bf16[256,2048]{1,0:T(8,128)(2,1)} %bitcast.68, bf16[256,256]{1,0:T(8,128)(2,1)} %all_gather.15.refs_2_), custom_call_target="tpu_custom_call" | custom-call | tf_op jit(solution)/shard_map/gather_plane/pallas_call | solution.py:204
  124.8 7.0 fusion.1
  131.8 7.1 fusion
  138.9 10.5 %attention_forward.1 = (bf16[8,2,128,256]{3,2,1,0:T(8,128)(2,1)}, f32[2,2,1024]{2,1,0:T(2,128)}) custom-call(s32[2,4]{1,0:T(2,128)} %docs_ref.3, bf16[8,2,128,256]{3,2,1,0:T(8,128)(2,1)} %bitcast.91, bf16[8,2,128,256]{3,2,1,0:T(8,128)(2,1)} %bitcast.89), custom_call_target="tpu_custom_call" | custom-call | flops 2147483648 | bytes 8388608 | tf_op jit(solution)/shard_map/attention_forward/pallas_call | solution.py:652
  149.4 43.3 %scatter_attn.1 = f32[256,2048]{1,0:T(8,128)} custom-call(bf16[2048,256]{1,0:T(8,128)(2,1)} %bitcast.70, bf16[256,2048]{1,0:T(8,128)(2,1)} %all-gather.7.cloned.1.call-done.refs_1_.w_ref), custom_call_target="tpu_custom_call" | custom-call | flops 2147483648 | bytes 41943040 | tf_op jit(solution)/shard_map/scatter_attn/pallas_call | solution.py:420
  196.8 44.8 %gather_fc.1 = (bf16[2048,2048]{1,0:T(8,128)(2,1)}, bf16[2048,1024]{1,0:T(8,128)(2,1)}, bf16[2048,1024]{1,0:T(8,128)(2,1)}) custom-call(bf16[256,2048]{1,0:T(8,128)(2,1)} %add_convert_fusion.own_ref, bf16[2048,1024]{1,0:T(8,128)(2,1)} %bitcast.85, f32[1,1024]{1,0:T(1,128)} %bitcast.84), custom_call_target="tpu_custom_call" | custom-call | flops 8589934592 | bytes 41943040 | tf_op jit(solution)/shard_map/gather_fc/pallas_call | solution.py:285
  241.6 7.6 %all-gather.11.cloned.1.call-done.refs_1_ = bf16[1024,2048]{1,0:T(8,128)(2,1)} async-done(((bf16[256,2048]{1,0:T(8,128)(2,1)}), bf16[1024,2048]{1,0:T(8,128)(2,1)}) %all-gather.11.cloned.1.call-update) | async-done | bytes 4194320 | tf_op jit(solution)/shard_map/all_gather | solution.py:817
  249.2 16.0 %convert_reduce_fusion = (f32[1024]{0:T(1024)S(1)}, bf16[2048,1024]{1,0:T(8,128)(2,1)}) fusion(bf16[2048,1024]{1,0:T(8,128)(2,1)} %get-tuple-element.40, bf16[2048,2048]{1,0:T(8,128)(2,1)} %get-tuple-element.39, bf16[1024,2048]{1,0:T(8,128)(2,1)} %all-gather.11.cloned.1.call-done.refs_1_), kind=kOutput, calls=%fused_computation | convolution fusion | flops 8600419328 | bytes 20975616 | tf_op jit(solution)/shard_map/dot_general | solution.py:56
  265.2 47.5 %scatter_fc.1 = f32[256,2048]{1,0:T(8,128)} custom-call(bf16[2048,1024]{1,0:T(8,128)(2,1)} %get-tuple-element.74.refs_0_, bf16[2048,1024]{1,0:T(8,128)(2,1)} %bitcast.86), custom_call_target="tpu_custom_call" | custom-call | flops 8589934592 | bytes 41943040 | tf_op jit(solution)/shard_map/scatter_fc/pallas_call | solution.py:420
  315.3 47.3 %scatter_proj.1 = f32[256,2048]{1,0:T(8,128)} custom-call(bf16[2048,1024]{1,0:T(8,128)(2,1)} %get-tuple-element.38.refs_0_, bf16[1024,2048]{1,0:T(8,128)(2,1)} %all-gather.11.cloned.1.call-done.refs_1_), custom_call_target="tpu_custom_call" | custom-call | flops 8589934592 | bytes 41943040 | tf_op jit(solution)/shard_map/scatter_proj/pallas_call | solution.py:420
  367.8 38.9 %gather_out.1 = (bf16[2048,2048]{1,0:T(8,128)(2,1)}, bf16[2048,256]{1,0:T(8,128)(2,1)}) custom-call(bf16[256,2048]{1,0:T(8,128)(2,1)} %get-tuple-element.59.own_ref, bf16[256,2048]{1,0:T(8,128)(2,1)} %all-gather.7.cloned.1.call-done.refs_1_.w_ref), custom_call_target="tpu_custom_call" | custom-call | flops 2147483648 | bytes 41943040 | tf_op jit(solution)/shard_map/gather_out/pallas_call | solution.py:285
  406.7 13.3 %attention_backward.1 = (bf16[8,2,128,256]{3,2,1,0:T(8,128)(2,1)}, bf16[8,2,128,256]{3,2,1,0:T(8,128)(2,1)}) custom-call(s32[2,4]{1,0:T(2,128)} %docs_ref.3, bf16[8,2,128,256]{3,2,1,0:T(8,128)(2,1)} %bitcast.92, bf16[8,2,128,256]{3,2,1,0:T(8,128)(2,1)} %bitcast.90, bf16[8,2,128,256]{3,2,1,0:T(8,128)(2,1)} %bitcast.93, f32[2,2,1024]{2,1,0:T(2,128)} %get-tuple-element.42.lse_ref), custom_call_target="tpu_custom_call" | custom-call | flops 5368709120 | bytes 8388608 | tf_op jit(solution)/shard_map/attention_backward/pallas_call | solution.py:711
  420.0 7.2 %convolution_convert_fusion.3 = bf16[2048,256]{1,0:T(8,128)(2,1)} fusion(bf16[2048,2048]{1,0:T(8,128)(2,1)} %get-tuple-element.33, bf16[2048,256]{1,0:T(8,128)(2,1)} %bitcast.77), kind=kOutput, calls=%fused_computation.9 | convolution fusion | flops 2148007936 | bytes 10485760 | tf_op jit(solution)/shard_map/dot_general | solution.py:60
  427.2 35.7 %reduce-scatter.11.cloned.1.call-done = bf16[256,256]{1,0:T(8,128)(2,1)} async-done(((bf16[2048,256]{1,0:T(8,128)(2,1)}), bf16[256,256]{1,0:T(8,128)(2,1)}) %reduce-scatter.11.cloned.1.call-update) | async-done | bytes 131088 | tf_op jit(solution)/shard_map/reduce_scatter | solution.py:882
  463.2 6.8 convolution_convert_fusion.2
  470.1 6.9 convolution_convert_fusion.4
  477.1 14.0 %convolution_convert_fusion.1 = bf16[2048,1024]{1,0:T(8,128)(2,1)} fusion(bf16[2048,2048]{1,0:T(8,128)(2,1)} %get-tuple-element.45, bf16[2048,1024]{1,0:T(8,128)(2,1)} %get-tuple-element.74.refs_0_), kind=kOutput, calls=%fused_computation.3 | convolution fusion | flops 8592031744 | bytes 16777216 | tf_op jit(solution)/shard_map/dot_general | solution.py:60
  491.5 14.0 %convolution_convert_fusion = bf16[1024,2048]{1,0:T(8,128)(2,1)} fusion(bf16[2048,1024]{1,0:T(8,128)(2,1)} %get-tuple-element.38.refs_0_, bf16[2048,2048]{1,0:T(8,128)(2,1)} %get-tuple-element.39), kind=kOutput, calls=%fused_computation.2 | convolution fusion | flops 8592031744 | bytes 16777216 | tf_op jit(solution)/shard_map/dot_general | solution.py:60
  507.8 44.7 %scatter_query.1 = f32[256,2048]{1,0:T(8,128)} custom-call(bf16[2048,256]{1,0:T(8,128)(2,1)} %bitcast.74, bf16[2048,256]{1,0:T(8,128)(2,1)} %bitcast.78, bf16[2048,256]{1,0:T(8,128)(2,1)} %bitcast.88, bf16[2048,256]{1,0:T(8,128)(2,1)} %get-tuple-element.35.refs_3_), custom_call_target="tpu_custom_call" | custom-call | flops 4294967296 | bytes 41943040 | tf_op jit(solution)/shard_map/scatter_query/pallas_call | solution.py:420
  562.6 56.0 %reduce-scatter.7.cloned.1.call-done.refs_0_ = bf16[8,64,1024]{2,1,0:T(8,128)(2,1)} async-done(((bf16[8,256,1024]{2,1,0:T(8,128)(2,1)}), bf16[8,64,1024]{2,1,0:T(8,128)(2,1)}) %reduce-scatter.7.cloned.1.call-update) | async-done | bytes 1048592 | tf_op jit(solution)/shard_map/reduce_scatter | solution.py:750
  618.5 23.8 %last_exchange.1 = (f32[8,24,128]{2,1,0:T(8,128)}, bf16[64,8192]{1,0:T(8,128)(2,1)}, bf16[64,2048]{1,0:T(8,128)(2,1)}) custom-call(f32[8,24,128]{2,1,0:T(8,128)} %bitcast.80, bf16[8,64,1024]{2,1,0:T(8,128)(2,1)} %reduce-scatter.7.cloned.1.call-done.refs_0_, bf16[8,64,256]{2,1,0:T(8,128)(2,1)} %reduce-scatter.9.cloned.1.call-done.refs_1_), custom_call_target="tpu_custom_call" | custom-call | tf_op jit(solution)/shard_map/last_exchange/pallas_call | solution.py:576
  649.1 49.6 %reduce-scatter.17.cloned.1.call-done = bf16[256,2048]{1,0:T(8,128)(2,1)} async-done(((bf16[1024,2048]{1,0:T(8,128)(2,1)}), bf16[256,2048]{1,0:T(8,128)(2,1)}) %reduce-scatter.17.cloned.1.call-update) | async-done | bytes 1048592 | tf_op jit(solution)/shard_map/reduce_scatter | solution.py:759
  (109 shorter events, 40.6 us)
Async XLA Ops:
  7.2 22.2 %copy-start.18 = (f32[128]{0:T(128)S(1)}, f32[128]{0:T(128)}, u32[]{:S(2)}) copy-start(f32[128]{0:T(128)} %param.27) | copy-start | bytes 1540
  7.2 23.4 %copy-start.13 = (bf16[64,256]{1,0:T(8,128)(2,1)S(1)}, bf16[64,256]{1,0:T(8,128)(2,1)}, u32[]{:S(2)}) copy-start(bf16[64,256]{1,0:T(8,128)(2,1)} %param.20) | copy-start | bytes 98308
  7.2 38.5 %copy-start = (bf16[2,128,2048]{2,1,0:T(8,128)(2,1)S(1)}, bf16[2,128,2048]{2,1,0:T(8,128)(2,1)}, u32[]{:S(2)}) copy-start(bf16[2,128,2048]{2,1,0:T(8,128)(2,1)} %param.17) | copy-start | bytes 3145732
  7.2 124.6 %all-gather.5.cloned.1.call-start = ((), (), s32[]{:S(2)}) async-start(), calls=%async_computation.6 | async-start | bytes 1310720 | tf_op jit(solution)/shard_map/all_gather | solution.py:744
  26.4 122.9 %all-gather.7.cloned.1.call-start = ((), (), s32[]{:S(2)}) async-start(), calls=%async_computation.7 | async-start | bytes 1310720 | tf_op jit(solution)/shard_map/all_gather | solution.py:814
  27.2 169.6 %all-gather.9.cloned.1.call-start = ((), (), s32[]{:S(2)}) async-start(), calls=%async_computation.8 | async-start | bytes 5242880 | tf_op jit(solution)/shard_map/all_gather | solution.py:744
  27.2 19.1 %copy-start.12 = (f32[2048]{0:T(1024)S(1)}, f32[2048]{0:T(1024)}, u32[]{:S(2)}) copy-start(f32[2048]{0:T(1024)} %param.24) | copy-start | bytes 24580
  27.3 19.1 %copy-start.14 = (f32[2048]{0:T(1024)S(1)}, f32[2048]{0:T(1024)}, u32[]{:S(2)}) copy-start(f32[2048]{0:T(1024)} %param.25) | copy-start | bytes 24580
  27.9 221.3 %all-gather.11.cloned.1.call-start = ((), (), s32[]{:S(2)}) async-start(), calls=%async_computation.9 | async-start | bytes 5242880 | tf_op jit(solution)/shard_map/all_gather | solution.py:817
  28.5 434.4 %reduce-scatter.11.cloned.1.call-start = ((), (), s32[]{:S(2)}) async-start(), calls=%async_computation.12 | async-start | bytes 1179648 | tf_op jit(solution)/shard_map/reduce_scatter | solution.py:882
  149.4 43.3 %copy-start.15 = (f32[2048]{0:T(1024)S(1)}, f32[2048]{0:T(1024)}, u32[]{:S(2)}) copy-start(f32[2048]{0:T(1024)} %param.28) | copy-start | bytes 24580
  315.2 47.4 %copy-start.1 = (bf16[2,128,2048]{2,1,0:T(8,128)(2,1)S(1)}, bf16[2,128,2048]{2,1,0:T(8,128)(2,1)}, u32[]{:S(2)}) copy-start(bf16[2,128,2048]{2,1,0:T(8,128)(2,1)} %param.33) | copy-start | bytes 3145732
  315.2 47.4 %copy-start.3 = (f32[256,2048]{1,0:T(8,128)S(1)}, f32[256,2048]{1,0:T(8,128)}, u32[]{:S(2)}) copy-start(f32[256,2048]{1,0:T(8,128)} %scatter_fc.1) | copy-start | bytes 6291460
  315.3 47.4 %copy-start.17 = (f32[2048]{0:T(1024)S(1)}, f32[2048]{0:T(1024)}, u32[]{:S(2)}) copy-start(f32[2048]{0:T(1024)} %param.32) | copy-start | bytes 24580
  427.1 36.1 %copy-start.5 = (bf16[8,2,128,256]{3,2,1,0:T(8,128)(2,1)S(1)}, bf16[8,2,128,256]{3,2,1,0:T(8,128)(2,1)}, u32[]{:S(2)}) copy-start(bf16[8,2,128,256]{3,2,1,0:T(8,128)(2,1)} %get-tuple-element.36) | copy-start | bytes 3145732
  427.1 132.2 %reduce-scatter.13.cloned.1.call-start = ((), (), s32[]{:S(2)}) async-start(), calls=%async_computation.13 | async-start | bytes 163840 | tf_op jit(solution)/shard_map/reduce_scatter | solution.py:759
  462.9 97.9 %reduce-scatter.15.cloned.1.call-start = ((), (), s32[]{:S(2)}) async-start(), calls=%async_computation.14 | async-start | bytes 1310720 | tf_op jit(solution)/shard_map/reduce_scatter | solution.py:759
  463.2 6.9 copy-start.6
  470.1 92.5 %reduce-scatter.9.cloned.1.call-start = ((), (), s32[]{:S(2)}) async-start(), calls=%async_computation.11 | async-start | bytes 1310720 | tf_op jit(solution)/shard_map/reduce_scatter | solution.py:750
  477.0 141.5 %reduce-scatter.7.cloned.1.call-start = ((), (), s32[]{:S(2)}) async-start(), calls=%async_computation.10 | async-start | bytes 5242880 | tf_op jit(solution)/shard_map/reduce_scatter | solution.py:750
  491.2 207.5 %reduce-scatter.17.cloned.1.call-start = ((), (), s32[]{:S(2)}) async-start(), calls=%async_computation.15 | async-start | bytes 5242880 | tf_op jit(solution)/shard_map/reduce_scatter | solution.py:759
  555.6 3.8 copy-start.9
  642.3 5.3 copy-start.7
  642.3 6.2 copy-start.10
  (5 other events, 8.6 us)
Sparse Core Ops, SparseCore 0:
  26.6 30.6 all-gather.4
  58.8 27.7 all-gather.6
  88.2 80.2 all-gather.8
  169.9 79.2 all-gather.10
  427.3 35.5 reduce-scatter.10
  465.0 19.1 reduce-scatter.12
  486.6 25.3 reduce-scatter.14
  514.8 25.7 reduce-scatter.8
  543.1 75.4 reduce-scatter.6
  620.7 77.9 reduce-scatter.16

commit v3 on v1

--- a/solution.py
+++ b/solution.py
@@ -1,6 +1,10 @@
+import functools
+
 import jax
 import jax.numpy as jnp
 from jax import lax
+from jax.experimental import pallas as pl
+from jax.experimental.pallas import tpu as pltpu
 from jax.sharding import PartitionSpec as P
 
 HEADS = 16
@@ -11,6 +15,11 @@
 epsilon = 1e-05
 f32 = jnp.float32
 bf16 = jnp.bfloat16
+MESH = pl.DeviceIdType.MESH
+ANY = pl.BlockSpec(memory_space=pl.ANY)
+WHOLE = pl.BlockSpec(memory_space=pltpu.VMEM)
+VMEM_LIMIT = 56 * 1024 * 1024
+PLANE = 8
 
 
 def normalize(values, gain_row, shift_row):
@@ -51,6 +60,1342 @@
     return lax.dot_general(a, b, (((0,), (0,)), ((), ())), preferred_element_type=f32)
 
 
+def push(src, dst, send, recv, to):
+    return pltpu.make_async_remote_copy(
+        src_ref=src, dst_ref=dst, send_sem=send, recv_sem=recv, device_id=to, device_id_type=MESH
+    )
+
+
+def sems(*shape):
+    return pltpu.SemaphoreType.DMA(shape)
+
+
+def rows_at(start, size):
+    return pl.ds(pl.multiple_of(start, size), size)
+
+
+class Place:
+    def __init__(self):
+        me = lax.axis_index("seq")
+        self.me = me
+        self.core = lax.rem(me, 2)
+        x = lax.rem(lax.div(me, 2), 2)
+        y = lax.div(me, 4)
+        self.sib = me + 1 - 2 * self.core
+        self.xn = me + 2 - 4 * x
+        self.yn = me + 4 - 8 * y
+        self.dg = me + 2 - 4 * x + 4 - 8 * y
+        turn = 1 - 2 * self.core
+        self.xs, self.ys, self.ds = self.xn + turn, self.yn + turn, self.dg + turn
+        self.layer = lax.axis_index("fsdp")
+
+    def plane_peer(self, step):
+        return lax.rem(self.me + step, PLANE)
+
+    def line_peer(self, step, layers):
+        return lax.rem(self.layer + step, layers)
+
+    def greet(self, whole_plane=False, layers=1):
+        barrier = pltpu.get_barrier_semaphore()
+        if whole_plane:
+            others = [self.plane_peer(step) for step in range(1, PLANE)]
+        else:
+            others = [self.sib, self.xn, self.yn]
+        for other in others:
+            pl.semaphore_signal(barrier, inc=1, device_id={"seq": other}, device_id_type=MESH)
+        for step in range(1, layers):
+            other = self.line_peer(step, layers)
+            pl.semaphore_signal(barrier, inc=1, device_id={"fsdp": other}, device_id_type=MESH)
+        pl.semaphore_wait(barrier, len(others) + layers - 1)
+
+
+class Gather:
+    sends = 14
+    scratch = [sems(14), sems(PLANE, 2)]
+
+    def __init__(self, place, buf, rows, send, recv):
+        self.p, self.buf, self.rows, self.half = place, buf, rows, rows // 2
+        self.send_sem, self.recv_sem = send, recv
+        self.copies = []
+
+    def piece(self, dev, half):
+        return self.buf.at[rows_at(dev * self.rows + half * self.half, self.half), :]
+
+    def pair(self, dev):
+        return rows_at(lax.div(dev, 2) * (2 * self.rows), 2 * self.rows)
+
+    def send(self, dev, half, to, src=None):
+        k = len(self.copies)
+        piece = self.piece(dev, half)
+        copy = push(
+            piece if src is None else src,
+            piece,
+            self.send_sem.at[k],
+            self.recv_sem.at[dev, half],
+            {"seq": to},
+        )
+        copy.start()
+        self.copies.append(copy)
+
+    def arrived(self, dev, half):
+        piece = self.piece(dev, half)
+        push(
+            piece, piece, self.send_sem.at[0], self.recv_sem.at[dev, half], {"seq": self.p.sib}
+        ).wait_recv()
+
+    def start(self, own):
+        p = self.p
+        parts = [own.at[pl.ds(h * self.half, self.half), :] for h in range(2)]
+        self.send(p.me, 0, p.yn, parts[0])
+        self.send(p.me, 1, p.xn, parts[1])
+        self.send(p.me, 1, p.yn, parts[1])
+        self.send(p.me, 0, p.xn, parts[0])
+        for h in range(2):
+            self.send(p.me, h, p.sib, parts[h])
+
+    def relay_first(self):
+        p = self.p
+        self.arrived(p.yn, 0)
+        self.send(p.yn, 0, p.xn)
+        self.arrived(p.xn, 1)
+        self.send(p.xn, 1, p.yn)
+        self.send(p.yn, 0, p.sib)
+        self.send(p.xn, 1, p.sib)
+
+    def relay_rest(self):
+        p = self.p
+        self.arrived(p.xn, 0)
+        self.send(p.xn, 0, p.sib)
+        self.arrived(p.yn, 1)
+        self.send(p.yn, 1, p.sib)
+
+    def relay(self):
+        self.relay_first()
+        self.relay_rest()
+
+    def have(self, dev):
+        self.arrived(dev, 0)
+        self.arrived(dev, 1)
+
+    def relay_corner(self):
+        p = self.p
+        for h in range(2):
+            self.arrived(p.dg, h)
+            self.send(p.dg, h, p.sib)
+
+    def finish(self):
+        for copy in self.copies:
+            copy.wait_send()
+
+
+class Scatter:
+    def __init__(self, place, rows, part, sib_out, sib_in, boxes, sib_send, sib_recv, send, recv):
+        self.p, self.rows, self.half = place, rows, rows // 2
+        self.part, self.sib_out, self.sib_in = part, sib_out, sib_in
+        self.out_d, self.out_x, self.out_y, self.in_d, self.in_x, self.in_y = boxes
+        self.sib_send, self.sib_recv, self.send, self.recv = sib_send, sib_recv, send, recv
+        self.copies = []
+
+    @staticmethod
+    def scratch(rows, wide):
+        return [
+            pltpu.VMEM((4, rows, wide), f32),
+            pltpu.VMEM((4, rows, wide), bf16),
+            pltpu.VMEM((4, rows, wide), bf16),
+            *[pltpu.VMEM((rows, wide), bf16)] * 6,
+            sems(4),
+            sems(4),
+            sems(6),
+            sems(6),
+        ]
+
+    @classmethod
+    def take(cls, place, rows, refs):
+        return cls(place, rows, refs[0], refs[1], refs[2], refs[3:9], *refs[9:13])
+
+    def swap(self, role, dev, product):
+        p = self.p
+        chip = lax.div(dev, 2) * (2 * self.rows)
+
+        def store_out(cols, value):
+            self.sib_out[role, :, cols] = value.astype(bf16)
+
+        def store_part(cols, value):
+            self.part[role, :, cols] = value
+
+        product(
+            rows_at(chip + (1 - p.core) * self.rows, self.rows),
+            rows_at(chip + p.core * self.rows, self.rows),
+            store_out,
+            store_part,
+        )
+        copy = push(
+            self.sib_out.at[role],
+            self.sib_in.at[role],
+            self.sib_send.at[role],
+            self.sib_recv.at[role],
+            {"seq": p.sib},
+        )
+        copy.start()
+        self.copies.append(copy)
+        return copy
+
+    def add_into(self, dst, role, first, size, more=()):
+        lines = 32
+
+        @pl.loop(0, size // lines)
+        def _(i):
+            line = rows_at(first + i * lines, lines)
+            value = self.part[role, line, :] + self.sib_in[role, line, :].astype(f32)
+            for ref in more:
+                value = value + ref[line, :].astype(f32)
+            dst[line, :] = value.astype(dst.dtype)
+
+    def ship(self, src, dst, h, k, to):
+        lines = pl.ds(h * self.half, self.half)
+        copy = push(
+            src.at[lines, :], dst.at[lines, :], self.send.at[k], self.recv.at[k], {"seq": to}
+        )
+        copy.start()
+        self.copies.append(copy)
+        return copy
+
+    def run(self, product, out_ref, idle=None):
+        p, rows, half = self.p, self.rows, self.half
+        to_d = self.swap(0, p.dg, product)
+        to_x = self.swap(1, p.xn, product)
+        to_d.wait_recv()
+        self.add_into(self.out_d, 0, 0, rows)
+        dx = self.ship(self.out_d, self.in_d, 0, 0, p.xn)
+        dy = self.ship(self.out_d, self.in_d, 1, 1, p.yn)
+        to_y = self.swap(2, p.yn, product)
+        to_x.wait_recv()
+        self.add_into(self.out_x, 1, 0, half)
+        x0 = self.ship(self.out_x, self.in_x, 0, 2, p.xn)
+        to_y.wait_recv()
+        self.add_into(self.out_y, 2, half, half)
+        y1 = self.ship(self.out_y, self.in_y, 1, 3, p.yn)
+        to_me = self.swap(3, p.me, product)
+        dy.wait_recv()
+        self.add_into(self.out_x, 1, half, half, (self.in_d,))
+        x1 = self.ship(self.out_x, self.in_x, 1, 4, p.xn)
+        dx.wait_recv()
+        self.add_into(self.out_y, 2, 0, half, (self.in_d,))
+        y0 = self.ship(self.out_y, self.in_y, 0, 5, p.yn)
+        if idle is not None:
+            idle()
+        to_me.wait_recv()
+        x0.wait_recv()
+        y0.wait_recv()
+        self.add_into(out_ref, 3, 0, half, (self.in_x, self.in_y))
+        y1.wait_recv()
+        x1.wait_recv()
+        self.add_into(out_ref, 3, half, half, (self.in_x, self.in_y))
+        for copy in self.copies:
+            copy.wait_send()
+
+
+def params(number, vmem=True):
+    return pltpu.CompilerParams(
+        collective_id=number,
+        has_side_effects=True,
+        vmem_limit_bytes=VMEM_LIMIT if vmem else None,
+    )
+
+
+def cost(flops, mib=40):
+    return pl.CostEstimate(flops=flops, bytes_accessed=mib * 1024 * 1024, transcendentals=0)
+
+
+def load(src, dst, sem):
+    copy = pltpu.make_async_copy(src, dst, sem)
+    copy.start()
+    return copy
+
+
+def split_weights(w_query, w_fc, w_kv, layers, number):
+    arrays = (w_query, w_fc)
+
+    def kernel(wq_ref, wf_ref, kv_ref, wq_out, wf_out, kv_out, send, recv, zsend, zrecv, local):
+        p = Place()
+        kv_rows = kv_ref.shape[0]
+        mine = kv_out.at[rows_at(p.layer * kv_rows, kv_rows), :]
+        ins, outs = (wq_ref, wf_ref), (wq_out, wf_out)
+
+        def block(i, dev):
+            cols = ins[i].shape[1] // PLANE
+            return ins[i].at[:, rows_at(dev * cols, cols)]
+
+        own = [load(kv_ref, mine, local.at[2])]
+        for i in range(2):
+            own.append(load(block(i, p.me), outs[i].at[p.me], local.at[i]))
+        p.greet(True, layers)
+        copies = []
+        for step in range(1, layers):
+            to = p.line_peer(step, layers)
+            copies.append(push(kv_ref, mine, zsend.at[step], zrecv.at[step], {"fsdp": to}))
+            copies[-1].start()
+        for i in range(2):
+            for step in range(1, PLANE):
+                to = p.plane_peer(step)
+                copies.append(
+                    push(
+                        block(i, to),
+                        outs[i].at[p.me],
+                        send.at[i, step],
+                        recv.at[i, step],
+                        {"seq": to},
+                    )
+                )
+                copies[-1].start()
+        for copy in own + copies:
+            copy.wait()
+
+    return pl.pallas_call(
+        kernel,
+        out_shape=[
+            jax.ShapeDtypeStruct((PLANE, a.shape[0], a.shape[1] // PLANE), a.dtype)
+            for a in arrays
+        ]
+        + [jax.ShapeDtypeStruct((layers * w_kv.shape[0], w_kv.shape[1]), w_kv.dtype)],
+        in_specs=[ANY] * 3,
+        out_specs=[ANY] * 3,
+        scratch_shapes=[
+            sems(2, PLANE),
+            sems(2, PLANE),
+            sems(layers),
+            sems(layers),
+            sems(3),
+        ],
+        compiler_params=params(number, False),
+        name="split_weights",
+    )(w_query, w_fc, w_kv)
+
+
+def gather_hidden1(hidden1, low_kv, wq_pieces, layers, number):
+    def kernel(h_ref, kv_ref, wq_ref, h_all, kv_all, wq_all, *refs):
+        hs, hr, ks, kr, zsend, zrecv, local = refs
+        p = Place()
+        h_rows, kv_rows = h_ref.shape[0], kv_ref.shape[0]
+        wq_mine = wq_all.at[:, p.layer]
+        own = [
+            load(h_ref, h_all.at[rows_at(p.me * h_rows, h_rows), :], local.at[0]),
+            load(kv_ref, kv_all.at[rows_at(p.me * kv_rows, kv_rows), :], local.at[1]),
+            load(wq_ref, wq_mine, local.at[2]),
+        ]
+        p.greet(False, layers)
+        kv = Gather(p, kv_all, kv_rows, ks, kr)
+        h = Gather(p, h_all, h_rows, hs, hr)
+        kv.start(kv_ref)
+        h.start(h_ref)
+        across = []
+        for step in range(1, layers):
+            to = p.line_peer(step, layers)
+            across.append(push(wq_ref, wq_mine, zsend.at[step], zrecv.at[step], {"fsdp": to}))
+            across[-1].start()
+        kv.relay()
+        kv.relay_corner()
+        h.relay()
+        h.relay_corner()
+        for g in (kv, h):
+            for dev in (p.sib, p.xs, p.ys, p.ds):
+                g.have(dev)
+            g.finish()
+        for copy in own + across:
+            copy.wait()
+
+    groups, piece_rows, cols = wq_pieces.shape
+    return pl.pallas_call(
+        kernel,
+        out_shape=[
+            jax.ShapeDtypeStruct((PLANE * hidden1.shape[0], hidden1.shape[1]), bf16),
+            jax.ShapeDtypeStruct((PLANE * low_kv.shape[0], low_kv.shape[1]), bf16),
+            jax.ShapeDtypeStruct((groups, layers, piece_rows, cols), bf16),
+        ],
+        in_specs=[ANY] * 3,
+        out_specs=[ANY] * 3,
+        scratch_shapes=Gather.scratch * 2 + [sems(layers), sems(layers), sems(3)],
+        compiler_params=params(number, False),
+        name="gather_hidden1",
+    )(hidden1, low_kv, wq_pieces)
+
+
+def project_attend(docs, hidden1, wq, w_kv, bq, bkv, cot, w_out, streams, heads, layers, number):
+    total, depth = hidden1.shape
+    cols, kv_cols = wq.shape[1], w_kv.shape[1]
+    rows = total // PLANE // streams
+    length = PLANE * rows
+    block = min(QROWS, length)
+    chunk = total // 4
+
+    def kernel(docs_ref, h_ref, wq_ref, wkv_ref, bq_ref, bkv_ref, cot_ref, wo_ref, *refs):
+        cot_all, wo_all, q_out, kv_out, mixed_out, lse_ref = refs[:6]
+        h_buf, wq_buf, wkv_buf, q_buf, kv_buf, mixed_buf = refs[6:12]
+        send, recv, zsend, zrecv, local = refs[12:]
+        p = Place()
+        own_rows = cot_ref.shape[0]
+        wo_rows = wo_ref.shape[0]
+        wo_mine = wo_all.at[rows_at(p.layer * wo_rows, wo_rows), :]
+
+        def fetch(k):
+            return load(
+                h_ref.at[pl.ds(k * chunk, chunk), :], h_buf.at[k % 2], local.at[k % 2]
+            )
+
+        fetches = [fetch(0)]
+        weights = [load(wq_ref, wq_buf, local.at[2]), load(wkv_ref, wkv_buf, local.at[3])]
+        own = [
+            load(cot_ref, cot_all.at[rows_at(p.me * own_rows, own_rows), :], local.at[4]),
+            load(wo_ref, wo_mine, local.at[8]),
+        ]
+        p.greet(False, layers)
+        g = Gather(p, cot_all, own_rows, send, recv)
+        g.start(cot_ref)
+        for step in range(1, layers):
+            to = p.line_peer(step, layers)
+            own.append(push(wo_ref, wo_mine, zsend.at[step], zrecv.at[step], {"fsdp": to}))
+            own[-1].start()
+        for copy in weights:
+            copy.wait()
+        per = chunk // (streams * rows)
+        for k in range(4):
+            fetches[k].wait()
+            if k < 3:
+                fetches.append(fetch(k + 1))
+            where = pl.ds(k * per, per)
+            q = dot(h_buf[k % 2], wq_buf[...]) + bq_ref[...]
+            q_buf[where] = q.astype(bf16).reshape(per, streams, rows, cols)
+            kv = dot(h_buf[k % 2], wkv_buf[...]) + bkv_ref[...]
+            kv_buf[where] = kv.astype(bf16).reshape(per, streams, rows, kv_cols)
+        stores = [load(q_buf, q_out, local.at[5]), load(kv_buf, kv_out, local.at[6])]
+        g.relay_first()
+        for stream in range(streams):
+            attend_stream(
+                docs_ref,
+                stream,
+                q_buf.at[:, stream],
+                kv_buf.at[:, stream],
+                mixed_buf.at[:, stream],
+                lse_ref.at[stream],
+                block,
+                heads,
+            )
+        stores.append(load(mixed_buf, mixed_out, local.at[7]))
+        g.relay_rest()
+        g.relay_corner()
+        for dev in (p.sib, p.xs, p.ys, p.ds):
+            g.have(dev)
+        g.finish()
+        for copy in own + stores:
+            copy.wait()
+
+    q_shape = (PLANE, streams, rows, cols)
+    kv_shape = (PLANE, streams, rows, kv_cols)
+    return pl.pallas_call(
+        kernel,
+        out_shape=[
+            jax.ShapeDtypeStruct((PLANE * cot.shape[0], cot.shape[1]), bf16),
+            jax.ShapeDtypeStruct((layers * w_out.shape[0], w_out.shape[1]), bf16),
+            jax.ShapeDtypeStruct(q_shape, bf16),
+            jax.ShapeDtypeStruct(kv_shape, bf16),
+            jax.ShapeDtypeStruct(q_shape, bf16),
+            jax.ShapeDtypeStruct((streams, heads, length), f32),
+        ],
+        in_specs=[pl.BlockSpec(memory_space=pltpu.SMEM)] + [ANY] * 3 + [WHOLE] * 2 + [ANY] * 2,
+        out_specs=[ANY] * 5 + [WHOLE],
+        scratch_shapes=[
+            pltpu.VMEM((2, chunk, depth), bf16),
+            pltpu.VMEM(wq.shape, bf16),
+            pltpu.VMEM(w_kv.shape, bf16),
+            pltpu.VMEM(q_shape, bf16),
+            pltpu.VMEM(kv_shape, bf16),
+            pltpu.VMEM(q_shape, bf16),
+        ]
+        + Gather.scratch
+        + [sems(layers), sems(layers), sems(9)],
+        compiler_params=params(number),
+        cost_estimate=cost(2 * total * depth * (cols + kv_cols)),
+        name="project_attend",
+    )(docs, hidden1, wq, w_kv, bq, bkv, cot, w_out)
+
+
+def gather_fc(hidden2, wf, bf, cot_all, number):
+    rows, depth = hidden2.shape
+    wide = wf.shape[1]
+    total = PLANE * rows
+    out_wide = cot_all.shape[1]
+    tile = 256
+
+    def kernel(own_ref, w_ref, b_ref, cot_ref, all_ref, act_ref, slope_ref, dw_ref, *refs):
+        buf, w_buf, act, slope, cot, acc, dw, send, recv, local = refs
+        p = Place()
+        load_own = load(own_ref, buf.at[rows_at(p.me * rows, rows), :], local.at[0])
+        load_w = load(w_ref, w_buf, local.at[1])
+        p.greet()
+        g = Gather(p, buf, rows, send, recv)
+        g.start(own_ref)
+        stores = []
+        cots = {}
+
+        def fetch(k, dev):
+            cots[k] = load(cot_ref.at[g.pair(dev), :], cot.at[k % 2], local.at[2 + k % 2])
+
+        def work(k, dev):
+            block = g.pair(dev)
+            stores.append(load(buf.at[block, :], all_ref.at[block, :], local.at[4 + 3 * k]))
+
+            @pl.loop(0, wide // tile)
+            def _(j):
+                cols = rows_at(j * tile, tile)
+                acc_fc = dot(buf[block, :], w_buf[:, cols]) + b_ref[:, cols]
+                activated, gradient = gelu_pair(acc_fc)
+                act[block, cols] = activated.astype(bf16)
+                slope[block, cols] = gradient.astype(bf16)
+
+            for i, (src, dst) in enumerate(((act, act_ref), (slope, slope_ref))):
+                stores.append(
+                    load(src.at[block, :], dst.at[block, :], local.at[4 + 3 * k + 1 + i])
+                )
+
+        def grads(k, dev):
+            block = g.pair(dev)
+            cots[k].wait()
+
+            @pl.loop(0, wide // tile)
+            def _(j):
+                cols = rows_at(j * tile, tile)
+                term = dot_tn(act[block, cols], cot[k % 2])
+                if k == 0:
+                    acc[cols, :] = term
+                elif k < 3:
+                    acc[cols, :] += term
+                else:
+                    dw[cols, :] = (acc[cols, :] + term).astype(bf16)
+
+        fetch(0, p.me)
+        fetch(1, p.xn)
+        load_own.wait()
+        load_w.wait()
+        g.have(p.sib)
+        work(0, p.me)
+        g.relay_first()
+        grads(0, p.me)
+        fetch(2, p.yn)
+        g.relay_rest()
+        g.have(p.xs)
+        work(1, p.xn)
+        g.have(p.ys)
+        work(2, p.yn)
+        grads(1, p.xn)
+        fetch(3, p.dg)
+        g.relay_corner()
+        grads(2, p.yn)
+        g.have(p.ds)
+        work(3, p.dg)
+        grads(3, p.dg)
+        stores.append(load(dw, dw_ref, local.at[16]))
+        g.finish()
+        for copy in stores:
+            copy.wait()
+
+    return pl.pallas_call(
+        kernel,
+        out_shape=[
+            jax.ShapeDtypeStruct((total, depth), bf16),
+            jax.ShapeDtypeStruct((total, wide), bf16),
+            jax.ShapeDtypeStruct((total, wide), bf16),
+            jax.ShapeDtypeStruct((wide, out_wide), bf16),
+        ],
+        in_specs=[ANY, ANY, WHOLE, ANY],
+        out_specs=[ANY] * 4,
+        scratch_shapes=[
+            pltpu.VMEM((total, depth), bf16),
+            pltpu.VMEM(wf.shape, bf16),
+            pltpu.VMEM((total, wide), bf16),
+            pltpu.VMEM((total, wide), bf16),
+            pltpu.VMEM((2, 2 * rows, out_wide), bf16),
+            pltpu.VMEM((wide, out_wide), f32),
+            pltpu.VMEM((wide, out_wide), bf16),
+        ]
+        + Gather.scratch
+        + [sems(17)],
+        compiler_params=params(number),
+        cost_estimate=cost(4 * total * depth * wide),
+        name="gather_fc",
+    )(hidden2, wf, bf, cot_all)
+
+
+def gather_out(grad_attn, wo, mixed, number):
+    rows, depth = grad_attn.shape
+    wide = wo.shape[0]
+    total = PLANE * rows
+
+    def kernel(own_ref, w_ref, mixed_ref, gm_ref, dw_ref, *refs):
+        buf, w_buf, mixed_buf, gm, acc, dw, send, recv, local = refs
+        p = Place()
+        load_own = load(own_ref, buf.at[rows_at(p.me * rows, rows), :], local.at[0])
+        loads = [load(w_ref, w_buf, local.at[1]), load(mixed_ref, mixed_buf, local.at[2])]
+        p.greet()
+        g = Gather(p, buf, rows, send, recv)
+        g.start(own_ref)
+
+        def work(dev):
+            block = g.pair(dev)
+            gm[block, :] = dot_nt(buf[block, :], w_buf[...]).astype(bf16)
+
+        def grads(k, dev):
+            block = g.pair(dev)
+            term = dot_tn(mixed_buf[block, :], buf[block, :])
+            if k == 0:
+                acc[...] = term
+            elif k < 3:
+                acc[...] += term
+            else:
+                dw[...] = (acc[...] + term).astype(bf16)
+
+        load_own.wait()
+        for copy in loads:
+            copy.wait()
+        g.have(p.sib)
+        work(p.me)
+        grads(0, p.me)
+        g.relay()
+        g.have(p.xs)
+        work(p.xn)
+        g.have(p.ys)
+        work(p.yn)
+        grads(1, p.xn)
+        g.relay_corner()
+        grads(2, p.yn)
+        g.have(p.ds)
+        work(p.dg)
+        store = load(gm, gm_ref, local.at[3])
+        grads(3, p.dg)
+        store_dw = load(dw, dw_ref, local.at[4])
+        g.finish()
+        store.wait()
+        store_dw.wait()
+
+    return pl.pallas_call(
+        kernel,
+        out_shape=[
+            jax.ShapeDtypeStruct((total, wide), bf16),
+            jax.ShapeDtypeStruct((wide, depth), bf16),
+        ],
+        in_specs=[ANY] * 3,
+        out_specs=[ANY] * 2,
+        scratch_shapes=[
+            pltpu.VMEM((total, depth), bf16),
+            pltpu.VMEM(wo.shape, bf16),
+            pltpu.VMEM(mixed.shape, bf16),
+            pltpu.VMEM((total, wide), bf16),
+            pltpu.VMEM((wide, depth), f32),
+            pltpu.VMEM((wide, depth), bf16),
+        ]
+        + Gather.scratch
+        + [sems(5)],
+        compiler_params=params(number),
+        cost_estimate=cost(4 * total * depth * wide),
+        name="gather_out",
+    )(grad_attn, wo, mixed)
+
+
+TILE = 512
+
+
+def scatter_attn(a, weight, number):
+    total, depth = a.shape
+    rows = total // PLANE
+    wide = weight.shape[1]
+
+    def kernel(a_ref, w_ref, out_ref, a_buf, w_buf, *refs):
+        s, local = refs[:13], refs[13]
+        p = Place()
+        loads = [load(a_ref, a_buf, local.at[0]), load(w_ref, w_buf, local.at[1])]
+        p.greet()
+        for copy in loads:
+            copy.wait()
+        Scatter.take(p, rows, s).run(plain_product(a_buf, w_buf), out_ref)
+
+    return pl.pallas_call(
+        kernel,
+        out_shape=jax.ShapeDtypeStruct((rows, wide), f32),
+        in_specs=[ANY] * 2,
+        out_specs=WHOLE,
+        scratch_shapes=[pltpu.VMEM(a.shape, bf16), pltpu.VMEM(weight.shape, bf16)]
+        + Scatter.scratch(rows, wide)
+        + [sems(2)],
+        compiler_params=params(number),
+        cost_estimate=cost(2 * total * depth * wide),
+        name="scatter_attn",
+    )(a, weight)
+
+
+def plain_product(a_buf, w_buf):
+    def product(theirs, ours, store_out, store_part):
+        @pl.loop(0, w_buf.shape[1] // TILE)
+        def _(j):
+            cols = rows_at(j * TILE, TILE)
+            store_out(cols, dot(a_buf[theirs, :], w_buf[:, cols]))
+            store_part(cols, dot(a_buf[ours, :], w_buf[:, cols]))
+
+    return product
+
+
+def scatter_fc(cot_all, slope, wp, wf, hidden2, number):
+    total, depth = cot_all.shape
+    rows = total // PLANE
+    wide = wp.shape[0]
+    tile = 256
+
+    def kernel(cot_ref, slope_ref, wp_ref, wf_ref, h_ref, out_ref, bias_ref, dw_ref, *refs):
+        cot, slopes, wp_buf, wf_buf, gp, h_buf, dw_buf = refs[:7]
+        s = refs[7:20]
+        (local,) = refs[20:]
+        p = Place()
+        order = (p.dg, p.xn, p.yn, p.me)
+
+        def chip(dev):
+            return rows_at(lax.div(dev, 2) * (2 * rows), 2 * rows)
+
+        def fetch(k):
+            here = chip(order[k])
+            return (
+                load(cot_ref.at[here, :], cot.at[k % 2], local.at[k % 2]),
+                load(slope_ref.at[here, :], slopes.at[k % 2], local.at[2 + k % 2]),
+            )
+
+        fetches = [fetch(0)]
+        load_wp = load(wp_ref, wp_buf, local.at[4])
+        load_wf = load(wf_ref, wf_buf, local.at[5])
+        bias_ref[...] = jnp.zeros_like(bias_ref)
+        p.greet()
+        load_wp.wait()
+        count = []
+
+        def product(theirs, ours, store_out, store_part):
+            k = len(count)
+            count.append(k)
+            for copy in fetches[k]:
+                copy.wait()
+            if k < 3:
+                fetches.append(fetch(k + 1))
+            here = chip(order[k])
+
+            @pl.loop(0, wide // tile)
+            def _(j):
+                cols = rows_at(j * tile, tile)
+                grad_act = dot_nt(cot[k % 2], wp_buf[cols, :])
+                grad_pre = (grad_act * slopes[k % 2, :, cols].astype(f32)).astype(bf16)
+                gp[here, cols] = grad_pre
+                bias_ref[:, cols] += jnp.sum(grad_pre.astype(f32), axis=0, keepdims=True)
+
+            if k == 0:
+                load_wf.wait()
+
+            @pl.loop(0, depth // TILE)
+            def _(j):
+                cols = rows_at(j * TILE, TILE)
+                store_out(cols, dot_nt(gp[theirs, :], wf_buf[cols, :]))
+                store_part(cols, dot_nt(gp[ours, :], wf_buf[cols, :]))
+
+        steps = depth // tile
+
+        def h_fetch(i):
+            return load(
+                h_ref.at[:, pl.ds(i * tile, tile)], h_buf.at[i % 2], local.at[6 + i % 2]
+            )
+
+        def idle():
+            tiles = [h_fetch(0)]
+            stores = []
+            for i in range(steps):
+                tiles[i].wait()
+                if i + 1 < steps:
+                    tiles.append(h_fetch(i + 1))
+                if i >= 2:
+                    stores[i - 2].wait()
+                dw_buf[i % 2] = dot_tn(h_buf[i % 2], gp[...]).astype(bf16)
+                stores.append(
+                    load(
+                        dw_buf.at[i % 2],
+                        dw_ref.at[pl.ds(i * tile, tile), :],
+                        local.at[8 + i % 2],
+                    )
+                )
+            for copy in stores[-2:]:
+                copy.wait()
+
+        Scatter.take(p, rows, s).run(product, out_ref, idle)
+
+    return pl.pallas_call(
+        kernel,
+        out_shape=[
+            jax.ShapeDtypeStruct((rows, depth), f32),
+            jax.ShapeDtypeStruct((1, wide), f32),
+            jax.ShapeDtypeStruct((depth, wide), bf16),
+        ],
+        in_specs=[ANY] * 5,
+        out_specs=[WHOLE, WHOLE, ANY],
+        scratch_shapes=[
+            pltpu.VMEM((2, 2 * rows, depth), bf16),
+            pltpu.VMEM((2, 2 * rows, wide), bf16),
+            pltpu.VMEM(wp.shape, bf16),
+            pltpu.VMEM(wf.shape, bf16),
+            pltpu.VMEM((total, wide), bf16),
+            pltpu.VMEM((2, total, tile), bf16),
+            pltpu.VMEM((2, tile, wide), bf16),
+        ]
+        + Scatter.scratch(rows, depth)
+        + [sems(10)],
+        compiler_params=params(number),
+        cost_estimate=cost(6 * total * depth * wide),
+        name="scatter_fc",
+    )(cot_all, slope, wp, wf, hidden2)
+
+
+class LineSum:
+    def __init__(self, place, block, box, layers, send, recv):
+        self.copies = []
+        self.box = box
+        for step in range(1, layers):
+            to = place.line_peer(step, layers)
+            copy = push(block(to), box.at[step - 1], send.at[step], recv.at[step], {"fsdp": to})
+            copy.start()
+            self.copies.append(copy)
+
+    def arrived(self):
+        for copy in self.copies:
+            copy.wait_recv()
+
+    def total(self, own, where):
+        value = own.astype(f32)
+        for k in range(len(self.copies)):
+            value = value + self.box[(k, *where)].astype(f32)
+        return value
+
+    def finish(self):
+        for copy in self.copies:
+            copy.wait_send()
+
+
+def scatter_query(gq, gkv, wq, w_kv, hidden1, grad_w_out, layers, number):
+    total, cols = gq.shape
+    kv_cols = gkv.shape[1]
+    rows = total // PLANE
+    depth = wq.shape[0]
+    part_rows = depth // PLANE
+    out_rows = grad_w_out.shape[0] // layers
+    out_wide = grad_w_out.shape[1]
+
+    def kernel(gq_ref, gkv_ref, wq_ref, wkv_ref, h_ref, dwo_ref, *refs):
+        out_ref, dwq_ref, dwkv_ref, dwo_out = refs[:4]
+        g_buf, wq_buf, wkv_buf, h_buf, dwq_buf, dkv, box, dwo_own, dwo_box = refs[4:13]
+        s = refs[13:26]
+        ksend, krecv, zsend, zrecv, local = refs[26:]
+        p = Place()
+
+        def dwo_block(layer):
+            return dwo_ref.at[rows_at(layer * out_rows, out_rows), :]
+
+        load_dwo = load(dwo_block(p.layer), dwo_own, local.at[7])
+        q_part, kv_part = pl.ds(0, cols), pl.ds(cols, kv_cols)
+        loads = [
+            load(gq_ref, g_buf.at[:, q_part], local.at[0]),
+            load(gkv_ref, g_buf.at[:, kv_part], local.at[1]),
+            load(wq_ref, wq_buf, local.at[2]),
+            load(wkv_ref, wkv_buf, local.at[3]),
+        ]
+
+        def h_fetch(i):
+            dev = p.plane_peer((i + 1) % PLANE)
+            return load(
+                h_ref.at[:, rows_at(dev * part_rows, part_rows)],
+                h_buf.at[i % 2],
+                local.at[4 + i % 2],
+            )
+
+        tiles = [h_fetch(0)]
+        p.greet(True, layers)
+        line = LineSum(p, dwo_block, dwo_box, layers, zsend, zrecv)
+        for copy in loads:
+            copy.wait()
+
+        def product(theirs, ours, store_out, store_part):
+            @pl.loop(0, depth // TILE)
+            def _(j):
+                where = rows_at(j * TILE, TILE)
+                for rows_of, store in ((theirs, store_out), (ours, store_part)):
+                    store(
+                        where,
+                        dot_nt(g_buf[rows_of, q_part], wq_buf[where, :])
+                        + dot_nt(g_buf[rows_of, kv_part], wkv_buf[where, :]),
+                    )
+
+        sent = []
+
+        def idle():
+            for i in range(PLANE):
+                step = (i + 1) % PLANE
+                dev = p.plane_peer(step)
+                tiles[i].wait()
+                if i + 1 < PLANE:
+                    tiles.append(h_fetch(i + 1))
+                term = dot_tn(h_buf[i % 2], g_buf[...]).astype(bf16)
+                dwq_buf[rows_at(dev * part_rows, part_rows), :] = term[:, :cols]
+                dkv[step] = term[:, cols:]
+                if step:
+                    copy = push(
+                        dkv.at[step], box.at[step], ksend.at[step], krecv.at[step], {"seq": dev}
+                    )
+                    copy.start()
+                    sent.append(copy)
+
+        Scatter.take(p, rows, s).run(product, out_ref, idle)
+        store = load(dwq_buf, dwq_ref, local.at[6])
+        sum_kv = dkv[0].astype(f32)
+        for i, copy in enumerate(sent):
+            copy.wait_recv()
+            sum_kv = sum_kv + box[i + 1].astype(f32)
+        dwkv_ref[...] = sum_kv.astype(bf16)
+        load_dwo.wait()
+        line.arrived()
+
+        @pl.loop(0, out_rows // 16)
+        def _(i):
+            lines = rows_at(i * 16, 16)
+            dwo_out[lines, :] = line.total(dwo_own[lines, :], (lines, slice(None)))
+
+        for copy in sent:
+            copy.wait_send()
+        line.finish()
+        store.wait()
+
+    return pl.pallas_call(
+        kernel,
+        out_shape=[
+            jax.ShapeDtypeStruct((rows, depth), f32),
+            jax.ShapeDtypeStruct((depth, cols), bf16),
+            jax.ShapeDtypeStruct((part_rows, kv_cols), bf16),
+            jax.ShapeDtypeStruct((out_rows, out_wide), f32),
+        ],
+        in_specs=[ANY] * 6,
+        out_specs=[WHOLE, ANY, WHOLE, WHOLE],
+        scratch_shapes=[
+            pltpu.VMEM((total, cols + kv_cols), bf16),
+            pltpu.VMEM(wq.shape, bf16),
+            pltpu.VMEM(w_kv.shape, bf16),
+            pltpu.VMEM((2, total, part_rows), bf16),
+            pltpu.VMEM((depth, cols), bf16),
+            pltpu.VMEM((PLANE, part_rows, kv_cols), bf16),
+            pltpu.VMEM((PLANE, part_rows, kv_cols), bf16),
+            pltpu.VMEM((out_rows, out_wide), bf16),
+            pltpu.VMEM((layers - 1, out_rows, out_wide), bf16),
+        ]
+        + Scatter.scratch(rows, depth)
+        + [sems(PLANE), sems(PLANE), sems(layers), sems(layers), sems(8)],
+        compiler_params=params(number),
+        cost_estimate=cost(4 * total * depth * (cols + kv_cols)),
+        name="scatter_query",
+    )(gq, gkv, wq, w_kv, hidden1, grad_w_out)
+
+
+def scatter_proj(act, wp, fc_pieces, grad_w_query, grad_w_kv, vector, layers, number):
+    total, depth = act.shape
+    rows = total // PLANE
+    wide = wp.shape[1]
+    lines = vector.shape[1]
+    q_rows, q_cols = grad_w_query.shape[2:]
+    kv_rows, kv_cols = grad_w_kv.shape[0] // layers, grad_w_kv.shape[1]
+    fc_rows, fc_cols = fc_pieces.shape[1:]
+
+    def kernel(act_ref, wp_ref, fc_ref, dwq_ref, dwkv_ref, vec, *refs):
+        out_ref, fc_out, q_out, kv_out, vec_out = refs[:5]
+        a_buf, w_buf, q_own, q_box, q_sum, kv_own, kv_box, box, plane_sum, zbox = refs[5:15]
+        s = refs[15:28]
+        (fsend, frecv, qsend, qrecv, qzsend, qzrecv, kzsend, kzrecv, vsend, vrecv, zsend, zrecv) = (
+            refs[28:40]
+        )
+        gsend, grecv, local = refs[40:]
+        p = Place()
+
+        def q_block(layer):
+            return dwq_ref.at[:, layer]
+
+        def kv_block(layer):
+            return dwkv_ref.at[rows_at(layer * kv_rows, kv_rows), :]
+
+        fc_place = fc_out.at[:, rows_at(p.me * fc_cols, fc_cols)]
+        q_place = q_out.at[:, rows_at(p.me * q_cols, q_cols)]
+        loads = [load(act_ref, a_buf, local.at[0]), load(wp_ref, w_buf, local.at[1])]
+        own_q = load(q_block(p.layer), q_own, local.at[2])
+        own_kv = load(kv_block(p.layer), kv_own, local.at[3])
+        ends = [load(fc_ref.at[p.me], fc_place, local.at[4])]
+        p.greet(True, layers)
+        first = []
+        for step in range(1, PLANE):
+            to = p.plane_peer(step)
+            copy = push(vec.at[to], box.at[step], vsend.at[step], vrecv.at[step], {"seq": to})
+            copy.start()
+            first.append(copy)
+        line_q = LineSum(p, q_block, q_box, layers, qzsend, qzrecv)
+        line_kv = LineSum(p, kv_block, kv_box, layers, kzsend, kzrecv)
+        for copy in loads:
+            copy.wait()
+        sent = []
+
+        def spread(src, dst, send, recv):
+            for step in range(1, PLANE):
+                to = p.plane_peer(step)
+                copy = push(src.at[to], dst, send.at[step], recv.at[step], {"seq": to})
+                copy.start()
+                ends.append(copy)
+
+        def idle():
+            spread(fc_ref, fc_place, fsend, frecv)
+            total_vec = vec[p.me]
+            for step in range(1, PLANE):
+                first[step - 1].wait_recv()
+                total_vec = total_vec + box[step]
+            plane_sum[...] = total_vec
+            zbox[0] = total_vec
+            for step in range(1, layers):
+                to = p.line_peer(step, layers)
+                copy = push(plane_sum, zbox.at[step], zsend.at[step], zrecv.at[step], {"fsdp": to})
+                copy.start()
+                sent.append(copy)
+            own_q.wait()
+            line_q.arrived()
+
+            @pl.loop(0, PLANE)
+            def _(i):
+                q_sum[i] = line_q.total(q_own[i], (i,)).astype(bf16)
+
+            ends.append(load(q_sum.at[p.me], q_place, local.at[5]))
+            spread(q_sum, q_place, qsend, qrecv)
+            own_kv.wait()
+            line_kv.arrived()
+            kv_out[...] = line_kv.total(kv_own[...], ())
+            for copy in sent:
+                copy.wait_recv()
+            total_vec = None
+            for k in range(layers):
+                term = zbox[lax.rem(p.layer - k + layers, layers)]
+                total_vec = term if total_vec is None else total_vec + term
+            vec_out[p.me] = total_vec
+            for step in range(1, PLANE):
+                to = p.plane_peer(step)
+                mine = vec_out.at[p.me]
+                copy = push(mine, mine, gsend.at[step], grecv.at[step], {"seq": to})
+                copy.start()
+                ends.append(copy)
+
+        Scatter.take(p, rows, s).run(plain_product(a_buf, w_buf), out_ref, idle)
+        for copy in first + sent:
+            copy.wait_send()
+        line_q.finish()
+        line_kv.finish()
+        for copy in ends:
+            copy.wait()
+
+    return pl.pallas_call(
+        kernel,
+        out_shape=[
+            jax.ShapeDtypeStruct((rows, wide), f32),
+            jax.ShapeDtypeStruct((fc_rows, PLANE * fc_cols), bf16),
+            jax.ShapeDtypeStruct((q_rows, PLANE * q_cols), bf16),
+            jax.ShapeDtypeStruct((kv_rows, kv_cols), f32),
+            jax.ShapeDtypeStruct(vector.shape, f32),
+        ],
+        in_specs=[ANY] * 5 + [WHOLE],
+        out_specs=[WHOLE, ANY, ANY, WHOLE, WHOLE],
+        scratch_shapes=[
+            pltpu.VMEM(act.shape, bf16),
+            pltpu.VMEM(wp.shape, bf16),
+            pltpu.VMEM((PLANE, q_rows, q_cols), bf16),
+            pltpu.VMEM((layers - 1, PLANE, q_rows, q_cols), bf16),
+            pltpu.VMEM((PLANE, q_rows, q_cols), bf16),
+            pltpu.VMEM((kv_rows, kv_cols), bf16),
+            pltpu.VMEM((layers - 1, kv_rows, kv_cols), bf16),
+            pltpu.VMEM((PLANE, lines, 128), f32),
+            pltpu.VMEM((lines, 128), f32),
+            pltpu.VMEM((layers, lines, 128), f32),
+        ]
+        + Scatter.scratch(rows, wide)
+        + [sems(PLANE)] * 4
+        + [sems(layers)] * 4
+        + [sems(PLANE)] * 2
+        + [sems(layers)] * 2
+        + [sems(PLANE)] * 2
+        + [sems(6)],
+        compiler_params=params(number),
+        cost_estimate=cost(2 * total * depth * wide),
+        name="scatter_proj",
+    )(act, wp, fc_pieces, grad_w_query, grad_w_kv, vector)
+
+
+def starts_of(docs, stream, positions):
+    start = jnp.zeros_like(positions)
+    for j in range(docs.shape[1]):
+        here = docs[stream, j]
+        start = jnp.maximum(start, jnp.where(here <= positions, here, 0))
+    return start
+
+
+def masked_scores(docs, stream, keys, q, first, limit):
+    scores = dot_nt(keys, q) * (HD**-0.5)
+    t = first + lax.broadcasted_iota(jnp.int32, (1, q.shape[0]), 1)
+    u = lax.broadcasted_iota(jnp.int32, scores.shape, 0)
+    return scores, (u >= starts_of(docs, stream, t)) & (u <= t)
+
+
+QROWS = 256
+
+
+def attend_stream(docs, stream, q_ref, kv_ref, mixed_ref, lse_ref, block, heads):
+    groups, rows, cols = q_ref.shape
+    length = groups * rows
+    kv = kv_ref[...].reshape(length, 2 * HD)
+    keys = kv[:, :HD]
+    values_t = kv[:, HD:].T
+    per = block // rows
+    for b in range(length // block):
+        limit = (b + 1) * block
+        q_rows = q_ref[b * per : (b + 1) * per].reshape(block, cols)
+        for h in range(heads):
+            q = q_rows[:, h * HD : (h + 1) * HD]
+            scores, allowed = masked_scores(docs, stream, keys[:limit], q, b * block, limit)
+            scores = jnp.where(allowed, scores, -1e30)
+            top = jnp.max(scores, axis=0, keepdims=True)
+            weights = jnp.exp(scores - top)
+            total = jnp.sum(weights, axis=0, keepdims=True)
+            mixed = dot(values_t[:, :limit], weights.astype(bf16)) / total
+            mixed_ref[b * per : (b + 1) * per, :, h * HD : (h + 1) * HD] = (
+                mixed.T.astype(bf16).reshape(per, rows, HD)
+            )
+            lse_ref[h : h + 1, b * block : (b + 1) * block] = top + jnp.log(total)
+
+
+def attention_backward(docs, queries, keyval, grads, lse, heads):
+    groups, streams, rows, cols = queries.shape
+    length = groups * rows
+    block = min(QROWS, length)
+
+    def kernel(docs_ref, q_ref, kv_ref, g_ref, lse_ref, gq_ref, gkv_ref, gk, gv):
+        stream = pl.program_id(0)
+        kv = kv_ref[...].reshape(length, 2 * HD)
+        keys, values = kv[:, :HD], kv[:, HD:]
+        keys_t = keys.T
+        per = block // rows
+        gk[...] = jnp.zeros_like(gk)
+        gv[...] = jnp.zeros_like(gv)
+        for b in range(length // block):
+            limit = (b + 1) * block
+            q_rows = q_ref[b * per : (b + 1) * per].reshape(block, cols)
+            g_rows = g_ref[b * per : (b + 1) * per].reshape(block, cols)
+            for h in range(heads):
+                q = q_rows[:, h * HD : (h + 1) * HD]
+                g = g_rows[:, h * HD : (h + 1) * HD]
+                scores, allowed = masked_scores(
+                    docs_ref, stream, keys[:limit], q, b * block, limit
+                )
+                shift = lse_ref[h : h + 1, b * block : (b + 1) * block]
+                probs = jnp.where(allowed, jnp.exp(scores - shift), 0.0)
+                grad_probs = dot_nt(values[:limit], g)
+                weighted = probs * grad_probs
+                delta = jnp.sum(weighted, axis=0, keepdims=True)
+                grad_scores = (weighted - probs * delta).astype(bf16)
+                gq = dot(keys_t[:, :limit], grad_scores) * (HD**-0.5)
+                gq_ref[b * per : (b + 1) * per, :, h * HD : (h + 1) * HD] = (
+                    gq.T.astype(bf16).reshape(per, rows, HD)
+                )
+                gk[:limit, :] += dot(grad_scores, q)
+                gv[:limit, :] += dot(probs.astype(bf16), g)
+        gkv_ref[:, :, :HD] = (gk[...] * (HD**-0.5)).astype(bf16).reshape(groups, rows, HD)
+        gkv_ref[:, :, HD:] = gv[...].astype(bf16).reshape(groups, rows, HD)
+
+    spec = pl.BlockSpec((groups, None, rows, cols), lambda s: (0, s, 0, 0))
+    spec_kv = pl.BlockSpec((groups, None, rows, 2 * HD), lambda s: (0, s, 0, 0))
+    return pl.pallas_call(
+        kernel,
+        grid=(streams,),
+        out_shape=[
+            jax.ShapeDtypeStruct(queries.shape, bf16),
+            jax.ShapeDtypeStruct(keyval.shape, bf16),
+        ],
+        in_specs=[
+            pl.BlockSpec(memory_space=pltpu.SMEM),
+            spec,
+            spec_kv,
+            spec,
+            pl.BlockSpec((None, heads, length), lambda s: (s, 0, 0)),
+        ],
+        out_specs=[spec, spec_kv],
+        scratch_shapes=[pltpu.VMEM((length, HD), f32)] * 2,
+        compiler_params=pltpu.CompilerParams(vmem_limit_bytes=VMEM_LIMIT),
+        cost_estimate=pl.CostEstimate(
+            flops=10 * streams * heads * length * length * HD,
+            bytes_accessed=8 * 1024 * 1024,
+            transcendentals=streams * heads * length * length,
+        ),
+        name="attention_backward",
+    )(docs, queries, keyval, grads, lse)
+
+
+def pack_vectors(vectors):
+    sizes = [v.shape[0] for v in vectors]
+    lines = -(-sum(sizes) // (PLANE * 8 * 128)) * 8
+    pad = PLANE * lines * 128 - sum(sizes)
+    return jnp.concatenate(vectors + (jnp.zeros((pad,), f32),)).reshape(PLANE, lines, 128)
+
+
+def unpack_vectors(packed, vectors):
+    flat = packed.reshape(-1)
+    sums, at = [], 0
+    for v in vectors:
+        sums.append(flat[at : at + v.shape[0]])
+        at += v.shape[0]
+    return sums
+
+
+def after(value, *earlier):
+    return lax.optimization_barrier((value, *earlier))[0]
+
+
+def line_gather(shard, axis=0):
+    return lax.all_gather(shard, "fsdp", axis=axis, tiled=True)
+
+
+def line_scatter(grad, axis=0):
+    return lax.psum_scatter(grad.astype(bf16), "fsdp", scatter_dimension=axis, tiled=True)
+
+
+def column_weight_grad(grad, groups):
+    rows, cols = grad.shape
+    return line_scatter(grad.reshape(groups, rows // groups, cols), 1)
+
+
+def shards(
+    tokens,
+    doc_starts,
+    w_query,
+    w_kv,
+    w_out,
+    w_fc,
+    w_proj,
+    ln1_gain,
+    ln1_bias,
+    b_query,
+    b_value,
+    b_out,
+    ln2_gain,
+    ln2_bias,
+    b_fc,
+    b_proj,
+    cotangent,
+):
+    layers = lax.axis_size("fsdp")
+    me = lax.axis_index("seq")
+    streams, rows, width = tokens.shape
+    own = streams * rows
+    heads = HEADS // PLANE
+    hidden = b_fc.shape[0]
+    my_cols = heads * HD
+    my_hidden = hidden // PLANE
+    total = PLANE * own
+
+    inputs = tokens.reshape(own, width).astype(f32)
+    cot_low = cotangent.reshape(own, width)
+    cot_full = cot_low.astype(f32)
+
+    wq_pieces, wf_pieces, low_kv = split_weights(w_query, w_fc, w_kv, layers, 1)
+    wf = line_gather(wf_pieces, 1).reshape(width, my_hidden)
+    wp = line_gather(w_proj)
+    my_bq = lax.dynamic_slice_in_dim(b_query, me * my_cols, my_cols, 0).reshape(1, my_cols)
+    my_bf = lax.dynamic_slice_in_dim(b_fc, me * my_hidden, my_hidden, 0).reshape(1, my_hidden)
+    bkv = jnp.concatenate([jnp.zeros((HD,), f32), b_value]).reshape(1, 2 * HD)
+
+    shifted1, normed1, inverse1 = normalize(inputs, ln1_gain, ln1_bias)
+    hidden1, w_kv_all, wq = gather_hidden1(shifted1.astype(bf16), low_kv, wq_pieces, layers, 2)
+    wq = wq.reshape(width, my_cols)
+    cot_all, wo, queries, keyval, mixed, lse = project_attend(
+        doc_starts, hidden1, wq, w_kv_all, my_bq, bkv, cot_low, w_out, streams, heads, layers, 3
+    )
+    mixed_rows = mixed.reshape(total, my_cols)
+    residual = inputs + scatter_attn(mixed_rows, wo, 4) + b_out
+    shifted2, normed2, inverse2 = normalize(residual, ln2_gain, ln2_bias)
+    hidden2, act_low, slope, grad_w_proj = gather_fc(shifted2.astype(bf16), wf, my_bf, cot_all, 5)
+    shard_proj = line_scatter(grad_w_proj)
+    grad_b_proj = jnp.sum(cot_full, axis=0)
+
+    grad_hidden2, my_grad_b_fc, grad_w_fc = scatter_fc(cot_all, slope, wp, wf, hidden2, 6)
+    fc_pieces = column_weight_grad(grad_w_fc, PLANE)
+    back_second, grad_ln2_gain, grad_ln2_bias = normalize_back(
+        grad_hidden2, normed2, inverse2, ln2_gain
+    )
+    grad_residual = cot_full + back_second
+    grad_attn = grad_residual.astype(bf16)
+    grad_b_out = jnp.sum(grad_attn.astype(f32), axis=0)
+    grad_mixed, grad_w_out = gather_out(grad_attn, wo, mixed_rows, 7)
+    gq, gkv = attention_backward(
+        doc_starts,
+        queries,
+        keyval,
+        after(grad_mixed, shard_proj).reshape(PLANE, streams, rows, my_cols),
+        lse,
+        heads,
+    )
+    gq_rows = gq.reshape(total, my_cols)
+    gkv_rows = gkv.reshape(total, 2 * HD)
+    grad_hidden1, grad_w_query, grad_w_kv, shard_out = scatter_query(
+        gq_rows, gkv_rows, wq, w_kv_all, hidden1, grad_w_out, layers, 8
+    )
+    my_grad_b_query = jnp.sum(gq_rows.astype(f32), axis=0)
+    grad_b_value = jnp.sum(gkv_rows[:, HD:].astype(f32), axis=0)
+    back_first, grad_ln1_gain, grad_ln1_bias = normalize_back(
+        grad_hidden1, normed1, inverse1, ln1_gain
+    )
+    input_grad = grad_residual + back_first
+    zero = jnp.zeros_like
+    grad_b_query = lax.dynamic_update_slice_in_dim(zero(b_query), my_grad_b_query, me * my_cols, 0)
+    grad_b_fc = lax.dynamic_update_slice_in_dim(
+        zero(b_fc), my_grad_b_fc.reshape(-1), me * my_hidden, 0
+    )
+    vectors = (
+        grad_ln1_gain,
+        grad_ln1_bias,
+        grad_b_query,
+        grad_b_value,
+        grad_b_out,
+        grad_ln2_gain,
+        grad_ln2_bias,
+        grad_b_fc,
+        grad_b_proj,
+    )
+    mlp, shard_fc, shard_query, shard_kv, packed = scatter_proj(
+        act_low,
+        wp,
+        fc_pieces,
+        grad_w_query.reshape(PLANE, layers, -1, my_cols),
+        grad_w_kv,
+        pack_vectors(vectors),
+        layers,
+        9,
+    )
+    output = residual + mlp + b_proj
+    sums = unpack_vectors(packed, vectors)
+    return (
+        output.reshape(streams, rows, width),
+        input_grad.reshape(streams, rows, width),
+        shard_query.astype(f32),
+        shard_kv,
+        shard_out,
+        shard_fc.astype(f32),
+        shard_proj.astype(f32),
+        *sums,
+    )
+
+
 def gather_seq(block):
     return lax.all_gather(block, "seq", axis=0, tiled=True)
 
@@ -71,7 +1416,7 @@
     return full.reshape(-1, full.shape[2])
 
 
-def column_weight_grad(grad, groups):
+def plain_column_grad(grad, groups):
     rows, cols = grad.shape
     kept = lax.psum_scatter(
         grad.astype(bf16).reshape(groups, rows // groups, cols), "fsdp", scatter_dimension=1, tiled=True
@@ -84,7 +1429,7 @@
     return lax.psum_scatter(grad.astype(bf16), "fsdp", scatter_dimension=0, tiled=True).astype(f32)
 
 
-def attend(queries, keyval, starts, groups, streams, rows, heads):
+def plain_attend(queries, keyval, starts, groups, streams, rows, heads):
     length = groups * rows
     scale = HD ** (-0.5)
     position = jnp.arange(length, dtype=jnp.int32)
@@ -106,7 +1451,7 @@
     return jnp.stack(mixed_list, axis=1), lse_list
 
 
-def attend_back(queries, keyval, grads, lse_list, starts, groups, streams, rows, heads):
+def plain_attend_back(queries, keyval, grads, lse_list, starts, groups, streams, rows, heads):
     length = groups * rows
     scale = HD ** (-0.5)
     position = jnp.arange(length, dtype=jnp.int32)
@@ -131,7 +1476,7 @@
     return jnp.stack(gq_list, axis=1), jnp.stack(gkv_list, axis=1)
 
 
-def shards(
+def plain_shards(
     tokens,
     doc_starts,
     w_query,
@@ -175,7 +1520,7 @@
     queries = (dot(hidden1, wq) + my_bq).astype(bf16).reshape(groups, streams, rows, my_cols)
     value_shift = jnp.concatenate([jnp.zeros((HD,), f32), b_value])
     keyval = (dot(hidden1, w_kv_all) + value_shift).astype(bf16).reshape(groups, streams, rows, 2 * HD)
-    mixed, lse = attend(queries, keyval, doc_starts, groups, streams, rows, heads)
+    mixed, lse = plain_attend(queries, keyval, doc_starts, groups, streams, rows, heads)
     mixed_rows = mixed.reshape(groups * own, my_cols)
     residual = inputs + scatter_seq(dot(mixed_rows, wo)) + b_out
     shifted2, normed2, inverse2 = normalize(residual, ln2_gain, ln2_bias)
@@ -190,7 +1535,7 @@
     shard_proj = row_weight_grad(dot_tn(act_low, cot_all))
     grad_pre = (dot_nt(cot_all, wp) * slope).astype(bf16)
     my_grad_b_fc = jnp.sum(grad_pre.astype(f32), axis=0)
-    shard_fc = column_weight_grad(dot_tn(hidden2, grad_pre), groups)
+    shard_fc = plain_column_grad(dot_tn(hidden2, grad_pre), groups)
     grad_hidden2 = scatter_seq(dot_nt(grad_pre, wf))
     back_second, grad_ln2_gain, grad_ln2_bias = normalize_back(
         grad_hidden2, normed2, inverse2, ln2_gain
@@ -201,7 +1546,7 @@
     grad_attn_all = gather_seq(grad_attn)
     shard_out = row_weight_grad(dot_tn(mixed_rows, grad_attn_all))
     grad_mixed = dot_nt(grad_attn_all, wo).astype(bf16).reshape(groups, streams, rows, my_cols)
-    gq, gkv = attend_back(
+    gq, gkv = plain_attend_back(
         queries, keyval, grad_mixed, lse, doc_starts, groups, streams, rows, heads
     )
     gq_rows = gq.reshape(groups * own, my_cols)
@@ -209,7 +1554,7 @@
     my_grad_b_query = jnp.sum(gq_rows.astype(f32), axis=0)
     grad_b_value = jnp.sum(gkv_rows[:, HD:], axis=0)
     gkv_low = gkv_rows.astype(bf16)
-    shard_query = column_weight_grad(dot_tn(hidden1, gq_rows), groups)
+    shard_query = plain_column_grad(dot_tn(hidden1, gq_rows), groups)
     shard_kv = row_weight_grad(scatter_seq(dot_tn(hidden1, gkv_low)))
     grad_hidden1 = scatter_seq(dot_nt(gq_rows, wq) + dot_nt(gkv_low, w_kv_all))
     back_first, grad_ln1_gain, grad_ln1_bias = normalize_back(
@@ -248,7 +1593,7 @@
     acts = P("fsdp", "seq", None)
     weight = P(("seq", "fsdp"), None)
     return jax.shard_map(
-        shards,
+        shards if mesh.shape["seq"] == PLANE else plain_shards,
         mesh=mesh,
         in_specs=(acts, P("fsdp", None)) + (weight,) * 5 + (P(),) * 9 + (acts,),
         out_specs=(acts, acts) + (weight,) * 5 + (P(),) * 9,

time: 1340 us -> 516 us (0.39)
  waiting for transfers between devices: 936 us -> 3.15 us
  Pallas kernels: 0 us -> 451 us
  matrix products: 207 us -> 0 us
  blocking collectives: 47.1 us -> 0 us
  local copies, waits for them, and re-layouts: 56.8 us -> 11.7 us
  other arithmetic: 57.8 us -> 25.8 us
    pallas_call x0 -> x10, Pallas kernels: none -> 451 us  [the longest x1 65.7 us: scatter_proj(): pl.pallas_call(kernel, out_shape=[jax.ShapeDtypeStruct((rows, wide), f32)...]
    reduce_scatter x10 -> x2, waiting for transfers between devices: 425 us -> 0.04 us  [line_scatter(): lax.psum_scatter(grad.astype(bf16), 'fsdp', scatter_dimension=axis, tiled...]
    all_gather x9 -> x2, waiting for transfers between devices: 382 us -> 2.36 us  [line_gather(): return lax.all_gather(shard, 'fsdp', axis=axis, tiled=True)]
    dot_general x27 -> x0, matrix products: 207 us -> none  [the longest x5 58.8 us: dot_nt(): lax.dot_general(a, b, (((1,), (1,)), ((), ())), preferred_element_type=f32)]
    psum x1 -> x0, waiting for transfers between devices: 127 us -> none  [shards(): sums = lax.psum(vectors, ('seq', 'fsdp'))]
    all_to_all x2 -> x0, blocking collectives: 30.7 us -> none  [columns_to_rows(): lax.all_to_all(spread, 'seq', split_axis=0, concat_axis=0, tiled=True)]
    unnamed x117 -> x51, local copies, waits for them, and re-layouts: 22.8 us -> 3.8 us
    all_gather x1 -> x0, blocking collectives: 16.4 us -> none  [shards(): w_kv_all = gather_seq(lax.all_gather(w_kv, 'fsdp', axis=0, tiled=True))]
  transfers between devices with their start and end apart: 22 -> 4, of which waited for: 19 -> 1; matrix products, arithmetic and copies ran while one was open for 14% -> 4% of each run, Pallas kernels for 0% -> 72%
where the time goes in v3:
time: 516 us; the launch traced here: 506 us
  Pallas kernels  451 us (87%)
  other arithmetic  25.8 us (5%)
  between operations  14.6 us (3%)
  local copies, waits for them, and re-layouts  11.7 us (2%)
    pallas_call x1, Pallas kernels, scatter_proj(): pl.pallas_call(kernel, out_shape=[jax.ShapeDtypeStruct((rows, wide), f32)...  65.7 us
    pallas_call x1, Pallas kernels, scatter_query(): pl.pallas_call(kernel, out_shape=[jax.ShapeDtypeStruct((rows, depth), f32...  63.9 us
    pallas_call x1, Pallas kernels, scatter_fc(): pl.pallas_call(kernel, out_shape=[jax.ShapeDtypeStruct((rows, depth), f32...  53.8 us
    pallas_call x1, Pallas kernels, gather_fc(): pl.pallas_call(kernel, out_shape=[jax.ShapeDtypeStruct((total, depth), bf...  51.4 us
    pallas_call x1, Pallas kernels, gather_hidden1(): pl.pallas_call(kernel, out_shape=[jax.ShapeDtypeStruct((PLANE * hidden1.s...  48.9 us
    pallas_call x1, Pallas kernels, scatter_attn(): pl.pallas_call(kernel, out_shape=jax.ShapeDtypeStruct((rows, wide), f32),...  46.5 us
    pallas_call x1, Pallas kernels, project_attend(): pl.pallas_call(kernel, out_shape=[jax.ShapeDtypeStruct((PLANE * cot.shape...  45.4 us
    pallas_call x1, Pallas kernels, gather_out(): pl.pallas_call(kernel, out_shape=[jax.ShapeDtypeStruct((total, wide), bf1...  41.3 us
  transfers between devices with their start and end apart: 4, of which 1 were waited for; matrix products, arithmetic and copies ran while one was open for 4% of the time, Pallas kernels for 72%

profile of v3, /device:TPU:0, one launch (start us, length us, event | category | flops | bytes accessed | tf_op | source)
XLA Modules:
  0.0 506.1 jit_solution(9465991312730110454)
XLA Ops:
  7.2 20.1 %split_weights.1 = (bf16[8,64,256]{2,1,0:T(8,128)(2,1)}, bf16[8,64,1024]{2,1,0:T(8,128)(2,1)}, bf16[256,256]{1,0:T(8,128)(2,1)}) custom-call(bf16[64,2048]{1,0:T(8,128)(2,1)} %wq_ref.1, bf16[64,8192]{1,0:T(8,128)(2,1)} %wf_ref.1, bf16[64,256]{1,0:T(8,128)(2,1)} %kv_ref.1), custom_call_target="tpu_custom_call" | custom-call | tf_op jit(solution)/shard_map/split_weights/pallas_call | solution.py:354
  32.1 1.4 fusion.8.h_ref
  33.6 48.9 %gather_hidden1.1 = (bf16[2048,2048]{1,0:T(8,128)(2,1)}, bf16[2048,256]{1,0:T(8,128)(2,1)}, bf16[8,4,64,256]{3,2,1,0:T(8,128)(2,1)}) custom-call(bf16[256,2048]{1,0:T(8,128)(2,1)} %fusion.8.h_ref, bf16[256,256]{1,0:T(8,128)(2,1)} %get-tuple-element.49.kv_ref, bf16[8,64,256]{2,1,0:T(8,128)(2,1)} %get-tuple-element.50.wq_ref), custom_call_target="tpu_custom_call" | custom-call | tf_op jit(solution)/shard_map/gather_hidden1/pallas_call | solution.py:408
  82.5 45.4 %project_attend.1 = (bf16[2048,2048]{1,0:T(8,128)(2,1)}, bf16[256,2048]{1,0:T(8,128)(2,1)}, bf16[8,2,128,256]{3,2,1,0:T(8,128)(2,1)}, bf16[8,2,128,256]{3,2,1,0:...) custom-call(s32[2,4]{1,0:T(2,128)} %docs_ref.3, bf16[2048,2048]{1,0:T(8,128)(2,1)} %get-tuple-element.51.h_ref, ...), custom_call_target="tpu_custom_call" | custom-call | flops 4294967296 | bytes 41943040 | tf_op jit(solution)/shard_map/project_attend/pallas_call | solution.py:494
  127.9 46.5 %scatter_attn.1 = f32[256,2048]{1,0:T(8,128)} custom-call(bf16[2048,256]{1,0:T(8,128)(2,1)} %bitcast.72, bf16[256,2048]{1,0:T(8,128)(2,1)} %get-tuple-element.55.w_ref), custom_call_target="tpu_custom_call" | custom-call | flops 2147483648 | bytes 41943040 | tf_op jit(solution)/shard_map/scatter_attn/pallas_call | solution.py:720
  174.4 1.9 fusion.16
  177.1 1.4 add_convert_fusion.own_ref
  178.5 51.4 %gather_fc.1 = (bf16[2048,2048]{1,0:T(8,128)(2,1)}, bf16[2048,1024]{1,0:T(8,128)(2,1)}, bf16[2048,1024]{1,0:T(8,128)(2,1)}, bf16[1024,2048]{1,0:T(8,128)(2,1)}) custom-call(bf16[256,2048]{1,0:T(8,128)(2,1)} %add_convert_fusion.own_ref, bf16[2048,1024]{1,0:T(8,128)(2,1)} %bitcast.68, f32[1,1024]{1,0:T(1,128)} %bitcast.63, ...), custom_call_target="tpu_custom_call" | custom-call | flops 17179869184 | bytes 41943040 | tf_op jit(solution)/shard_map/gather_fc/pallas_call | solution.py:601
  230.0 2.4 all-gather.5.cloned.1.call-done.wp_ref
  232.4 53.8 %scatter_fc.1 = (f32[256,2048]{1,0:T(8,128)}, f32[1,1024]{1,0:T(1,128)}, bf16[2048,1024]{1,0:T(8,128)(2,1)}) custom-call(bf16[2048,2048]{1,0:T(8,128)(2,1)} %get-tuple-element.57.cot_ref, bf16[2048,1024]{1,0:T(8,128)(2,1)} %get-tuple-element.59.slope_ref, bf16[1024,2048]{1,0:T(8,128)(2,1)} %all-gather.5.cloned.1.call-done.wp_ref, ...), custom_call_target="tpu_custom_call" | custom-call | flops 25769803776 | bytes 41943040 | tf_op jit(solution)/shard_map/scatter_fc/pallas_call | solution.py:831
  286.3 1.4 convert_reduce_fusion.1
  288.0 2.6 multiply_reduce_fusion
  290.7 2.7 convert_reduce_fusion.2
  293.3 41.3 %gather_out.1 = (bf16[2048,256]{1,0:T(8,128)(2,1)}, bf16[256,2048]{1,0:T(8,128)(2,1)}) custom-call(bf16[256,2048]{1,0:T(8,128)(2,1)} %get-tuple-element.91.own_ref, bf16[256,2048]{1,0:T(8,128)(2,1)} %get-tuple-element.55.w_ref, bf16[2048,256]{1,0:T(8,128)(2,1)} %bitcast.73), custom_call_target="tpu_custom_call" | custom-call | flops 4294967296 | bytes 41943040 | tf_op jit(solution)/shard_map/gather_out/pallas_call | solution.py:679
  334.6 13.5 %attention_backward.1 = (bf16[8,2,128,256]{3,2,1,0:T(8,128)(2,1)}, bf16[8,2,128,256]{3,2,1,0:T(8,128)(2,1)}) custom-call(s32[2,4]{1,0:T(2,128)} %docs_ref.3, bf16[8,2,128,256]{3,2,1,0:T(8,128)(2,1)} %get-tuple-element.62.q_ref, bf16[8,2,128,256]{3,2,1,0:T(8,128)(2,1)} %get-tuple-element.63.kv_ref, bf16[8,2,128,256]{3,2,1,0:T(8,128)(2,1)} %bitcast.75, ...), custom_call_target="tpu_custom_call" | custom-call | flops 5368709120 | bytes 8388608 | tf_op jit(solution)/shard_map/attention_backward/pallas_call | solution.py:1219
  348.2 1.5 convert_reduce_fusion.3
  350.0 63.9 %scatter_query.1 = (f32[256,2048]{1,0:T(8,128)}, bf16[2048,256]{1,0:T(8,128)(2,1)}, bf16[256,256]{1,0:T(8,128)(2,1)}, f32[64,2048]{1,0:T(8,128)}) custom-call(bf16[2048,256]{1,0:T(8,128)(2,1)} %bitcast.57, bf16[2048,256]{1,0:T(8,128)(2,1)} %bitcast.58, bf16[2048,256]{1,0:T(8,128)(2,1)} %bitcast.71, bf16[2048,256]{1,0:T(8,128)(2,1)} %get-tuple-element.53.wkv_ref, ...), custom_call_target="tpu_custom_call" | custom-call | flops 8589934592 | bytes 41943040 | tf_op jit(solution)/shard_map/scatter_query/pallas_call | solution.py:974
  413.9 2.7 fusion.10
  417.7 65.7 %scatter_proj.1 = (f32[256,2048]{1,0:T(8,128)}, bf16[64,8192]{1,0:T(8,128)(2,1)}, bf16[64,2048]{1,0:T(8,128)(2,1)}, f32[64,256]{1,0:T(8,128)}, f32[8,24,128]{2,1,0:T(8,128)}) custom-call(bf16[2048,1024]{1,0:T(8,128)(2,1)} %get-tuple-element.58.act_ref, bf16[1024,2048]{1,0:T(8,128)(2,1)} %all-gather.5.cloned.1.call-done.wp_ref, ...), custom_call_target="tpu_custom_call" | custom-call | flops 8589934592 | bytes 41943040 | tf_op jit(solution)/shard_map/scatter_proj/pallas_call | solution.py:1101
  483.3 1.6 fusion.18
  487.5 2.7 convert_element_type.56
  491.0 1.7 add_add_fusion
  494.0 2.1 fusion.13
  496.1 1.6 convert_element_type.57
  (84 shorter events, 13.2 us)
Async XLA Ops:
  7.2 22.4 %copy-start.19 = (f32[128]{0:T(128)S(1)}, f32[128]{0:T(128)}, u32[]{:S(2)}) copy-start(f32[128]{0:T(128)} %param.27) | copy-start | bytes 1540
  7.2 24.2 %copy-start = (bf16[2,128,2048]{2,1,0:T(8,128)(2,1)S(1)}, bf16[2,128,2048]{2,1,0:T(8,128)(2,1)}, u32[]{:S(2)}) copy-start(bf16[2,128,2048]{2,1,0:T(8,128)(2,1)} %param.17) | copy-start | bytes 3145732
  7.2 171.3 %all-gather.3.cloned.1.call-start = ((), (), s32[]{:S(2)}) async-start(), calls=%async_computation.2 | async-start | bytes 5242880 | tf_op jit(solution)/shard_map/all_gather | solution.py:1266
  27.4 4.7 copy-start.11
  27.4 4.7 copy-start.13
  27.5 204.9 %all-gather.5.cloned.1.call-start = ((), (), s32[]{:S(2)}) async-start(), calls=%async_computation.3 | async-start | bytes 5242880 | tf_op jit(solution)/shard_map/all_gather | solution.py:1266
  28.2 306.4 %reduce-scatter.5.cloned.1.call-start = ((), (), s32[]{:S(2)}) async-start(), calls=%async_computation.5 | async-start | bytes 5242880 | tf_op jit(solution)/shard_map/reduce_scatter | solution.py:1270
  127.9 46.6 %copy-start.14 = (f32[2048]{0:T(1024)S(1)}, f32[2048]{0:T(1024)}, u32[]{:S(2)}) copy-start(f32[2048]{0:T(1024)} %param.28) | copy-start | bytes 24580
  176.4 0.7 copy-start.10
  176.4 0.7 copy-start.15
  230.0 187.1 %reduce-scatter.3.cloned.1.call-start = ((), (), s32[]{:S(2)}) async-start(), calls=%async_computation.4 | async-start | bytes 5242880 | tf_op jit(solution)/shard_map/reduce_scatter | solution.py:1270
  286.2 1.5 copy-start.17
  288.0 2.7 copy-start.1
  288.0 2.7 copy-start.4
  413.9 2.7 copy-start.9
  417.0 0.6 copy-start.18
  483.3 6.9 %copy-start.8 = (bf16[64,2048]{1,0:T(8,128)(2,1)S(1)}, bf16[64,2048]{1,0:T(8,128)(2,1)}, u32[]{:S(2)}) copy-start(bf16[64,2048]{1,0:T(8,128)(2,1)} %get-tuple-element.77) | copy-start | bytes 786436
  483.3 7.7 %copy-start.5 = (f32[256,2048]{1,0:T(8,128)S(1)}, f32[256,2048]{1,0:T(8,128)}, u32[]{:S(2)}) copy-start(f32[256,2048]{1,0:T(8,128)} %get-tuple-element.76) | copy-start | bytes 6291460
  483.3 7.7 %copy-start.16 = (f32[2048]{0:T(1024)S(1)}, f32[2048]{0:T(1024)}, u32[]{:S(2)}) copy-start(f32[2048]{0:T(1024)} %param.32) | copy-start | bytes 24580
  491.0 2.3 copy-start.2
  491.0 3.0 copy-start.3
  494.0 2.1 copy-start.6
  496.1 1.6 copy-start.12
  496.1 2.2 copy-start.7
Sparse Core Ops, SparseCore 0:
  27.6 123.7 all-gather.2
  153.0 79.3 all-gather.4
  234.7 82.9 reduce-scatter.4
  319.9 94.1 reduce-scatter.2

commit v4 on v3

--- a/solution.py
+++ b/solution.py
@@ -313,28 +313,38 @@
     return copy
 
 
-def split_weights(w_query, w_fc, w_kv, layers, number):
-    arrays = (w_query, w_fc)
-
-    def kernel(wq_ref, wf_ref, kv_ref, wq_out, wf_out, kv_out, send, recv, zsend, zrecv, local):
+def split_weights(w_query, w_fc, w_kv, w_out, layers, number):
+    arrays, lined = (w_query, w_fc), (w_kv, w_out)
+
+    def kernel(wq_ref, wf_ref, kv_ref, wo_ref, wq_out, wf_out, kv_out, wo_out, *refs):
+        send, recv, zsend, zrecv, local = refs
         p = Place()
-        kv_rows = kv_ref.shape[0]
-        mine = kv_out.at[rows_at(p.layer * kv_rows, kv_rows), :]
         ins, outs = (wq_ref, wf_ref), (wq_out, wf_out)
+        line_ins = (kv_ref, wo_ref)
+        mine = [
+            out.at[rows_at(p.layer * src.shape[0], src.shape[0]), :]
+            for src, out in zip(line_ins, (kv_out, wo_out))
+        ]
 
         def block(i, dev):
             cols = ins[i].shape[1] // PLANE
             return ins[i].at[:, rows_at(dev * cols, cols)]
 
-        own = [load(kv_ref, mine, local.at[2])]
+        own = []
         for i in range(2):
+            own.append(load(line_ins[i], mine[i], local.at[2 + i]))
             own.append(load(block(i, p.me), outs[i].at[p.me], local.at[i]))
         p.greet(True, layers)
         copies = []
-        for step in range(1, layers):
-            to = p.line_peer(step, layers)
-            copies.append(push(kv_ref, mine, zsend.at[step], zrecv.at[step], {"fsdp": to}))
-            copies[-1].start()
+        for i in range(2):
+            for step in range(1, layers):
+                to = p.line_peer(step, layers)
+                copies.append(
+                    push(
+                        line_ins[i], mine[i], zsend.at[i, step], zrecv.at[i, step], {"fsdp": to}
+                    )
+                )
+                copies[-1].start()
         for i in range(2):
             for step in range(1, PLANE):
                 to = p.plane_peer(step)
@@ -357,19 +367,19 @@
             jax.ShapeDtypeStruct((PLANE, a.shape[0], a.shape[1] // PLANE), a.dtype)
             for a in arrays
         ]
-        + [jax.ShapeDtypeStruct((layers * w_kv.shape[0], w_kv.shape[1]), w_kv.dtype)],
-        in_specs=[ANY] * 3,
-        out_specs=[ANY] * 3,
+        + [jax.ShapeDtypeStruct((layers * a.shape[0], a.shape[1]), a.dtype) for a in lined],
+        in_specs=[ANY] * 4,
+        out_specs=[ANY] * 4,
         scratch_shapes=[
             sems(2, PLANE),
             sems(2, PLANE),
-            sems(layers),
-            sems(layers),
-            sems(3),
+            sems(2, layers),
+            sems(2, layers),
+            sems(4),
         ],
         compiler_params=params(number, False),
         name="split_weights",
-    )(w_query, w_fc, w_kv)
+    )(w_query, w_fc, w_kv, w_out)
 
 
 def gather_hidden1(hidden1, low_kv, wq_pieces, layers, number):
@@ -420,7 +430,7 @@
     )(hidden1, low_kv, wq_pieces)
 
 
-def project_attend(docs, hidden1, wq, w_kv, bq, bkv, cot, w_out, streams, heads, layers, number):
+def project_attend(docs, hidden1, wq, w_kv, bq, bkv, cot, streams, heads, number):
     total, depth = hidden1.shape
     cols, kv_cols = wq.shape[1], w_kv.shape[1]
     rows = total // PLANE // streams
@@ -428,14 +438,11 @@
     block = min(QROWS, length)
     chunk = total // 4
 
-    def kernel(docs_ref, h_ref, wq_ref, wkv_ref, bq_ref, bkv_ref, cot_ref, wo_ref, *refs):
-        cot_all, wo_all, q_out, kv_out, mixed_out, lse_ref = refs[:6]
-        h_buf, wq_buf, wkv_buf, q_buf, kv_buf, mixed_buf = refs[6:12]
-        send, recv, zsend, zrecv, local = refs[12:]
+    def kernel(docs_ref, h_ref, wq_ref, wkv_ref, bq_ref, bkv_ref, cot_ref, *refs):
+        cot_all, q_out, kv_out, mixed_out, lse_ref = refs[:5]
+        h_buf, wq_buf, wkv_buf, q_buf, kv_buf, mixed_buf, send, recv, local = refs[5:]
         p = Place()
         own_rows = cot_ref.shape[0]
-        wo_rows = wo_ref.shape[0]
-        wo_mine = wo_all.at[rows_at(p.layer * wo_rows, wo_rows), :]
 
         def fetch(k):
             return load(
@@ -444,17 +451,10 @@
 
         fetches = [fetch(0)]
         weights = [load(wq_ref, wq_buf, local.at[2]), load(wkv_ref, wkv_buf, local.at[3])]
-        own = [
-            load(cot_ref, cot_all.at[rows_at(p.me * own_rows, own_rows), :], local.at[4]),
-            load(wo_ref, wo_mine, local.at[8]),
-        ]
-        p.greet(False, layers)
+        own = load(cot_ref, cot_all.at[rows_at(p.me * own_rows, own_rows), :], local.at[4])
+        p.greet()
         g = Gather(p, cot_all, own_rows, send, recv)
         g.start(cot_ref)
-        for step in range(1, layers):
-            to = p.line_peer(step, layers)
-            own.append(push(wo_ref, wo_mine, zsend.at[step], zrecv.at[step], {"fsdp": to}))
-            own[-1].start()
         for copy in weights:
             copy.wait()
         per = chunk // (streams * rows)
@@ -486,7 +486,8 @@
         for dev in (p.sib, p.xs, p.ys, p.ds):
             g.have(dev)
         g.finish()
-        for copy in own + stores:
+        own.wait()
+        for copy in stores:
             copy.wait()
 
     q_shape = (PLANE, streams, rows, cols)
@@ -495,14 +496,13 @@
         kernel,
         out_shape=[
             jax.ShapeDtypeStruct((PLANE * cot.shape[0], cot.shape[1]), bf16),
-            jax.ShapeDtypeStruct((layers * w_out.shape[0], w_out.shape[1]), bf16),
             jax.ShapeDtypeStruct(q_shape, bf16),
             jax.ShapeDtypeStruct(kv_shape, bf16),
             jax.ShapeDtypeStruct(q_shape, bf16),
             jax.ShapeDtypeStruct((streams, heads, length), f32),
         ],
-        in_specs=[pl.BlockSpec(memory_space=pltpu.SMEM)] + [ANY] * 3 + [WHOLE] * 2 + [ANY] * 2,
-        out_specs=[ANY] * 5 + [WHOLE],
+        in_specs=[pl.BlockSpec(memory_space=pltpu.SMEM)] + [ANY] * 3 + [WHOLE] * 2 + [ANY],
+        out_specs=[ANY] * 4 + [WHOLE],
         scratch_shapes=[
             pltpu.VMEM((2, chunk, depth), bf16),
             pltpu.VMEM(wq.shape, bf16),
@@ -512,11 +512,11 @@
             pltpu.VMEM(q_shape, bf16),
         ]
         + Gather.scratch
-        + [sems(layers), sems(layers), sems(9)],
+        + [sems(8)],
         compiler_params=params(number),
         cost_estimate=cost(2 * total * depth * (cols + kv_cols)),
         name="project_attend",
-    )(docs, hidden1, wq, w_kv, bq, bkv, cot, w_out)
+    )(docs, hidden1, wq, w_kv, bq, bkv, cot)
 
 
 def gather_fc(hidden2, wf, bf, cot_all, number):
@@ -885,14 +885,15 @@
     rows = total // PLANE
     depth = wq.shape[0]
     part_rows = depth // PLANE
+    line_rows = part_rows // layers
     out_rows = grad_w_out.shape[0] // layers
     out_wide = grad_w_out.shape[1]
 
     def kernel(gq_ref, gkv_ref, wq_ref, wkv_ref, h_ref, dwo_ref, *refs):
         out_ref, dwq_ref, dwkv_ref, dwo_out = refs[:4]
-        g_buf, wq_buf, wkv_buf, h_buf, dwq_buf, dkv, box, dwo_own, dwo_box = refs[4:13]
-        s = refs[13:26]
-        ksend, krecv, zsend, zrecv, local = refs[26:]
+        g_buf, wq_buf, wkv_buf, h_buf, dwq_buf, dwq_box, dkv, box, dwo_own, dwo_box = refs[4:14]
+        s = refs[14:27]
+        ksend, krecv, zsend, zrecv, qsend, qrecv, local = refs[27:]
         p = Place()
 
         def dwo_block(layer):
@@ -933,6 +934,7 @@
                     )
 
         sent = []
+        lines_q = []
 
         def idle():
             for i in range(PLANE):
@@ -942,7 +944,7 @@
                 if i + 1 < PLANE:
                     tiles.append(h_fetch(i + 1))
                 term = dot_tn(h_buf[i % 2], g_buf[...]).astype(bf16)
-                dwq_buf[rows_at(dev * part_rows, part_rows), :] = term[:, :cols]
+                dwq_buf[dev] = term[:, :cols].reshape(layers, line_rows, cols)
                 dkv[step] = term[:, cols:]
                 if step:
                     copy = push(
@@ -950,9 +952,11 @@
                     )
                     copy.start()
                     sent.append(copy)
+            lines_q.append(
+                LineSum(p, lambda layer: dwq_buf.at[:, layer], dwq_box, layers, qsend, qrecv)
+            )
 
         Scatter.take(p, rows, s).run(product, out_ref, idle)
-        store = load(dwq_buf, dwq_ref, local.at[6])
         sum_kv = dkv[0].astype(f32)
         for i, copy in enumerate(sent):
             copy.wait_recv()
@@ -966,172 +970,136 @@
             lines = rows_at(i * 16, 16)
             dwo_out[lines, :] = line.total(dwo_own[lines, :], (lines, slice(None)))
 
+        (line_q,) = lines_q
+        line_q.arrived()
+
+        @pl.loop(0, PLANE)
+        def _(i):
+            dwq_ref[i] = line_q.total(dwq_buf[i, p.layer], (i,)).astype(bf16)
+
         for copy in sent:
             copy.wait_send()
         line.finish()
-        store.wait()
+        line_q.finish()
 
     return pl.pallas_call(
         kernel,
         out_shape=[
             jax.ShapeDtypeStruct((rows, depth), f32),
-            jax.ShapeDtypeStruct((depth, cols), bf16),
+            jax.ShapeDtypeStruct((PLANE, line_rows, cols), bf16),
             jax.ShapeDtypeStruct((part_rows, kv_cols), bf16),
             jax.ShapeDtypeStruct((out_rows, out_wide), f32),
         ],
         in_specs=[ANY] * 6,
-        out_specs=[WHOLE, ANY, WHOLE, WHOLE],
+        out_specs=[WHOLE] * 4,
         scratch_shapes=[
             pltpu.VMEM((total, cols + kv_cols), bf16),
             pltpu.VMEM(wq.shape, bf16),
             pltpu.VMEM(w_kv.shape, bf16),
             pltpu.VMEM((2, total, part_rows), bf16),
-            pltpu.VMEM((depth, cols), bf16),
+            pltpu.VMEM((PLANE, layers, line_rows, cols), bf16),
+            pltpu.VMEM((layers - 1, PLANE, line_rows, cols), bf16),
             pltpu.VMEM((PLANE, part_rows, kv_cols), bf16),
             pltpu.VMEM((PLANE, part_rows, kv_cols), bf16),
             pltpu.VMEM((out_rows, out_wide), bf16),
             pltpu.VMEM((layers - 1, out_rows, out_wide), bf16),
         ]
         + Scatter.scratch(rows, depth)
-        + [sems(PLANE), sems(PLANE), sems(layers), sems(layers), sems(8)],
+        + [sems(PLANE)] * 2
+        + [sems(layers)] * 4
+        + [sems(8)],
         compiler_params=params(number),
         cost_estimate=cost(4 * total * depth * (cols + kv_cols)),
         name="scatter_query",
     )(gq, gkv, wq, w_kv, hidden1, grad_w_out)
 
 
-def scatter_proj(act, wp, fc_pieces, grad_w_query, grad_w_kv, vector, layers, number):
-    total, depth = act.shape
-    rows = total // PLANE
-    wide = wp.shape[1]
+def last_exchange(vector, fc_pieces, q_pieces, grad_w_kv, layers, number):
     lines = vector.shape[1]
-    q_rows, q_cols = grad_w_query.shape[2:]
+    pieces = (fc_pieces, q_pieces)
     kv_rows, kv_cols = grad_w_kv.shape[0] // layers, grad_w_kv.shape[1]
-    fc_rows, fc_cols = fc_pieces.shape[1:]
-
-    def kernel(act_ref, wp_ref, fc_ref, dwq_ref, dwkv_ref, vec, *refs):
-        out_ref, fc_out, q_out, kv_out, vec_out = refs[:5]
-        a_buf, w_buf, q_own, q_box, q_sum, kv_own, kv_box, box, plane_sum, zbox = refs[5:15]
-        s = refs[15:28]
-        (fsend, frecv, qsend, qrecv, qzsend, qzrecv, kzsend, kzrecv, vsend, vrecv, zsend, zrecv) = (
-            refs[28:40]
-        )
-        gsend, grecv, local = refs[40:]
+
+    def kernel(vec, kv_ref, fc_ref, q_ref, vec_out, kv_out, fc_out, q_out, *refs):
+        box, plane_sum, zbox, kv_box = refs[:4]
+        vsend, vrecv, zsend, zrecv, kzsend, kzrecv, gsend, grecv, send, recv, local = refs[4:]
         p = Place()
 
-        def q_block(layer):
-            return dwq_ref.at[:, layer]
-
         def kv_block(layer):
-            return dwkv_ref.at[rows_at(layer * kv_rows, kv_rows), :]
-
-        fc_place = fc_out.at[:, rows_at(p.me * fc_cols, fc_cols)]
-        q_place = q_out.at[:, rows_at(p.me * q_cols, q_cols)]
-        loads = [load(act_ref, a_buf, local.at[0]), load(wp_ref, w_buf, local.at[1])]
-        own_q = load(q_block(p.layer), q_own, local.at[2])
-        own_kv = load(kv_block(p.layer), kv_own, local.at[3])
-        ends = [load(fc_ref.at[p.me], fc_place, local.at[4])]
+            return kv_ref.at[rows_at(layer * kv_rows, kv_rows), :]
+
         p.greet(True, layers)
-        first = []
+        first, copies = [], []
         for step in range(1, PLANE):
             to = p.plane_peer(step)
             copy = push(vec.at[to], box.at[step], vsend.at[step], vrecv.at[step], {"seq": to})
             copy.start()
             first.append(copy)
-        line_q = LineSum(p, q_block, q_box, layers, qzsend, qzrecv)
         line_kv = LineSum(p, kv_block, kv_box, layers, kzsend, kzrecv)
-        for copy in loads:
-            copy.wait()
-        sent = []
-
-        def spread(src, dst, send, recv):
+        for i, (src, out) in enumerate(((fc_ref, fc_out), (q_ref, q_out))):
+            cols = src.shape[2]
+            place = out.at[:, rows_at(p.me * cols, cols)]
+            copies.append(load(src.at[p.me], place, local.at[i]))
             for step in range(1, PLANE):
                 to = p.plane_peer(step)
-                copy = push(src.at[to], dst, send.at[step], recv.at[step], {"seq": to})
-                copy.start()
-                ends.append(copy)
-
-        def idle():
-            spread(fc_ref, fc_place, fsend, frecv)
-            total_vec = vec[p.me]
-            for step in range(1, PLANE):
-                first[step - 1].wait_recv()
-                total_vec = total_vec + box[step]
-            plane_sum[...] = total_vec
-            zbox[0] = total_vec
-            for step in range(1, layers):
-                to = p.line_peer(step, layers)
-                copy = push(plane_sum, zbox.at[step], zsend.at[step], zrecv.at[step], {"fsdp": to})
-                copy.start()
-                sent.append(copy)
-            own_q.wait()
-            line_q.arrived()
-
-            @pl.loop(0, PLANE)
-            def _(i):
-                q_sum[i] = line_q.total(q_own[i], (i,)).astype(bf16)
-
-            ends.append(load(q_sum.at[p.me], q_place, local.at[5]))
-            spread(q_sum, q_place, qsend, qrecv)
-            own_kv.wait()
-            line_kv.arrived()
-            kv_out[...] = line_kv.total(kv_own[...], ())
-            for copy in sent:
-                copy.wait_recv()
-            total_vec = None
-            for k in range(layers):
-                term = zbox[lax.rem(p.layer - k + layers, layers)]
-                total_vec = term if total_vec is None else total_vec + term
-            vec_out[p.me] = total_vec
-            for step in range(1, PLANE):
-                to = p.plane_peer(step)
-                mine = vec_out.at[p.me]
-                copy = push(mine, mine, gsend.at[step], grecv.at[step], {"seq": to})
-                copy.start()
-                ends.append(copy)
-
-        Scatter.take(p, rows, s).run(plain_product(a_buf, w_buf), out_ref, idle)
-        for copy in first + sent:
+                copies.append(
+                    push(src.at[to], place, send.at[i, step], recv.at[i, step], {"seq": to})
+                )
+                copies[-1].start()
+        total = vec[p.me]
+        for step in range(1, PLANE):
+            first[step - 1].wait_recv()
+            total = total + box[step]
+        plane_sum[...] = total
+        zbox[0] = total
+        across = []
+        for step in range(1, layers):
+            to = p.line_peer(step, layers)
+            copy = push(plane_sum, zbox.at[step], zsend.at[step], zrecv.at[step], {"fsdp": to})
+            copy.start()
+            across.append(copy)
+        line_kv.arrived()
+        kv_out[...] = line_kv.total(kv_ref[rows_at(p.layer * kv_rows, kv_rows), :], ())
+        for copy in across:
+            copy.wait_recv()
+        total = None
+        for k in range(layers):
+            term = zbox[lax.rem(p.layer - k + layers, layers)]
+            total = term if total is None else total + term
+        vec_out[p.me] = total
+        for step in range(1, PLANE):
+            to = p.plane_peer(step)
+            mine = vec_out.at[p.me]
+            copies.append(push(mine, mine, gsend.at[step], grecv.at[step], {"seq": to}))
+            copies[-1].start()
+        for copy in copies:
+            copy.wait()
+        for copy in first + across:
             copy.wait_send()
-        line_q.finish()
         line_kv.finish()
-        for copy in ends:
-            copy.wait()
 
     return pl.pallas_call(
         kernel,
         out_shape=[
-            jax.ShapeDtypeStruct((rows, wide), f32),
-            jax.ShapeDtypeStruct((fc_rows, PLANE * fc_cols), bf16),
-            jax.ShapeDtypeStruct((q_rows, PLANE * q_cols), bf16),
+            jax.ShapeDtypeStruct(vector.shape, f32),
             jax.ShapeDtypeStruct((kv_rows, kv_cols), f32),
-            jax.ShapeDtypeStruct(vector.shape, f32),
-        ],
-        in_specs=[ANY] * 5 + [WHOLE],
-        out_specs=[WHOLE, ANY, ANY, WHOLE, WHOLE],
+        ]
+        + [jax.ShapeDtypeStruct((a.shape[1], PLANE * a.shape[2]), a.dtype) for a in pieces],
+        in_specs=[WHOLE, WHOLE, ANY, ANY],
+        out_specs=[WHOLE, WHOLE, ANY, ANY],
         scratch_shapes=[
-            pltpu.VMEM(act.shape, bf16),
-            pltpu.VMEM(wp.shape, bf16),
-            pltpu.VMEM((PLANE, q_rows, q_cols), bf16),
-            pltpu.VMEM((layers - 1, PLANE, q_rows, q_cols), bf16),
-            pltpu.VMEM((PLANE, q_rows, q_cols), bf16),
-            pltpu.VMEM((kv_rows, kv_cols), bf16),
-            pltpu.VMEM((layers - 1, kv_rows, kv_cols), bf16),
             pltpu.VMEM((PLANE, lines, 128), f32),
             pltpu.VMEM((lines, 128), f32),
             pltpu.VMEM((layers, lines, 128), f32),
+            pltpu.VMEM((layers - 1, kv_rows, kv_cols), bf16),
         ]
-        + Scatter.scratch(rows, wide)
-        + [sems(PLANE)] * 4
+        + [sems(PLANE)] * 2
         + [sems(layers)] * 4
         + [sems(PLANE)] * 2
-        + [sems(layers)] * 2
-        + [sems(PLANE)] * 2
-        + [sems(6)],
-        compiler_params=params(number),
-        cost_estimate=cost(2 * total * depth * wide),
-        name="scatter_proj",
-    )(act, wp, fc_pieces, grad_w_query, grad_w_kv, vector)
+        + [sems(2, PLANE)] * 2
+        + [sems(2)],
+        compiler_params=params(number, False),
+        name="last_exchange",
+    )(vector, grad_w_kv, *pieces)
 
 
 def starts_of(docs, stream, positions):
@@ -1176,70 +1144,115 @@
             lse_ref[h : h + 1, b * block : (b + 1) * block] = top + jnp.log(total)
 
 
-def attention_backward(docs, queries, keyval, grads, lse, heads):
+def attend_stream_back(docs, stream, q_ref, kv_ref, g_ref, lse_ref, gq_ref, gkv_ref, gk, gv, heads):
+    groups, rows, cols = q_ref.shape
+    length = groups * rows
+    block = min(QROWS, length)
+    kv = kv_ref[...].reshape(length, 2 * HD)
+    keys, values = kv[:, :HD], kv[:, HD:]
+    keys_t = keys.T
+    per = block // rows
+    gk[...] = jnp.zeros_like(gk)
+    gv[...] = jnp.zeros_like(gv)
+    for b in range(length // block):
+        limit = (b + 1) * block
+        q_rows = q_ref[b * per : (b + 1) * per].reshape(block, cols)
+        g_rows = g_ref[b * per : (b + 1) * per].reshape(block, cols)
+        for h in range(heads):
+            q = q_rows[:, h * HD : (h + 1) * HD]
+            g = g_rows[:, h * HD : (h + 1) * HD]
+            scores, allowed = masked_scores(docs, stream, keys[:limit], q, b * block, limit)
+            shift = lse_ref[h : h + 1, b * block : (b + 1) * block]
+            probs = jnp.where(allowed, jnp.exp(scores - shift), 0.0)
+            grad_probs = dot_nt(values[:limit], g)
+            weighted = probs * grad_probs
+            delta = jnp.sum(weighted, axis=0, keepdims=True)
+            grad_scores = (weighted - probs * delta).astype(bf16)
+            gq = dot(keys_t[:, :limit], grad_scores) * (HD**-0.5)
+            gq_ref[b * per : (b + 1) * per, :, h * HD : (h + 1) * HD] = (
+                gq.T.astype(bf16).reshape(per, rows, HD)
+            )
+            gk[:limit, :] += dot(grad_scores, q)
+            gv[:limit, :] += dot(probs.astype(bf16), g)
+    gkv_ref[:, :, :HD] = (gk[...] * (HD**-0.5)).astype(bf16).reshape(groups, rows, HD)
+    gkv_ref[:, :, HD:] = gv[...].astype(bf16).reshape(groups, rows, HD)
+
+
+def attend_back_scatter_proj(docs, queries, keyval, grads, lse, act, wp, heads, number):
     groups, streams, rows, cols = queries.shape
     length = groups * rows
-    block = min(QROWS, length)
-
-    def kernel(docs_ref, q_ref, kv_ref, g_ref, lse_ref, gq_ref, gkv_ref, gk, gv):
-        stream = pl.program_id(0)
-        kv = kv_ref[...].reshape(length, 2 * HD)
-        keys, values = kv[:, :HD], kv[:, HD:]
-        keys_t = keys.T
-        per = block // rows
-        gk[...] = jnp.zeros_like(gk)
-        gv[...] = jnp.zeros_like(gv)
-        for b in range(length // block):
-            limit = (b + 1) * block
-            q_rows = q_ref[b * per : (b + 1) * per].reshape(block, cols)
-            g_rows = g_ref[b * per : (b + 1) * per].reshape(block, cols)
-            for h in range(heads):
-                q = q_rows[:, h * HD : (h + 1) * HD]
-                g = g_rows[:, h * HD : (h + 1) * HD]
-                scores, allowed = masked_scores(
-                    docs_ref, stream, keys[:limit], q, b * block, limit
-                )
-                shift = lse_ref[h : h + 1, b * block : (b + 1) * block]
-                probs = jnp.where(allowed, jnp.exp(scores - shift), 0.0)
-                grad_probs = dot_nt(values[:limit], g)
-                weighted = probs * grad_probs
-                delta = jnp.sum(weighted, axis=0, keepdims=True)
-                grad_scores = (weighted - probs * delta).astype(bf16)
-                gq = dot(keys_t[:, :limit], grad_scores) * (HD**-0.5)
-                gq_ref[b * per : (b + 1) * per, :, h * HD : (h + 1) * HD] = (
-                    gq.T.astype(bf16).reshape(per, rows, HD)
-                )
-                gk[:limit, :] += dot(grad_scores, q)
-                gv[:limit, :] += dot(probs.astype(bf16), g)
-        gkv_ref[:, :, :HD] = (gk[...] * (HD**-0.5)).astype(bf16).reshape(groups, rows, HD)
-        gkv_ref[:, :, HD:] = gv[...].astype(bf16).reshape(groups, rows, HD)
-
-    spec = pl.BlockSpec((groups, None, rows, cols), lambda s: (0, s, 0, 0))
-    spec_kv = pl.BlockSpec((groups, None, rows, 2 * HD), lambda s: (0, s, 0, 0))
+    total, depth = act.shape
+    own = total // PLANE
+    wide = wp.shape[1]
+
+    def kernel(docs_ref, q_ref, kv_ref, g_ref, lse_ref, act_ref, wp_ref, *refs):
+        gq_out, gkv_out, out_ref = refs[:3]
+        a_buf, w_buf, q_buf, kv_buf, g_buf, gq_buf, gkv_buf, gk, gv = refs[3:12]
+        s, local = refs[12:25], refs[25]
+        p = Place()
+        loads = [load(act_ref, a_buf, local.at[0]), load(wp_ref, w_buf, local.at[1])]
+        ins = [
+            load(q_ref, q_buf, local.at[2]),
+            load(kv_ref, kv_buf, local.at[3]),
+            load(g_ref, g_buf, local.at[4]),
+        ]
+        p.greet()
+        for copy in loads:
+            copy.wait()
+
+        def idle(stream):
+            if stream == 0:
+                for copy in ins:
+                    copy.wait()
+            attend_stream_back(
+                docs_ref,
+                stream,
+                q_buf.at[:, stream],
+                kv_buf.at[:, stream],
+                g_buf.at[:, stream],
+                lse_ref.at[stream],
+                gq_buf.at[:, stream],
+                gkv_buf.at[:, stream],
+                gk,
+                gv,
+                heads,
+            )
+
+        def idle_all():
+            for stream in range(streams):
+                idle(stream)
+
+        Scatter.take(p, own, s).run(plain_product(a_buf, w_buf), out_ref, idle_all)
+        stores = [load(gq_buf, gq_out, local.at[5]), load(gkv_buf, gkv_out, local.at[6])]
+        for copy in stores:
+            copy.wait()
+
     return pl.pallas_call(
         kernel,
-        grid=(streams,),
         out_shape=[
             jax.ShapeDtypeStruct(queries.shape, bf16),
             jax.ShapeDtypeStruct(keyval.shape, bf16),
+            jax.ShapeDtypeStruct((own, wide), f32),
         ],
-        in_specs=[
-            pl.BlockSpec(memory_space=pltpu.SMEM),
-            spec,
-            spec_kv,
-            spec,
-            pl.BlockSpec((None, heads, length), lambda s: (s, 0, 0)),
-        ],
-        out_specs=[spec, spec_kv],
-        scratch_shapes=[pltpu.VMEM((length, HD), f32)] * 2,
-        compiler_params=pltpu.CompilerParams(vmem_limit_bytes=VMEM_LIMIT),
-        cost_estimate=pl.CostEstimate(
-            flops=10 * streams * heads * length * length * HD,
-            bytes_accessed=8 * 1024 * 1024,
-            transcendentals=streams * heads * length * length,
-        ),
-        name="attention_backward",
-    )(docs, queries, keyval, grads, lse)
+        in_specs=[pl.BlockSpec(memory_space=pltpu.SMEM)] + [ANY] * 3 + [WHOLE] + [ANY] * 2,
+        out_specs=[ANY, ANY, WHOLE],
+        scratch_shapes=[
+            pltpu.VMEM(act.shape, bf16),
+            pltpu.VMEM(wp.shape, bf16),
+            pltpu.VMEM(queries.shape, bf16),
+            pltpu.VMEM(keyval.shape, bf16),
+            pltpu.VMEM(grads.shape, bf16),
+            pltpu.VMEM(queries.shape, bf16),
+            pltpu.VMEM(keyval.shape, bf16),
+            pltpu.VMEM((length, HD), f32),
+            pltpu.VMEM((length, HD), f32),
+        ]
+        + Scatter.scratch(own, wide)
+        + [sems(7)],
+        compiler_params=params(number),
+        cost_estimate=cost(2 * total * depth * wide),
+        name="attend_back_scatter_proj",
+    )(docs, queries, keyval, grads, lse, act, wp)
 
 
 def pack_vectors(vectors):
@@ -1308,7 +1321,7 @@
     cot_low = cotangent.reshape(own, width)
     cot_full = cot_low.astype(f32)
 
-    wq_pieces, wf_pieces, low_kv = split_weights(w_query, w_fc, w_kv, layers, 1)
+    wq_pieces, wf_pieces, low_kv, wo = split_weights(w_query, w_fc, w_kv, w_out, layers, 1)
     wf = line_gather(wf_pieces, 1).reshape(width, my_hidden)
     wp = line_gather(w_proj)
     my_bq = lax.dynamic_slice_in_dim(b_query, me * my_cols, my_cols, 0).reshape(1, my_cols)
@@ -1318,8 +1331,8 @@
     shifted1, normed1, inverse1 = normalize(inputs, ln1_gain, ln1_bias)
     hidden1, w_kv_all, wq = gather_hidden1(shifted1.astype(bf16), low_kv, wq_pieces, layers, 2)
     wq = wq.reshape(width, my_cols)
-    cot_all, wo, queries, keyval, mixed, lse = project_attend(
-        doc_starts, hidden1, wq, w_kv_all, my_bq, bkv, cot_low, w_out, streams, heads, layers, 3
+    cot_all, queries, keyval, mixed, lse = project_attend(
+        doc_starts, hidden1, wq, w_kv_all, my_bq, bkv, cot_low, streams, heads, 3
     )
     mixed_rows = mixed.reshape(total, my_cols)
     residual = inputs + scatter_attn(mixed_rows, wo, 4) + b_out
@@ -1337,18 +1350,22 @@
     grad_attn = grad_residual.astype(bf16)
     grad_b_out = jnp.sum(grad_attn.astype(f32), axis=0)
     grad_mixed, grad_w_out = gather_out(grad_attn, wo, mixed_rows, 7)
-    gq, gkv = attention_backward(
+    gq, gkv, mlp = attend_back_scatter_proj(
         doc_starts,
         queries,
         keyval,
         after(grad_mixed, shard_proj).reshape(PLANE, streams, rows, my_cols),
         lse,
+        act_low,
+        wp,
         heads,
-    )
+        8,
+    )
+    output = residual + mlp + b_proj
     gq_rows = gq.reshape(total, my_cols)
     gkv_rows = gkv.reshape(total, 2 * HD)
-    grad_hidden1, grad_w_query, grad_w_kv, shard_out = scatter_query(
-        gq_rows, gkv_rows, wq, w_kv_all, hidden1, grad_w_out, layers, 8
+    grad_hidden1, query_pieces, grad_w_kv, shard_out = scatter_query(
+        gq_rows, gkv_rows, wq, w_kv_all, hidden1, grad_w_out, layers, 9
     )
     my_grad_b_query = jnp.sum(gq_rows.astype(f32), axis=0)
     grad_b_value = jnp.sum(gkv_rows[:, HD:].astype(f32), axis=0)
@@ -1372,17 +1389,9 @@
         grad_b_fc,
         grad_b_proj,
     )
-    mlp, shard_fc, shard_query, shard_kv, packed = scatter_proj(
-        act_low,
-        wp,
-        fc_pieces,
-        grad_w_query.reshape(PLANE, layers, -1, my_cols),
-        grad_w_kv,
-        pack_vectors(vectors),
-        layers,
-        9,
-    )
-    output = residual + mlp + b_proj
+    packed, shard_kv, shard_fc, shard_query = last_exchange(
+        pack_vectors(vectors), fc_pieces, query_pieces, grad_w_kv, layers, 10
+    )
     sums = unpack_vectors(packed, vectors)
     return (
         output.reshape(streams, rows, width),

time: 516 us -> 510 us (0.988)
    pallas_call x1, Pallas kernels: 20.1 us -> 28.5 us  [split_weights(): pl.pallas_call(kernel, out_shape=[jax.ShapeDtypeStruct((PLANE, a.shape[0]...]
    pallas_call x2, Pallas kernels: 79.2 us -> 73.7 us  [the longest x1 49.6 us: attend_back_scatter_proj(): pl.pallas_call(kernel, out_shape=[jax.ShapeDtypeStruct(queries.shape, bf1...]
  transfers between devices with their start and end apart: 4 -> 4, of which waited for: 1 -> 0; matrix products, arithmetic and copies ran while one was open for 4% -> 4% of each run, Pallas kernels for 72% -> 79%
where the time goes in v4:
time: 510 us; the launch traced here: 500 us
  Pallas kernels  447 us (88%)
  other arithmetic  25.9 us (5%)
  between operations  14.6 us (3%)
  local copies, waits for them, and re-layouts  11.7 us (2%)
    pallas_call x1, Pallas kernels, scatter_query(): pl.pallas_call(kernel, out_shape=[jax.ShapeDtypeStruct((rows, depth), f32...  63.7 us
    pallas_call x1, Pallas kernels, scatter_fc(): pl.pallas_call(kernel, out_shape=[jax.ShapeDtypeStruct((rows, depth), f32...  54.6 us
    pallas_call x1, Pallas kernels, gather_fc(): pl.pallas_call(kernel, out_shape=[jax.ShapeDtypeStruct((total, depth), bf...  51.1 us
    pallas_call x1, Pallas kernels, gather_hidden1(): pl.pallas_call(kernel, out_shape=[jax.ShapeDtypeStruct((PLANE * hidden1.s...  49.6 us
    pallas_call x1, Pallas kernels, attend_back_scatter_proj(): pl.pallas_call(kernel, out_shape=[jax.ShapeDtypeStruct(queries.shape, bf1...  49.6 us
    pallas_call x1, Pallas kernels, scatter_attn(): pl.pallas_call(kernel, out_shape=jax.ShapeDtypeStruct((rows, wide), f32),...  43 us
    pallas_call x1, Pallas kernels, gather_out(): pl.pallas_call(kernel, out_shape=[jax.ShapeDtypeStruct((total, wide), bf1...  41.6 us
    pallas_call x1, Pallas kernels, project_attend(): pl.pallas_call(kernel, out_shape=[jax.ShapeDtypeStruct((PLANE * cot.shape...  41.4 us
  transfers between devices with their start and end apart: 4, of which 0 were waited for; matrix products, arithmetic and copies ran while one was open for 4% of the time, Pallas kernels for 79%

profile of v4, /device:TPU:0, one launch (start us, length us, event | category | flops | bytes accessed | tf_op | source)
XLA Modules:
  0.0 500.4 jit_solution(954239969645764114)
XLA Ops:
  7.2 28.5 %split_weights.1 = (bf16[8,64,256]{2,1,0:T(8,128)(2,1)}, bf16[8,64,1024]{2,1,0:T(8,128)(2,1)}, bf16[256,256]{1,0:T(8,128)(2,1)}, bf16[256,2048]{1,0:T(8,128)(2,1)}) custom-call(bf16[64,2048]{1,0:T(8,128)(2,1)} %wq_ref.1, bf16[64,8192]{1,0:T(8,128)(2,1)} %wf_ref.1, bf16[64,256]{1,0:T(8,128)(2,1)} %kv_ref.1, bf16[64,2048]{1,0:T(8,128)(2,1)} %wo_ref.1), custom_call_target="tpu_custom_call" | custom-call | tf_op jit(solution)/shard_map/split_weights/pallas_call | solution.py:364
  40.5 1.4 fusion.8.h_ref
  41.9 49.6 %gather_hidden1.1 = (bf16[2048,2048]{1,0:T(8,128)(2,1)}, bf16[2048,256]{1,0:T(8,128)(2,1)}, bf16[8,4,64,256]{3,2,1,0:T(8,128)(2,1)}) custom-call(bf16[256,2048]{1,0:T(8,128)(2,1)} %fusion.8.h_ref, bf16[256,256]{1,0:T(8,128)(2,1)} %get-tuple-element.49.kv_ref, bf16[8,64,256]{2,1,0:T(8,128)(2,1)} %get-tuple-element.50.wq_ref), custom_call_target="tpu_custom_call" | custom-call | tf_op jit(solution)/shard_map/gather_hidden1/pallas_call | solution.py:418
  91.6 41.4 %project_attend.1 = (bf16[2048,2048]{1,0:T(8,128)(2,1)}, bf16[8,2,128,256]{3,2,1,0:T(8,128)(2,1)}, bf16[8,2,128,256]{3,2,1,0:T(8,128)(2,1)}, bf16[8,2,128,256]{3,2,1,0:T(8,128)(2,1)}, f32[2,2,1024]{2,1,0:T(2,128)}) custom-call(s32[2,4]{1,0:T(2,128)} %docs_ref.3, bf16[2048,2048]{1,0:T(8,128)(2,1)} %get-tuple-element.51.h_ref, bf16[2048,256]{1,0:T(8,128)(2,1)} %bitcast.69, ...), custom_call_target="tpu_custom_call" | custom-call | flops 4294967296 | bytes 41943040 | tf_op jit(solution)/shard_map/project_attend/pallas_call | solution.py:495
  133.0 43.0 %scatter_attn.1 = f32[256,2048]{1,0:T(8,128)} custom-call(bf16[2048,256]{1,0:T(8,128)(2,1)} %bitcast.71, bf16[256,2048]{1,0:T(8,128)(2,1)} %get-tuple-element.55.w_ref), custom_call_target="tpu_custom_call" | custom-call | flops 2147483648 | bytes 41943040 | tf_op jit(solution)/shard_map/scatter_attn/pallas_call | solution.py:720
  175.9 2.0 fusion.16
  178.6 1.4 add_convert_fusion.own_ref
  180.0 51.1 %gather_fc.1 = (bf16[2048,2048]{1,0:T(8,128)(2,1)}, bf16[2048,1024]{1,0:T(8,128)(2,1)}, bf16[2048,1024]{1,0:T(8,128)(2,1)}, bf16[1024,2048]{1,0:T(8,128)(2,1)}) custom-call(bf16[256,2048]{1,0:T(8,128)(2,1)} %add_convert_fusion.own_ref, bf16[2048,1024]{1,0:T(8,128)(2,1)} %bitcast.67, f32[1,1024]{1,0:T(1,128)} %bitcast.63, ...), custom_call_target="tpu_custom_call" | custom-call | flops 17179869184 | bytes 41943040 | tf_op jit(solution)/shard_map/gather_fc/pallas_call | solution.py:601
  231.3 54.6 %scatter_fc.1 = (f32[256,2048]{1,0:T(8,128)}, f32[1,1024]{1,0:T(1,128)}, bf16[2048,1024]{1,0:T(8,128)(2,1)}) custom-call(bf16[2048,2048]{1,0:T(8,128)(2,1)} %get-tuple-element.58.cot_ref, bf16[2048,1024]{1,0:T(8,128)(2,1)} %get-tuple-element.60.slope_ref, bf16[1024,2048]{1,0:T(8,128)(2,1)} %all-gather.5.cloned.1.call-done.wp_ref, ...), custom_call_target="tpu_custom_call" | custom-call | flops 25769803776 | bytes 41943040 | tf_op jit(solution)/shard_map/scatter_fc/pallas_call | solution.py:831
  285.9 1.4 convert_reduce_fusion.1
  287.7 2.6 multiply_reduce_fusion
  290.4 2.7 convert_reduce_fusion.2
  293.0 41.6 %gather_out.1 = (bf16[2048,256]{1,0:T(8,128)(2,1)}, bf16[256,2048]{1,0:T(8,128)(2,1)}) custom-call(bf16[256,2048]{1,0:T(8,128)(2,1)} %get-tuple-element.91.own_ref, bf16[256,2048]{1,0:T(8,128)(2,1)} %get-tuple-element.55.w_ref, bf16[2048,256]{1,0:T(8,128)(2,1)} %bitcast.72), custom_call_target="tpu_custom_call" | custom-call | flops 4294967296 | bytes 41943040 | tf_op jit(solution)/shard_map/gather_out/pallas_call | solution.py:679
  334.7 49.6 %attend_back_scatter_proj.1 = (bf16[8,2,128,256]{3,2,1,0:T(8,128)(2,1)}, bf16[8,2,128,256]{3,2,1,0:T(8,128)(2,1)}, f32[256,2048]{1,0:T(8,128)}) custom-call(s32[2,4]{1,0:T(2,128)} %docs_ref.3, bf16[8,2,128,256]{3,2,1,0:T(8,128)(2,1)} %get-tuple-element.56.q_ref, bf16[8,2,128,256]{3,2,1,0:T(8,128)(2,1)} %get-tuple-element.57.kv_ref, ...), custom_call_target="tpu_custom_call" | custom-call | flops 8589934592 | bytes 41943040 | tf_op jit(solution)/shard_map/attend_back_scatter_proj/pallas_call | solution.py:1230
  384.2 1.6 convert_reduce_fusion.3
  386.1 63.7 %scatter_query.1 = (f32[256,2048]{1,0:T(8,128)}, bf16[8,64,256]{2,1,0:T(8,128)(2,1)}, bf16[256,256]{1,0:T(8,128)(2,1)}, f32[64,2048]{1,0:T(8,128)}) custom-call(bf16[2048,256]{1,0:T(8,128)(2,1)} %bitcast.56, bf16[2048,256]{1,0:T(8,128)(2,1)} %bitcast.57, bf16[2048,256]{1,0:T(8,128)(2,1)} %bitcast.70, bf16[2048,256]{1,0:T(8,128)(2,1)} %get-tuple-element.53.wkv_ref, ...), custom_call_target="tpu_custom_call" | custom-call | flops 8589934592 | bytes 41943040 | tf_op jit(solution)/shard_map/scatter_query/pallas_call | solution.py:985
  449.8 2.6 fusion.13
  453.5 24.1 %last_exchange.1 = (f32[8,24,128]{2,1,0:T(8,128)}, f32[64,256]{1,0:T(8,128)}, bf16[64,8192]{1,0:T(8,128)(2,1)}, bf16[64,2048]{1,0:T(8,128)(2,1)}) custom-call(f32[8,24,128]{2,1,0:T(8,128)} %bitcast.59, bf16[256,256]{1,0:T(8,128)(2,1)} %get-tuple-element.74.kv_ref, bf16[8,64,1024]{2,1,0:T(8,128)(2,1)} %reduce-scatter.5.cloned.1.call-done.fc_ref, ...), custom_call_target="tpu_custom_call" | custom-call | tf_op jit(solution)/shard_map/last_exchange/pallas_call | solution.py:1080
  477.7 1.6 fusion.18
  479.2 1.4 slice.48
  481.8 2.7 convert_element_type.56
  485.3 1.7 add_add_fusion
  488.3 2.1 fusion.12
  490.4 1.6 convert_element_type.57
  (84 shorter events, 11.8 us)
Async XLA Ops:
  7.2 30.8 %copy-start.19 = (f32[128]{0:T(128)S(1)}, f32[128]{0:T(128)}, u32[]{:S(2)}) copy-start(f32[128]{0:T(128)} %param.27) | copy-start | bytes 1540
  7.2 32.6 %copy-start = (bf16[2,128,2048]{2,1,0:T(8,128)(2,1)S(1)}, bf16[2,128,2048]{2,1,0:T(8,128)(2,1)}, u32[]{:S(2)}) copy-start(bf16[2,128,2048]{2,1,0:T(8,128)(2,1)} %param.17) | copy-start | bytes 3145732
  7.2 172.8 %all-gather.3.cloned.1.call-start = ((), (), s32[]{:S(2)}) async-start(), calls=%async_computation.2 | async-start | bytes 5242880 | tf_op jit(solution)/shard_map/all_gather | solution.py:1279
  35.8 4.7 copy-start.12
  35.8 4.7 copy-start.14
  35.9 195.4 %all-gather.5.cloned.1.call-start = ((), (), s32[]{:S(2)}) async-start(), calls=%async_computation.3 | async-start | bytes 5242880 | tf_op jit(solution)/shard_map/all_gather | solution.py:1279
  36.6 298.1 %reduce-scatter.3.cloned.1.call-start = ((), (), s32[]{:S(2)}) async-start(), calls=%async_computation.4 | async-start | bytes 5242880 | tf_op jit(solution)/shard_map/reduce_scatter | solution.py:1283
  132.9 43.0 %copy-start.15 = (f32[2048]{0:T(1024)S(1)}, f32[2048]{0:T(1024)}, u32[]{:S(2)}) copy-start(f32[2048]{0:T(1024)} %param.28) | copy-start | bytes 24580
  177.9 0.7 copy-start.11
  177.9 0.7 copy-start.16
  231.2 221.7 %reduce-scatter.5.cloned.1.call-start = ((), (), s32[]{:S(2)}) async-start(), calls=%async_computation.5 | async-start | bytes 5242880 | tf_op jit(solution)/shard_map/reduce_scatter | solution.py:1283
  285.9 1.5 copy-start.18
  287.7 2.7 copy-start.1
  287.7 2.7 copy-start.4
  449.8 2.7 copy-start.9
  452.9 0.6 copy-start.10
  477.6 6.8 %copy-start.8 = (bf16[64,2048]{1,0:T(8,128)(2,1)S(1)}, bf16[64,2048]{1,0:T(8,128)(2,1)}, u32[]{:S(2)}) copy-start(bf16[64,2048]{1,0:T(8,128)(2,1)} %get-tuple-element.77) | copy-start | bytes 786436
  477.6 7.7 %copy-start.5 = (f32[256,2048]{1,0:T(8,128)S(1)}, f32[256,2048]{1,0:T(8,128)}, u32[]{:S(2)}) copy-start(f32[256,2048]{1,0:T(8,128)} %get-tuple-element.68) | copy-start | bytes 6291460
  477.6 7.7 %copy-start.17 = (f32[2048]{0:T(1024)S(1)}, f32[2048]{0:T(1024)}, u32[]{:S(2)}) copy-start(f32[2048]{0:T(1024)} %param.32) | copy-start | bytes 24580
  485.3 2.2 copy-start.2
  485.3 3.0 copy-start.3
  488.3 2.1 copy-start.6
  490.4 1.6 copy-start.13
  490.4 2.2 copy-start.7
Sparse Core Ops, SparseCore 0:
  36.0 103.9 all-gather.2
  141.6 79.6 all-gather.4
  231.3 85.2 reduce-scatter.2
  318.9 77.2 reduce-scatter.4

commit v5 on v4

--- a/solution.py
+++ b/solution.py
@@ -37,6 +37,21 @@
         - normed * jnp.mean(scaled * normed, axis=-1, keepdims=True)
     )
     return (grad_in, jnp.sum(grad_out * normed, axis=0), jnp.sum(grad_out, axis=0))
+
+
+def norm_stats(values):
+    mean = jnp.mean(values, axis=-1, keepdims=True)
+    center = values - mean
+    return mean, lax.rsqrt(jnp.mean(center * center, axis=-1, keepdims=True) + epsilon)
+
+
+def norm_back(grad_out, normed, inverse, gain_row):
+    scaled = grad_out * gain_row
+    return inverse * (
+        scaled
+        - jnp.mean(scaled, axis=-1, keepdims=True)
+        - normed * jnp.mean(scaled * normed, axis=-1, keepdims=True)
+    )
 
 
 def gelu_pair(inputs):
@@ -189,8 +204,11 @@
 
 
 class Scatter:
+    LINES = 32
+
     def __init__(self, place, rows, part, sib_out, sib_in, boxes, sib_send, sib_recv, send, recv):
         self.p, self.rows, self.half = place, rows, rows // 2
+        self.wide = part.shape[2]
         self.part, self.sib_out, self.sib_in = part, sib_out, sib_in
         self.out_d, self.out_x, self.out_y, self.in_d, self.in_x, self.in_y = boxes
         self.sib_send, self.sib_recv, self.send, self.recv = sib_send, sib_recv, send, recv
@@ -203,17 +221,20 @@
             pltpu.VMEM((4, rows, wide), bf16),
             pltpu.VMEM((4, rows, wide), bf16),
             *[pltpu.VMEM((rows, wide), bf16)] * 6,
-            sems(4),
-            sems(4),
-            sems(6),
-            sems(6),
+            sems(4, 2),
+            sems(4, 2),
+            sems(8),
+            sems(8),
         ]
 
     @classmethod
     def take(cls, place, rows, refs):
         return cls(place, rows, refs[0], refs[1], refs[2], refs[3:9], *refs[9:13])
 
-    def swap(self, role, dev, product):
+    def cols(self, c):
+        return pl.ds(c * (self.wide // 2), self.wide // 2)
+
+    def swap(self, role, dev, product, c):
         p = self.p
         chip = lax.div(dev, 2) * (2 * self.rows)
 
@@ -224,75 +245,251 @@
             self.part[role, :, cols] = value
 
         product(
+            role,
             rows_at(chip + (1 - p.core) * self.rows, self.rows),
             rows_at(chip + p.core * self.rows, self.rows),
             store_out,
             store_part,
+            c,
         )
         copy = push(
-            self.sib_out.at[role],
-            self.sib_in.at[role],
-            self.sib_send.at[role],
-            self.sib_recv.at[role],
+            self.sib_out.at[role, :, self.cols(c)],
+            self.sib_in.at[role, :, self.cols(c)],
+            self.sib_send.at[role, c],
+            self.sib_recv.at[role, c],
             {"seq": p.sib},
         )
         copy.start()
         self.copies.append(copy)
         return copy
 
-    def add_into(self, dst, role, first, size, more=()):
-        lines = 32
+    def swap_all(self, role, dev, product):
+        return [self.swap(role, dev, product, c) for c in range(2)]
+
+    def add_into(self, dst, role, first, size, more=(), cols=slice(None)):
+        lines = self.LINES
 
         @pl.loop(0, size // lines)
         def _(i):
             line = rows_at(first + i * lines, lines)
-            value = self.part[role, line, :] + self.sib_in[role, line, :].astype(f32)
+            value = self.part[role, line, cols] + self.sib_in[role, line, cols].astype(f32)
             for ref in more:
-                value = value + ref[line, :].astype(f32)
-            dst[line, :] = value.astype(dst.dtype)
-
-    def ship(self, src, dst, h, k, to):
+                value = value + ref[line, cols].astype(f32)
+            if dst is None:
+                self.emit(line, value)
+            else:
+                dst[line, cols] = value.astype(dst.dtype)
+
+    def ship(self, src, dst, h, k, to, cols=slice(None)):
         lines = pl.ds(h * self.half, self.half)
         copy = push(
-            src.at[lines, :], dst.at[lines, :], self.send.at[k], self.recv.at[k], {"seq": to}
+            src.at[lines, cols], dst.at[lines, cols], self.send.at[k], self.recv.at[k], {"seq": to}
         )
         copy.start()
         self.copies.append(copy)
         return copy
 
-    def run(self, product, out_ref, idle=None):
+    def ship_corner(self, c):
+        cols = self.cols(c)
+        self.add_into(self.out_d, 0, 0, self.rows, (), cols)
+        return (
+            self.ship(self.out_d, self.in_d, 0, 2 * c, self.p.xn, cols),
+            self.ship(self.out_d, self.in_d, 1, 2 * c + 1, self.p.yn, cols),
+        )
+
+    def run(self, product, emit, idle=None):
         p, rows, half = self.p, self.rows, self.half
-        to_d = self.swap(0, p.dg, product)
-        to_x = self.swap(1, p.xn, product)
-        to_d.wait_recv()
-        self.add_into(self.out_d, 0, 0, rows)
-        dx = self.ship(self.out_d, self.in_d, 0, 0, p.xn)
-        dy = self.ship(self.out_d, self.in_d, 1, 1, p.yn)
-        to_y = self.swap(2, p.yn, product)
-        to_x.wait_recv()
+        self.emit = emit
+        d0 = self.swap(0, p.dg, product, 0)
+        d1 = self.swap(0, p.dg, product, 1)
+        d0.wait_recv()
+        dx0, dy0 = self.ship_corner(0)
+        to_x = [self.swap(1, p.xn, product, 0)]
+        d1.wait_recv()
+        dx1, dy1 = self.ship_corner(1)
+        to_x.append(self.swap(1, p.xn, product, 1))
+        to_y = self.swap_all(2, p.yn, product)
+        for copy in to_x:
+            copy.wait_recv()
         self.add_into(self.out_x, 1, 0, half)
-        x0 = self.ship(self.out_x, self.in_x, 0, 2, p.xn)
-        to_y.wait_recv()
+        x0 = self.ship(self.out_x, self.in_x, 0, 4, p.xn)
+        for copy in to_y:
+            copy.wait_recv()
         self.add_into(self.out_y, 2, half, half)
-        y1 = self.ship(self.out_y, self.in_y, 1, 3, p.yn)
-        to_me = self.swap(3, p.me, product)
-        dy.wait_recv()
+        y1 = self.ship(self.out_y, self.in_y, 1, 5, p.yn)
+        to_me = self.swap_all(3, p.me, product)
+        dy0.wait_recv()
+        dy1.wait_recv()
         self.add_into(self.out_x, 1, half, half, (self.in_d,))
-        x1 = self.ship(self.out_x, self.in_x, 1, 4, p.xn)
-        dx.wait_recv()
+        x1 = self.ship(self.out_x, self.in_x, 1, 6, p.xn)
+        dx0.wait_recv()
+        dx1.wait_recv()
         self.add_into(self.out_y, 2, 0, half, (self.in_d,))
-        y0 = self.ship(self.out_y, self.in_y, 0, 5, p.yn)
+        y0 = self.ship(self.out_y, self.in_y, 0, 7, p.yn)
         if idle is not None:
             idle()
-        to_me.wait_recv()
+        for copy in to_me:
+            copy.wait_recv()
         x0.wait_recv()
         y0.wait_recv()
-        self.add_into(out_ref, 3, 0, half, (self.in_x, self.in_y))
+        self.add_into(None, 3, 0, half, (self.in_x, self.in_y))
         y1.wait_recv()
         x1.wait_recv()
-        self.add_into(out_ref, 3, half, half, (self.in_x, self.in_y))
+        self.add_into(None, 3, half, half, (self.in_x, self.in_y))
         for copy in self.copies:
             copy.wait_send()
+
+
+class LineGather:
+    def __init__(self, place, src, out, layers, send, recv):
+        self.p, self.src, self.out, self.layers = place, src, out, layers
+        self.send, self.recv = send, recv
+        self.moves = [d for d in (2, -2, 1, -1) if abs(d) < layers]
+
+    def block(self, layer):
+        rows = self.src.shape[0]
+        return self.out.at[rows_at(layer * rows, rows), :]
+
+    def copy(self, src, layer, k, to):
+        return push(src, self.block(layer), self.send.at[k], self.recv.at[layer], {"fsdp": to})
+
+    def inside(self, layer):
+        return (layer >= 0) & (layer < self.layers)
+
+    def start(self):
+        me = self.p.layer
+        for k, d in enumerate(self.moves):
+
+            @pl.when(self.inside(me + d))
+            def _(k=k, d=d):
+                self.copy(self.src, me, k, me + d).start()
+
+    def wait_from(self, layer):
+        block = self.block(layer)
+        other = lax.rem(self.p.layer + 1, self.layers)
+        push(block, block, self.send.at[0], self.recv.at[layer], {"fsdp": other}).wait_recv()
+
+    def passing(self):
+        me = self.p.layer
+        found = []
+        for far in range(3, self.layers):
+            for sign in (1, -1):
+                source, to = me - sign * (far - 1), me + sign
+                found.append((self.inside(source) & self.inside(to), source, to))
+        return found
+
+    def relay(self):
+        for k, (here, source, to) in enumerate(self.passing()):
+
+            @pl.when(here)
+            def _(k=k, source=source, to=to):
+                self.wait_from(source)
+                self.copy(self.block(source), source, len(self.moves) + k, to).start()
+
+    def finish(self):
+        me = self.p.layer
+        passed = self.passing()
+        for step in range(1, self.layers):
+            source = lax.rem(me + step, self.layers)
+            waited = None
+            for here, whose, _ in passed:
+                hit = here & (whose == source)
+                waited = hit if waited is None else waited | hit
+            if waited is None:
+                self.wait_from(source)
+            else:
+                pl.when(jnp.logical_not(waited))(lambda source=source: self.wait_from(source))
+        for k, d in enumerate(self.moves):
+
+            @pl.when(self.inside(me + d))
+            def _(k=k, d=d):
+                self.copy(self.src, me, k, me + d).wait_send()
+
+        for k, (here, source, to) in enumerate(passed):
+
+            @pl.when(here)
+            def _(k=k, source=source, to=to):
+                self.copy(self.block(source), source, len(self.moves) + k, to).wait_send()
+
+    @staticmethod
+    def scratch(layers):
+        return [sems(4 + 2 * max(0, layers - 3)), sems(layers)]
+
+
+class LineSum:
+    def __init__(self, place, block, box, layers, send, recv):
+        self.copies = []
+        self.box = box
+        for step in range(1, layers):
+            to = place.line_peer(step, layers)
+            copy = push(block(to), box.at[step - 1], send.at[step], recv.at[step], {"fsdp": to})
+            copy.start()
+            self.copies.append(copy)
+
+    def arrived(self):
+        for copy in self.copies:
+            copy.wait_recv()
+
+    def total(self, own, where):
+        value = own.astype(f32)
+        for k in range(len(self.copies)):
+            value = value + self.box[(k, *where)].astype(f32)
+        return value
+
+    def finish(self):
+        for copy in self.copies:
+            copy.wait_send()
+
+
+class PlaneSum:
+    def __init__(self, place, src, box, send, recv):
+        self.p, self.src, self.box = place, src, box
+        self.copies = []
+        for step in range(1, PLANE):
+            to = place.plane_peer(step)
+            copy = push(src.at[to], box.at[step], send.at[step], recv.at[step], {"seq": to})
+            copy.start()
+            self.copies.append(copy)
+
+    def total(self):
+        value = self.src[self.p.me].astype(f32)
+        for step, copy in enumerate(self.copies):
+            copy.wait_recv()
+            value = value + self.box[step + 1].astype(f32)
+        return value
+
+    def finish(self):
+        for copy in self.copies:
+            copy.wait_send()
+
+
+class Spread:
+    def __init__(self, place, src, out, send, recv, local):
+        cols = src.shape[2]
+        spot = out.at[:, rows_at(place.me * cols, cols)]
+        self.copies = [load(src.at[place.me], spot, local)]
+        for step in range(1, PLANE):
+            to = place.plane_peer(step)
+            copy = push(src.at[to], spot, send.at[step], recv.at[step], {"seq": to})
+            copy.start()
+            self.copies.append(copy)
+
+    def finish(self):
+        for copy in self.copies:
+            copy.wait()
+
+
+def fold(ref, first, value):
+    rows, wide = value.shape
+    total = jnp.sum(value.reshape(rows // 8, 8, wide), axis=0)
+
+    @pl.when(first)
+    def _():
+        ref[...] = total
+
+    @pl.when(jnp.logical_not(first))
+    def _():
+        ref[...] += total
 
 
 def params(number, vmem=True):
@@ -313,18 +510,19 @@
     return copy
 
 
-def split_weights(w_query, w_fc, w_kv, w_out, layers, number):
+def split_weights(tokens, gain, shift, w_query, w_fc, w_kv, w_out, layers, number):
     arrays, lined = (w_query, w_fc), (w_kv, w_out)
-
-    def kernel(wq_ref, wf_ref, kv_ref, wo_ref, wq_out, wf_out, kv_out, wo_out, *refs):
-        send, recv, zsend, zrecv, local = refs
+    own_rows, width = tokens.shape
+
+    def kernel(tok_ref, gain_ref, shift_ref, wq_ref, wf_ref, kv_ref, wo_ref, *refs):
+        wq_out, wf_out, kv_out, wo_out, hidden, mean_out, inverse_out = refs[:7]
+        send, recv, kv_send, kv_recv, wo_send, wo_recv, local = refs[7:]
         p = Place()
         ins, outs = (wq_ref, wf_ref), (wq_out, wf_out)
-        line_ins = (kv_ref, wo_ref)
-        mine = [
-            out.at[rows_at(p.layer * src.shape[0], src.shape[0]), :]
-            for src, out in zip(line_ins, (kv_out, wo_out))
-        ]
+        lines = (
+            LineGather(p, kv_ref, kv_out, layers, kv_send, kv_recv),
+            LineGather(p, wo_ref, wo_out, layers, wo_send, wo_recv),
+        )
 
         def block(i, dev):
             cols = ins[i].shape[1] // PLANE
@@ -332,20 +530,13 @@
 
         own = []
         for i in range(2):
-            own.append(load(line_ins[i], mine[i], local.at[2 + i]))
+            own.append(load(lines[i].src, lines[i].block(p.layer), local.at[2 + i]))
             own.append(load(block(i, p.me), outs[i].at[p.me], local.at[i]))
         p.greet(True, layers)
+        for line in lines:
+            line.start()
         copies = []
-        for i in range(2):
-            for step in range(1, layers):
-                to = p.line_peer(step, layers)
-                copies.append(
-                    push(
-                        line_ins[i], mine[i], zsend.at[i, step], zrecv.at[i, step], {"fsdp": to}
-                    )
-                )
-                copies[-1].start()
-        for i in range(2):
+        for i in (1, 0):
             for step in range(1, PLANE):
                 to = p.plane_peer(step)
                 copies.append(
@@ -358,8 +549,24 @@
                     )
                 )
                 copies[-1].start()
+
+        @pl.loop(0, own_rows // 32)
+        def _(i):
+            here = rows_at(i * 32, 32)
+            values = tok_ref[here, :].astype(f32)
+            mean, inverse = norm_stats(values)
+            hidden[here, :] = (
+                (values - mean) * inverse * gain_ref[...] + shift_ref[...]
+            ).astype(bf16)
+            mean_out[here, :] = mean
+            inverse_out[here, :] = inverse
+
+        for line in lines:
+            line.relay()
         for copy in own + copies:
             copy.wait()
+        for line in lines:
+            line.finish()
 
     return pl.pallas_call(
         kernel,
@@ -367,19 +574,17 @@
             jax.ShapeDtypeStruct((PLANE, a.shape[0], a.shape[1] // PLANE), a.dtype)
             for a in arrays
         ]
-        + [jax.ShapeDtypeStruct((layers * a.shape[0], a.shape[1]), a.dtype) for a in lined],
-        in_specs=[ANY] * 4,
-        out_specs=[ANY] * 4,
-        scratch_shapes=[
-            sems(2, PLANE),
-            sems(2, PLANE),
-            sems(2, layers),
-            sems(2, layers),
-            sems(4),
-        ],
-        compiler_params=params(number, False),
+        + [jax.ShapeDtypeStruct((layers * a.shape[0], a.shape[1]), a.dtype) for a in lined]
+        + [jax.ShapeDtypeStruct((own_rows, width), bf16)]
+        + [jax.ShapeDtypeStruct((own_rows, 1), f32)] * 2,
+        in_specs=[WHOLE] * 3 + [ANY] * 4,
+        out_specs=[ANY] * 4 + [WHOLE] * 3,
+        scratch_shapes=[sems(2, PLANE), sems(2, PLANE)]
+        + LineGather.scratch(layers) * 2
+        + [sems(4)],
+        compiler_params=params(number),
         name="split_weights",
-    )(w_query, w_fc, w_kv, w_out)
+    )(tokens, gain, shift, w_query, w_fc, w_kv, w_out)
 
 
 def gather_hidden1(hidden1, low_kv, wq_pieces, layers, number):
@@ -703,55 +908,77 @@
 TILE = 512
 
 
-def scatter_attn(a, weight, number):
-    total, depth = a.shape
+def scatter_attn(mixed, wo, tokens, b_out, gain, shift, number):
+    total, depth = mixed.shape
     rows = total // PLANE
-    wide = weight.shape[1]
-
-    def kernel(a_ref, w_ref, out_ref, a_buf, w_buf, *refs):
-        s, local = refs[:13], refs[13]
+    wide = wo.shape[1]
+
+    def kernel(a_ref, w_ref, tok_ref, bias_ref, gain_ref, shift_ref, *refs):
+        residual, hidden, mean_out, inverse_out = refs[:4]
+        a_buf, w_buf = refs[4:6]
+        s, local = refs[6:19], refs[19]
         p = Place()
         loads = [load(a_ref, a_buf, local.at[0]), load(w_ref, w_buf, local.at[1])]
         p.greet()
         for copy in loads:
             copy.wait()
-        Scatter.take(p, rows, s).run(plain_product(a_buf, w_buf), out_ref)
+
+        def emit(line, value):
+            values = tok_ref[line, :].astype(f32) + value + bias_ref[...]
+            mean, inverse = norm_stats(values)
+            residual[line, :] = values
+            hidden[line, :] = (
+                (values - mean) * inverse * gain_ref[...] + shift_ref[...]
+            ).astype(bf16)
+            mean_out[line, :] = mean
+            inverse_out[line, :] = inverse
+
+        Scatter.take(p, rows, s).run(plain_product(a_buf, w_buf), emit)
 
     return pl.pallas_call(
         kernel,
-        out_shape=jax.ShapeDtypeStruct((rows, wide), f32),
-        in_specs=[ANY] * 2,
-        out_specs=WHOLE,
-        scratch_shapes=[pltpu.VMEM(a.shape, bf16), pltpu.VMEM(weight.shape, bf16)]
+        out_shape=[
+            jax.ShapeDtypeStruct((rows, wide), f32),
+            jax.ShapeDtypeStruct((rows, wide), bf16),
+            jax.ShapeDtypeStruct((rows, 1), f32),
+            jax.ShapeDtypeStruct((rows, 1), f32),
+        ],
+        in_specs=[ANY] * 2 + [WHOLE] * 4,
+        out_specs=[WHOLE] * 4,
+        scratch_shapes=[pltpu.VMEM(mixed.shape, bf16), pltpu.VMEM(wo.shape, bf16)]
         + Scatter.scratch(rows, wide)
         + [sems(2)],
         compiler_params=params(number),
         cost_estimate=cost(2 * total * depth * wide),
         name="scatter_attn",
-    )(a, weight)
+    )(mixed, wo, tokens, b_out, gain, shift)
 
 
 def plain_product(a_buf, w_buf):
-    def product(theirs, ours, store_out, store_part):
-        @pl.loop(0, w_buf.shape[1] // TILE)
+    steps = w_buf.shape[1] // 2 // TILE
+
+    def product(role, theirs, ours, store_out, store_part, c):
+        @pl.loop(0, steps)
         def _(j):
-            cols = rows_at(j * TILE, TILE)
+            cols = rows_at((c * steps + j) * TILE, TILE)
             store_out(cols, dot(a_buf[theirs, :], w_buf[:, cols]))
             store_part(cols, dot(a_buf[ours, :], w_buf[:, cols]))
 
     return product
 
 
-def scatter_fc(cot_all, slope, wp, wf, hidden2, number):
+def scatter_fc(cot_all, slope, wp, wf, hidden2, cot, residual, mean, inverse, gain, number):
     total, depth = cot_all.shape
     rows = total // PLANE
     wide = wp.shape[0]
     tile = 256
 
-    def kernel(cot_ref, slope_ref, wp_ref, wf_ref, h_ref, out_ref, bias_ref, dw_ref, *refs):
-        cot, slopes, wp_buf, wf_buf, gp, h_buf, dw_buf = refs[:7]
-        s = refs[7:20]
-        (local,) = refs[20:]
+    def kernel(cot_ref, slope_ref, wp_ref, wf_ref, h_ref, *refs):
+        cot_own, residual_ref, mean_ref, inverse_ref, gain_ref = refs[:5]
+        grad_residual, grad_attn, sums_ref, bias_ref, dw_ref = refs[5:10]
+        cot, slopes, wp_buf, wf_buf, gp, h_buf, dw_buf, folds = refs[10:18]
+        s = refs[18:31]
+        (local,) = refs[31:]
         p = Place()
         order = (p.dg, p.xn, p.yn, p.me)
 
@@ -771,11 +998,9 @@
         bias_ref[...] = jnp.zeros_like(bias_ref)
         p.greet()
         load_wp.wait()
-        count = []
-
-        def product(theirs, ours, store_out, store_part):
-            k = len(count)
-            count.append(k)
+        halves = depth // 2 // TILE
+
+        def back_through_gelu(k):
             for copy in fetches[k]:
                 copy.wait()
             if k < 3:
@@ -793,11 +1018,27 @@
             if k == 0:
                 load_wf.wait()
 
-            @pl.loop(0, depth // TILE)
+        def product(role, theirs, ours, store_out, store_part, c):
+            if c == 0:
+                back_through_gelu(role)
+
+            @pl.loop(0, halves)
             def _(j):
-                cols = rows_at(j * TILE, TILE)
+                cols = rows_at((c * halves + j) * TILE, TILE)
                 store_out(cols, dot_nt(gp[theirs, :], wf_buf[cols, :]))
                 store_part(cols, dot_nt(gp[ours, :], wf_buf[cols, :]))
+
+        def emit(line, value):
+            first = line.start == 0
+            grad_out = cot_own[line, :].astype(f32)
+            back = inverse_ref[line, :]
+            normed = (residual_ref[line, :] - mean_ref[line, :]) * back
+            result = grad_out + norm_back(value, normed, back, gain_ref[...])
+            low = result.astype(bf16)
+            grad_residual[line, :] = result
+            grad_attn[line, :] = low
+            for i, term in enumerate((value * normed, value, low.astype(f32), grad_out)):
+                fold(folds.at[i], first, term)
 
         steps = depth // tile
 
@@ -826,17 +1067,20 @@
             for copy in stores[-2:]:
                 copy.wait()
 
-        Scatter.take(p, rows, s).run(product, out_ref, idle)
+        Scatter.take(p, rows, s).run(product, emit, idle)
+        sums_ref[...] = jnp.sum(folds[...], axis=1)
 
     return pl.pallas_call(
         kernel,
         out_shape=[
             jax.ShapeDtypeStruct((rows, depth), f32),
+            jax.ShapeDtypeStruct((rows, depth), bf16),
+            jax.ShapeDtypeStruct((4, depth), f32),
             jax.ShapeDtypeStruct((1, wide), f32),
             jax.ShapeDtypeStruct((depth, wide), bf16),
         ],
-        in_specs=[ANY] * 5,
-        out_specs=[WHOLE, WHOLE, ANY],
+        in_specs=[ANY] * 5 + [WHOLE] * 5,
+        out_specs=[WHOLE] * 4 + [ANY],
         scratch_shapes=[
             pltpu.VMEM((2, 2 * rows, depth), bf16),
             pltpu.VMEM((2, 2 * rows, wide), bf16),
@@ -845,210 +1089,163 @@
             pltpu.VMEM((total, wide), bf16),
             pltpu.VMEM((2, total, tile), bf16),
             pltpu.VMEM((2, tile, wide), bf16),
+            pltpu.VMEM((4, 8, depth), f32),
         ]
         + Scatter.scratch(rows, depth)
         + [sems(10)],
         compiler_params=params(number),
         cost_estimate=cost(6 * total * depth * wide),
         name="scatter_fc",
-    )(cot_all, slope, wp, wf, hidden2)
-
-
-class LineSum:
-    def __init__(self, place, block, box, layers, send, recv):
-        self.copies = []
-        self.box = box
-        for step in range(1, layers):
-            to = place.line_peer(step, layers)
-            copy = push(block(to), box.at[step - 1], send.at[step], recv.at[step], {"fsdp": to})
-            copy.start()
-            self.copies.append(copy)
-
-    def arrived(self):
-        for copy in self.copies:
-            copy.wait_recv()
-
-    def total(self, own, where):
-        value = own.astype(f32)
-        for k in range(len(self.copies)):
-            value = value + self.box[(k, *where)].astype(f32)
-        return value
-
-    def finish(self):
-        for copy in self.copies:
-            copy.wait_send()
-
-
-def scatter_query(gq, gkv, wq, w_kv, hidden1, grad_w_out, layers, number):
+    )(cot_all, slope, wp, wf, hidden2, cot, residual, mean, inverse, gain)
+
+
+def scatter_query(
+    gq, gkv, wq, w_kv, grad_w_out, grad_w_query, grad_w_kv, back, layers, number
+):
     total, cols = gq.shape
     kv_cols = gkv.shape[1]
     rows = total // PLANE
     depth = wq.shape[0]
-    part_rows = depth // PLANE
-    line_rows = part_rows // layers
-    out_rows = grad_w_out.shape[0] // layers
-    out_wide = grad_w_out.shape[1]
-
-    def kernel(gq_ref, gkv_ref, wq_ref, wkv_ref, h_ref, dwo_ref, *refs):
-        out_ref, dwq_ref, dwkv_ref, dwo_out = refs[:4]
-        g_buf, wq_buf, wkv_buf, h_buf, dwq_buf, dwq_box, dkv, box, dwo_own, dwo_box = refs[4:14]
-        s = refs[14:27]
-        ksend, krecv, zsend, zrecv, qsend, qrecv, local = refs[27:]
+    out_rows, out_wide = grad_w_out.shape[0] // layers, grad_w_out.shape[1]
+    q_rows, q_cols = grad_w_query.shape[2:]
+    kv_part = grad_w_kv.shape[1]
+    kv_rows = kv_part // layers
+
+    def kernel(gq_ref, gkv_ref, wq_ref, wkv_ref, dwo_ref, dwq_ref, dwkv_ref, *refs):
+        tok_ref, mean_ref, inverse_ref, gain_ref, residual_ref = refs[:5]
+        out_ref, sums_ref, dwo_out, dwq_out, dwkv_out = refs[5:10]
+        g_buf, wq_buf, wkv_buf, folds = refs[10:14]
+        dwo_own, dwo_box, q_own, q_box, q_sum, kv_box, kv_sum, kvz_box = refs[14:22]
+        s = refs[22:35]
+        (osend, orecv, qzsend, qzrecv, qsend, qrecv, ksend, krecv, kzsend, kzrecv, local) = refs[
+            35:
+        ]
         p = Place()
-
-        def dwo_block(layer):
-            return dwo_ref.at[rows_at(layer * out_rows, out_rows), :]
-
-        load_dwo = load(dwo_block(p.layer), dwo_own, local.at[7])
-        q_part, kv_part = pl.ds(0, cols), pl.ds(cols, kv_cols)
+        q_side, kv_side = pl.ds(0, cols), pl.ds(cols, kv_cols)
         loads = [
-            load(gq_ref, g_buf.at[:, q_part], local.at[0]),
-            load(gkv_ref, g_buf.at[:, kv_part], local.at[1]),
+            load(gq_ref, g_buf.at[:, q_side], local.at[0]),
+            load(gkv_ref, g_buf.at[:, kv_side], local.at[1]),
             load(wq_ref, wq_buf, local.at[2]),
             load(wkv_ref, wkv_buf, local.at[3]),
         ]
 
-        def h_fetch(i):
-            dev = p.plane_peer((i + 1) % PLANE)
-            return load(
-                h_ref.at[:, rows_at(dev * part_rows, part_rows)],
-                h_buf.at[i % 2],
-                local.at[4 + i % 2],
-            )
-
-        tiles = [h_fetch(0)]
+        def dwo_block(layer):
+            return dwo_ref.at[rows_at(layer * out_rows, out_rows), :]
+
+        def dwq_block(layer):
+            return dwq_ref.at[:, layer]
+
+        own = [
+            load(dwo_block(p.layer), dwo_own, local.at[4]),
+            load(dwq_block(p.layer), q_own, local.at[5]),
+        ]
         p.greet(True, layers)
-        line = LineSum(p, dwo_block, dwo_box, layers, zsend, zrecv)
+        plane_kv = PlaneSum(p, dwkv_ref, kv_box, ksend, krecv)
+        line_q = LineSum(p, dwq_block, q_box, layers, qzsend, qzrecv)
+        line_o = LineSum(p, dwo_block, dwo_box, layers, osend, orecv)
         for copy in loads:
             copy.wait()
-
-        def product(theirs, ours, store_out, store_part):
-            @pl.loop(0, depth // TILE)
+        halves = depth // 2 // TILE
+
+        def product(role, theirs, ours, store_out, store_part, c):
+            @pl.loop(0, halves)
             def _(j):
-                where = rows_at(j * TILE, TILE)
+                where = rows_at((c * halves + j) * TILE, TILE)
                 for rows_of, store in ((theirs, store_out), (ours, store_part)):
                     store(
                         where,
-                        dot_nt(g_buf[rows_of, q_part], wq_buf[where, :])
-                        + dot_nt(g_buf[rows_of, kv_part], wkv_buf[where, :]),
+                        dot_nt(g_buf[rows_of, q_side], wq_buf[where, :])
+                        + dot_nt(g_buf[rows_of, kv_side], wkv_buf[where, :]),
                     )
 
-        sent = []
-        lines_q = []
+        later = []
 
         def idle():
-            for i in range(PLANE):
-                step = (i + 1) % PLANE
-                dev = p.plane_peer(step)
-                tiles[i].wait()
-                if i + 1 < PLANE:
-                    tiles.append(h_fetch(i + 1))
-                term = dot_tn(h_buf[i % 2], g_buf[...]).astype(bf16)
-                dwq_buf[dev] = term[:, :cols].reshape(layers, line_rows, cols)
-                dkv[step] = term[:, cols:]
-                if step:
-                    copy = push(
-                        dkv.at[step], box.at[step], ksend.at[step], krecv.at[step], {"seq": dev}
-                    )
-                    copy.start()
-                    sent.append(copy)
-            lines_q.append(
-                LineSum(p, lambda layer: dwq_buf.at[:, layer], dwq_box, layers, qsend, qrecv)
+            for copy in own:
+                copy.wait()
+            kv_sum[...] = plane_kv.total().astype(bf16).reshape(layers, kv_rows, kv_cols)
+            line_kv = LineSum(p, lambda layer: kv_sum.at[layer], kvz_box, layers, kzsend, kzrecv)
+            line_q.arrived()
+
+            @pl.loop(0, PLANE)
+            def _(i):
+                q_sum[i] = line_q.total(q_own[i], (i,)).astype(bf16)
+
+            later.append(Spread(p, q_sum, dwq_out, qsend, qrecv, local.at[6]))
+            line_kv.arrived()
+            dwkv_out[...] = line_kv.total(kv_sum[p.layer], ())
+            later.append(line_kv)
+            line_o.arrived()
+
+            @pl.loop(0, out_rows // 16)
+            def _(i):
+                lines = rows_at(i * 16, 16)
+                dwo_out[lines, :] = line_o.total(dwo_own[lines, :], (lines, slice(None)))
+
+        def emit(line, value):
+            first = line.start == 0
+            normed = (tok_ref[line, :].astype(f32) - mean_ref[line, :]) * inverse_ref[line, :]
+            out_ref[line, :] = residual_ref[line, :] + norm_back(
+                value, normed, inverse_ref[line, :], gain_ref[...]
             )
-
-        Scatter.take(p, rows, s).run(product, out_ref, idle)
-        sum_kv = dkv[0].astype(f32)
-        for i, copy in enumerate(sent):
-            copy.wait_recv()
-            sum_kv = sum_kv + box[i + 1].astype(f32)
-        dwkv_ref[...] = sum_kv.astype(bf16)
-        load_dwo.wait()
-        line.arrived()
-
-        @pl.loop(0, out_rows // 16)
-        def _(i):
-            lines = rows_at(i * 16, 16)
-            dwo_out[lines, :] = line.total(dwo_own[lines, :], (lines, slice(None)))
-
-        (line_q,) = lines_q
-        line_q.arrived()
-
-        @pl.loop(0, PLANE)
-        def _(i):
-            dwq_ref[i] = line_q.total(dwq_buf[i, p.layer], (i,)).astype(bf16)
-
-        for copy in sent:
-            copy.wait_send()
-        line.finish()
+            fold(folds.at[0], first, value * normed)
+            fold(folds.at[1], first, value)
+
+        Scatter.take(p, rows, s).run(product, emit, idle)
+        sums_ref[...] = jnp.sum(folds[...], axis=1)
+        plane_kv.finish()
         line_q.finish()
+        line_o.finish()
+        for item in later:
+            item.finish()
 
     return pl.pallas_call(
         kernel,
         out_shape=[
             jax.ShapeDtypeStruct((rows, depth), f32),
-            jax.ShapeDtypeStruct((PLANE, line_rows, cols), bf16),
-            jax.ShapeDtypeStruct((part_rows, kv_cols), bf16),
+            jax.ShapeDtypeStruct((2, depth), f32),
             jax.ShapeDtypeStruct((out_rows, out_wide), f32),
+            jax.ShapeDtypeStruct((q_rows, PLANE * q_cols), bf16),
+            jax.ShapeDtypeStruct((kv_rows, kv_cols), f32),
         ],
-        in_specs=[ANY] * 6,
-        out_specs=[WHOLE] * 4,
+        in_specs=[ANY] * 6 + [WHOLE] * 6,
+        out_specs=[WHOLE] * 3 + [ANY, WHOLE],
         scratch_shapes=[
             pltpu.VMEM((total, cols + kv_cols), bf16),
             pltpu.VMEM(wq.shape, bf16),
             pltpu.VMEM(w_kv.shape, bf16),
-            pltpu.VMEM((2, total, part_rows), bf16),
-            pltpu.VMEM((PLANE, layers, line_rows, cols), bf16),
-            pltpu.VMEM((layers - 1, PLANE, line_rows, cols), bf16),
-            pltpu.VMEM((PLANE, part_rows, kv_cols), bf16),
-            pltpu.VMEM((PLANE, part_rows, kv_cols), bf16),
+            pltpu.VMEM((2, 8, depth), f32),
             pltpu.VMEM((out_rows, out_wide), bf16),
             pltpu.VMEM((layers - 1, out_rows, out_wide), bf16),
+            pltpu.VMEM((PLANE, q_rows, q_cols), bf16),
+            pltpu.VMEM((layers - 1, PLANE, q_rows, q_cols), bf16),
+            pltpu.VMEM((PLANE, q_rows, q_cols), bf16),
+            pltpu.VMEM((PLANE, kv_part, kv_cols), bf16),
+            pltpu.VMEM((layers, kv_rows, kv_cols), bf16),
+            pltpu.VMEM((layers - 1, kv_rows, kv_cols), bf16),
         ]
         + Scatter.scratch(rows, depth)
-        + [sems(PLANE)] * 2
         + [sems(layers)] * 4
-        + [sems(8)],
+        + [sems(PLANE)] * 4
+        + [sems(layers)] * 2
+        + [sems(7)],
         compiler_params=params(number),
-        cost_estimate=cost(4 * total * depth * (cols + kv_cols)),
+        cost_estimate=cost(2 * total * depth * (cols + kv_cols)),
         name="scatter_query",
-    )(gq, gkv, wq, w_kv, hidden1, grad_w_out)
-
-
-def last_exchange(vector, fc_pieces, q_pieces, grad_w_kv, layers, number):
+    )(gq, gkv, wq, w_kv, grad_w_out, grad_w_query, grad_w_kv, *back)
+
+
+def last_exchange(vector, fc_pieces, layers, number):
     lines = vector.shape[1]
-    pieces = (fc_pieces, q_pieces)
-    kv_rows, kv_cols = grad_w_kv.shape[0] // layers, grad_w_kv.shape[1]
-
-    def kernel(vec, kv_ref, fc_ref, q_ref, vec_out, kv_out, fc_out, q_out, *refs):
-        box, plane_sum, zbox, kv_box = refs[:4]
-        vsend, vrecv, zsend, zrecv, kzsend, kzrecv, gsend, grecv, send, recv, local = refs[4:]
+
+    def kernel(vec, fc_ref, vec_out, fc_out, *refs):
+        box, plane_sum, zbox = refs[:3]
+        vsend, vrecv, zsend, zrecv, gsend, grecv, send, recv, local = refs[3:]
         p = Place()
-
-        def kv_block(layer):
-            return kv_ref.at[rows_at(layer * kv_rows, kv_rows), :]
-
         p.greet(True, layers)
-        first, copies = [], []
-        for step in range(1, PLANE):
-            to = p.plane_peer(step)
-            copy = push(vec.at[to], box.at[step], vsend.at[step], vrecv.at[step], {"seq": to})
-            copy.start()
-            first.append(copy)
-        line_kv = LineSum(p, kv_block, kv_box, layers, kzsend, kzrecv)
-        for i, (src, out) in enumerate(((fc_ref, fc_out), (q_ref, q_out))):
-            cols = src.shape[2]
-            place = out.at[:, rows_at(p.me * cols, cols)]
-            copies.append(load(src.at[p.me], place, local.at[i]))
-            for step in range(1, PLANE):
-                to = p.plane_peer(step)
-                copies.append(
-                    push(src.at[to], place, send.at[i, step], recv.at[i, step], {"seq": to})
-                )
-                copies[-1].start()
-        total = vec[p.me]
-        for step in range(1, PLANE):
-            first[step - 1].wait_recv()
-            total = total + box[step]
+        plane = PlaneSum(p, vec, box, vsend, vrecv)
+        spread = Spread(p, fc_ref, fc_out, send, recv, local.at[0])
+        total = plane.total()
         plane_sum[...] = total
         zbox[0] = total
         across = []
@@ -1057,8 +1254,6 @@
             copy = push(plane_sum, zbox.at[step], zsend.at[step], zrecv.at[step], {"fsdp": to})
             copy.start()
             across.append(copy)
-        line_kv.arrived()
-        kv_out[...] = line_kv.total(kv_ref[rows_at(p.layer * kv_rows, kv_rows), :], ())
         for copy in across:
             copy.wait_recv()
         total = None
@@ -1066,40 +1261,39 @@
             term = zbox[lax.rem(p.layer - k + layers, layers)]
             total = term if total is None else total + term
         vec_out[p.me] = total
+        last = []
         for step in range(1, PLANE):
             to = p.plane_peer(step)
             mine = vec_out.at[p.me]
-            copies.append(push(mine, mine, gsend.at[step], grecv.at[step], {"seq": to}))
-            copies[-1].start()
-        for copy in copies:
+            last.append(push(mine, mine, gsend.at[step], grecv.at[step], {"seq": to}))
+            last[-1].start()
+        for copy in last:
             copy.wait()
-        for copy in first + across:
+        spread.finish()
+        plane.finish()
+        for copy in across:
             copy.wait_send()
-        line_kv.finish()
 
     return pl.pallas_call(
         kernel,
         out_shape=[
             jax.ShapeDtypeStruct(vector.shape, f32),
-            jax.ShapeDtypeStruct((kv_rows, kv_cols), f32),
-        ]
-        + [jax.ShapeDtypeStruct((a.shape[1], PLANE * a.shape[2]), a.dtype) for a in pieces],
-        in_specs=[WHOLE, WHOLE, ANY, ANY],
-        out_specs=[WHOLE, WHOLE, ANY, ANY],
+            jax.ShapeDtypeStruct((fc_pieces.shape[1], PLANE * fc_pieces.shape[2]), bf16),
+        ],
+        in_specs=[WHOLE, ANY],
+        out_specs=[WHOLE, ANY],
         scratch_shapes=[
             pltpu.VMEM((PLANE, lines, 128), f32),
             pltpu.VMEM((lines, 128), f32),
             pltpu.VMEM((layers, lines, 128), f32),
-            pltpu.VMEM((layers - 1, kv_rows, kv_cols), bf16),
         ]
         + [sems(PLANE)] * 2
-        + [sems(layers)] * 4
-        + [sems(PLANE)] * 2
-        + [sems(2, PLANE)] * 2
-        + [sems(2)],
+        + [sems(layers)] * 2
+        + [sems(PLANE)] * 4
+        + [sems(1)],
         compiler_params=params(number, False),
         name="last_exchange",
-    )(vector, grad_w_kv, *pieces)
+    )(vector, fc_pieces)
 
 
 def starts_of(docs, stream, positions):
@@ -1178,17 +1372,23 @@
     gkv_ref[:, :, HD:] = gv[...].astype(bf16).reshape(groups, rows, HD)
 
 
-def attend_back_scatter_proj(docs, queries, keyval, grads, lse, act, wp, heads, number):
+def attend_back_scatter_proj(
+    docs, queries, keyval, grads, lse, act, wp, hidden1, residual, b_proj, layers, heads, number
+):
     groups, streams, rows, cols = queries.shape
+    kv_cols = keyval.shape[3]
     length = groups * rows
     total, depth = act.shape
     own = total // PLANE
     wide = wp.shape[1]
-
-    def kernel(docs_ref, q_ref, kv_ref, g_ref, lse_ref, act_ref, wp_ref, *refs):
-        gq_out, gkv_out, out_ref = refs[:3]
-        a_buf, w_buf, q_buf, kv_buf, g_buf, gq_buf, gkv_buf, gk, gv = refs[3:12]
-        s, local = refs[12:25], refs[25]
+    part = hidden1.shape[1] // PLANE
+
+    def kernel(docs_ref, q_ref, kv_ref, g_ref, lse_ref, act_ref, wp_ref, h_ref, *refs):
+        residual_ref, bias_ref = refs[:2]
+        gq_out, gkv_out, gq_sum, gkv_sum, dwq_out, dwkv_out, out_ref = refs[2:9]
+        a_buf, w_buf, q_buf, kv_buf, g_buf, grad_buf, gk, gv, h_buf = refs[9:18]
+        dwq_buf, dwkv_buf = refs[18:20]
+        s, local = refs[20:33], refs[33]
         p = Place()
         loads = [load(act_ref, a_buf, local.at[0]), load(wp_ref, w_buf, local.at[1])]
         ins = [
@@ -1196,34 +1396,53 @@
             load(kv_ref, kv_buf, local.at[3]),
             load(g_ref, g_buf, local.at[4]),
         ]
+
+        def h_fetch(i):
+            return load(h_ref.at[:, pl.ds(i * part, part)], h_buf.at[i % 2], local.at[5 + i % 2])
+
+        tiles = [h_fetch(0)]
         p.greet()
         for copy in loads:
             copy.wait()
-
-        def idle(stream):
-            if stream == 0:
-                for copy in ins:
-                    copy.wait()
-            attend_stream_back(
-                docs_ref,
-                stream,
-                q_buf.at[:, stream],
-                kv_buf.at[:, stream],
-                g_buf.at[:, stream],
-                lse_ref.at[stream],
-                gq_buf.at[:, stream],
-                gkv_buf.at[:, stream],
-                gk,
-                gv,
-                heads,
-            )
-
-        def idle_all():
+        stores = []
+
+        def idle():
+            for copy in ins:
+                copy.wait()
             for stream in range(streams):
-                idle(stream)
-
-        Scatter.take(p, own, s).run(plain_product(a_buf, w_buf), out_ref, idle_all)
-        stores = [load(gq_buf, gq_out, local.at[5]), load(gkv_buf, gkv_out, local.at[6])]
+                attend_stream_back(
+                    docs_ref,
+                    stream,
+                    q_buf.at[:, stream],
+                    kv_buf.at[:, stream],
+                    g_buf.at[:, stream],
+                    lse_ref.at[stream],
+                    grad_buf.at[:, stream, :, pl.ds(0, cols)],
+                    grad_buf.at[:, stream, :, pl.ds(cols, kv_cols)],
+                    gk,
+                    gv,
+                    heads,
+                )
+            stores.append(load(grad_buf.at[:, :, :, pl.ds(0, cols)], gq_out, local.at[7]))
+            stores.append(load(grad_buf.at[:, :, :, pl.ds(cols, kv_cols)], gkv_out, local.at[8]))
+            grad = grad_buf[...].reshape(total, cols + kv_cols)
+            sums = jnp.sum(grad.astype(f32), axis=0, keepdims=True)
+            gq_sum[...] = sums[:, :cols]
+            gkv_sum[...] = sums[:, cols:]
+            for i in range(PLANE):
+                tiles[i].wait()
+                if i + 1 < PLANE:
+                    tiles.append(h_fetch(i + 1))
+                term = dot_tn(h_buf[i % 2], grad).astype(bf16)
+                dwq_buf[i] = term[:, :cols].reshape(layers, part // layers, cols)
+                dwkv_buf[i] = term[:, cols:]
+            stores.append(load(dwq_buf, dwq_out, local.at[9]))
+            stores.append(load(dwkv_buf, dwkv_out, local.at[10]))
+
+        def emit(line, value):
+            out_ref[line, :] = residual_ref[line, :] + value + bias_ref[...]
+
+        Scatter.take(p, own, s).run(plain_product(a_buf, w_buf), emit, idle)
         for copy in stores:
             copy.wait()
 
@@ -1232,27 +1451,37 @@
         out_shape=[
             jax.ShapeDtypeStruct(queries.shape, bf16),
             jax.ShapeDtypeStruct(keyval.shape, bf16),
+            jax.ShapeDtypeStruct((1, cols), f32),
+            jax.ShapeDtypeStruct((1, kv_cols), f32),
+            jax.ShapeDtypeStruct((PLANE, layers, part // layers, cols), bf16),
+            jax.ShapeDtypeStruct((PLANE, part, kv_cols), bf16),
             jax.ShapeDtypeStruct((own, wide), f32),
         ],
-        in_specs=[pl.BlockSpec(memory_space=pltpu.SMEM)] + [ANY] * 3 + [WHOLE] + [ANY] * 2,
-        out_specs=[ANY, ANY, WHOLE],
+        in_specs=[pl.BlockSpec(memory_space=pltpu.SMEM)]
+        + [ANY] * 3
+        + [WHOLE]
+        + [ANY] * 3
+        + [WHOLE] * 2,
+        out_specs=[ANY, ANY, WHOLE, WHOLE, ANY, ANY, WHOLE],
         scratch_shapes=[
             pltpu.VMEM(act.shape, bf16),
             pltpu.VMEM(wp.shape, bf16),
             pltpu.VMEM(queries.shape, bf16),
             pltpu.VMEM(keyval.shape, bf16),
             pltpu.VMEM(grads.shape, bf16),
-            pltpu.VMEM(queries.shape, bf16),
-            pltpu.VMEM(keyval.shape, bf16),
+            pltpu.VMEM((groups, streams, rows, cols + kv_cols), bf16),
             pltpu.VMEM((length, HD), f32),
             pltpu.VMEM((length, HD), f32),
+            pltpu.VMEM((2, total, part), bf16),
+            pltpu.VMEM((PLANE, layers, part // layers, cols), bf16),
+            pltpu.VMEM((PLANE, part, kv_cols), bf16),
         ]
         + Scatter.scratch(own, wide)
-        + [sems(7)],
+        + [sems(11)],
         compiler_params=params(number),
         cost_estimate=cost(2 * total * depth * wide),
         name="attend_back_scatter_proj",
-    )(docs, queries, keyval, grads, lse, act, wp)
+    )(docs, queries, keyval, grads, lse, act, wp, hidden1, residual, b_proj)
 
 
 def pack_vectors(vectors):
@@ -1317,40 +1546,39 @@
     my_hidden = hidden // PLANE
     total = PLANE * own
 
-    inputs = tokens.reshape(own, width).astype(f32)
+    own_tokens = tokens.reshape(own, width)
     cot_low = cotangent.reshape(own, width)
-    cot_full = cot_low.astype(f32)
-
-    wq_pieces, wf_pieces, low_kv, wo = split_weights(w_query, w_fc, w_kv, w_out, layers, 1)
+
+    def row(vector):
+        return vector.reshape(1, -1)
+
+    wq_pieces, wf_pieces, low_kv, wo, low_hidden1, mean1, inverse1 = split_weights(
+        own_tokens, row(ln1_gain), row(ln1_bias), w_query, w_fc, w_kv, w_out, layers, 1
+    )
     wf = line_gather(wf_pieces, 1).reshape(width, my_hidden)
     wp = line_gather(w_proj)
-    my_bq = lax.dynamic_slice_in_dim(b_query, me * my_cols, my_cols, 0).reshape(1, my_cols)
-    my_bf = lax.dynamic_slice_in_dim(b_fc, me * my_hidden, my_hidden, 0).reshape(1, my_hidden)
-    bkv = jnp.concatenate([jnp.zeros((HD,), f32), b_value]).reshape(1, 2 * HD)
-
-    shifted1, normed1, inverse1 = normalize(inputs, ln1_gain, ln1_bias)
-    hidden1, w_kv_all, wq = gather_hidden1(shifted1.astype(bf16), low_kv, wq_pieces, layers, 2)
+    my_bq = row(lax.dynamic_slice_in_dim(b_query, me * my_cols, my_cols, 0))
+    my_bf = row(lax.dynamic_slice_in_dim(b_fc, me * my_hidden, my_hidden, 0))
+    bkv = row(jnp.concatenate([jnp.zeros((HD,), f32), b_value]))
+
+    hidden1, w_kv_all, wq = gather_hidden1(low_hidden1, low_kv, wq_pieces, layers, 2)
     wq = wq.reshape(width, my_cols)
     cot_all, queries, keyval, mixed, lse = project_attend(
         doc_starts, hidden1, wq, w_kv_all, my_bq, bkv, cot_low, streams, heads, 3
     )
     mixed_rows = mixed.reshape(total, my_cols)
-    residual = inputs + scatter_attn(mixed_rows, wo, 4) + b_out
-    shifted2, normed2, inverse2 = normalize(residual, ln2_gain, ln2_bias)
-    hidden2, act_low, slope, grad_w_proj = gather_fc(shifted2.astype(bf16), wf, my_bf, cot_all, 5)
+    residual, low_hidden2, mean2, inverse2 = scatter_attn(
+        mixed_rows, wo, own_tokens, row(b_out), row(ln2_gain), row(ln2_bias), 4
+    )
+    hidden2, act_low, slope, grad_w_proj = gather_fc(low_hidden2, wf, my_bf, cot_all, 5)
     shard_proj = line_scatter(grad_w_proj)
-    grad_b_proj = jnp.sum(cot_full, axis=0)
-
-    grad_hidden2, my_grad_b_fc, grad_w_fc = scatter_fc(cot_all, slope, wp, wf, hidden2, 6)
+
+    grad_residual, grad_attn, sums2, my_grad_b_fc, grad_w_fc = scatter_fc(
+        cot_all, slope, wp, wf, hidden2, cot_low, residual, mean2, inverse2, row(ln2_gain), 6
+    )
     fc_pieces = column_weight_grad(grad_w_fc, PLANE)
-    back_second, grad_ln2_gain, grad_ln2_bias = normalize_back(
-        grad_hidden2, normed2, inverse2, ln2_gain
-    )
-    grad_residual = cot_full + back_second
-    grad_attn = grad_residual.astype(bf16)
-    grad_b_out = jnp.sum(grad_attn.astype(f32), axis=0)
     grad_mixed, grad_w_out = gather_out(grad_attn, wo, mixed_rows, 7)
-    gq, gkv, mlp = attend_back_scatter_proj(
+    gq, gkv, my_grad_b_query, sums_kv, grad_w_query, grad_w_kv, output = attend_back_scatter_proj(
         doc_starts,
         queries,
         keyval,
@@ -1358,40 +1586,45 @@
         lse,
         act_low,
         wp,
+        hidden1,
+        residual,
+        row(b_proj),
+        layers,
         heads,
         8,
     )
-    output = residual + mlp + b_proj
-    gq_rows = gq.reshape(total, my_cols)
-    gkv_rows = gkv.reshape(total, 2 * HD)
-    grad_hidden1, query_pieces, grad_w_kv, shard_out = scatter_query(
-        gq_rows, gkv_rows, wq, w_kv_all, hidden1, grad_w_out, layers, 9
-    )
-    my_grad_b_query = jnp.sum(gq_rows.astype(f32), axis=0)
-    grad_b_value = jnp.sum(gkv_rows[:, HD:].astype(f32), axis=0)
-    back_first, grad_ln1_gain, grad_ln1_bias = normalize_back(
-        grad_hidden1, normed1, inverse1, ln1_gain
-    )
-    input_grad = grad_residual + back_first
+    input_grad, sums1, shard_out, shard_query, shard_kv = scatter_query(
+        gq.reshape(total, my_cols),
+        gkv.reshape(total, 2 * HD),
+        wq,
+        w_kv_all,
+        grad_w_out,
+        grad_w_query,
+        grad_w_kv,
+        (own_tokens, mean1, inverse1, row(ln1_gain), grad_residual),
+        layers,
+        9,
+    )
+
     zero = jnp.zeros_like
-    grad_b_query = lax.dynamic_update_slice_in_dim(zero(b_query), my_grad_b_query, me * my_cols, 0)
+    grad_b_query = lax.dynamic_update_slice_in_dim(
+        zero(b_query), my_grad_b_query.reshape(-1), me * my_cols, 0
+    )
     grad_b_fc = lax.dynamic_update_slice_in_dim(
         zero(b_fc), my_grad_b_fc.reshape(-1), me * my_hidden, 0
     )
     vectors = (
-        grad_ln1_gain,
-        grad_ln1_bias,
+        sums1[0],
+        sums1[1],
         grad_b_query,
-        grad_b_value,
-        grad_b_out,
-        grad_ln2_gain,
-        grad_ln2_bias,
+        sums_kv[0, HD:],
+        sums2[2],
+        sums2[0],
+        sums2[1],
         grad_b_fc,
-        grad_b_proj,
-    )
-    packed, shard_kv, shard_fc, shard_query = last_exchange(
-        pack_vectors(vectors), fc_pieces, query_pieces, grad_w_kv, layers, 10
-    )
+        sums2[3],
+    )
+    packed, shard_fc = last_exchange(pack_vectors(vectors), fc_pieces, layers, 10)
     sums = unpack_vectors(packed, vectors)
     return (
         output.reshape(streams, rows, width),

time: 510 us -> 492 us (0.965)
  other arithmetic: 25.9 us -> 5.07 us
    reduce_sum x10 -> x0, other arithmetic: 14.2 us -> none  [the longest x2 5.28 us: normalize_back(): jnp.sum(grad_out * normed, axis=0)]
  transfers between devices with their start and end apart: 4 -> 4, of which waited for: 0 -> 0; matrix products, arithmetic and copies ran while one was open for 4% -> 1% of each run, Pallas kernels for 79% -> 82%
where the time goes in v5:
time: 492 us; the launch traced here: 482 us
  Pallas kernels  447 us (91%)
  local copies, waits for them, and re-layouts  14.6 us (3%)
  between operations  14.5 us (3%)
  other arithmetic  5.07 us (1%)
    pallas_call x1, Pallas kernels, scatter_query(): pl.pallas_call(kernel, out_shape=[jax.ShapeDtypeStruct((rows, depth), f32...  68.6 us
    pallas_call x1, Pallas kernels, scatter_fc(): pl.pallas_call(kernel, out_shape=[jax.ShapeDtypeStruct((rows, depth), f32...  55.6 us
    pallas_call x1, Pallas kernels, gather_fc(): pl.pallas_call(kernel, out_shape=[jax.ShapeDtypeStruct((total, depth), bf...  51.2 us
    pallas_call x1, Pallas kernels, attend_back_scatter_proj(): pl.pallas_call(kernel, out_shape=[jax.ShapeDtypeStruct(queries.shape, bf1...  47.7 us
    pallas_call x1, Pallas kernels, gather_hidden1(): pl.pallas_call(kernel, out_shape=[jax.ShapeDtypeStruct((PLANE * hidden1.s...  45.7 us
    pallas_call x1, Pallas kernels, scatter_attn(): pl.pallas_call(kernel, out_shape=[jax.ShapeDtypeStruct((rows, wide), f32)...  45.3 us
    pallas_call x1, Pallas kernels, project_attend(): pl.pallas_call(kernel, out_shape=[jax.ShapeDtypeStruct((PLANE * cot.shape...  41.4 us
    pallas_call x1, Pallas kernels, gather_out(): pl.pallas_call(kernel, out_shape=[jax.ShapeDtypeStruct((total, wide), bf1...  40.8 us
  transfers between devices with their start and end apart: 4, of which 0 were waited for; matrix products, arithmetic and copies ran while one was open for 1% of the time, Pallas kernels for 82%

profile of v5, /device:TPU:0, one launch (start us, length us, event | category | flops | bytes accessed | tf_op | source)
XLA Modules:
  0.0 482.1 jit_solution(6892316769256814149)
XLA Ops:
  7.2 29.7 %split_weights.1 = (bf16[8,64,256]{2,1,0:T(8,128)(2,1)}, bf16[8,64,1024]{2,1,0:T(8,128)(2,1)}, bf16[256,256]{1,0:T(8,128)(2,1)}, bf16[256,2048]{1,0:T(8,128)(2,1...) custom-call(bf16[256,2048]{1,0:T(8,128)(2,1)} %bitcast.35, f32[1,2048]{1,0:T(1,128)} %bitcast.49, ...), custom_call_target="tpu_custom_call" | custom-call | tf_op jit(solution)/shard_map/split_weights/pallas_call | solution.py:571
  37.0 0.7 all-gather.5.cloned.1.call-update
  37.8 1.3 dynamic_slice.6
  39.7 1.3 dynamic_slice.7
  41.0 45.7 %gather_hidden1.1 = (bf16[2048,2048]{1,0:T(8,128)(2,1)}, bf16[2048,256]{1,0:T(8,128)(2,1)}, bf16[8,4,64,256]{3,2,1,0:T(8,128)(2,1)}) custom-call(bf16[256,2048]{1,0:T(8,128)(2,1)} %get-tuple-element.61.h_ref, bf16[256,256]{1,0:T(8,128)(2,1)} %get-tuple-element.62.kv_ref, bf16[8,64,256]{2,1,0:T(8,128)(2,1)} %get-tuple-element.63.wq_ref), custom_call_target="tpu_custom_call" | custom-call | tf_op jit(solution)/shard_map/gather_hidden1/pallas_call | solution.py:623
  86.6 41.4 %project_attend.1 = (bf16[2048,2048]{1,0:T(8,128)(2,1)}, bf16[8,2,128,256]{3,2,1,0:T(8,128)(2,1)}, bf16[8,2,128,256]{3,2,1,0:T(8,128)(2,1)}, bf16[8,2,128,256]{3,2,1,0:T(8,128)(2,1)}, f32[2,2,1024]{2,1,0:T(2,128)}) custom-call(s32[2,4]{1,0:T(2,128)} %docs_ref.3, bf16[2048,2048]{1,0:T(8,128)(2,1)} %get-tuple-element.64.h_ref, bf16[2048,256]{1,0:T(8,128)(2,1)} %bitcast.60, ...), custom_call_target="tpu_custom_call" | custom-call | flops 4294967296 | bytes 41943040 | tf_op jit(solution)/shard_map/project_attend/pallas_call | solution.py:700
  128.0 45.3 %scatter_attn.1 = (f32[256,2048]{1,0:T(8,128)}, bf16[256,2048]{1,0:T(8,128)(2,1)}, f32[256,1]{1,0:T(8,128)}, f32[256,1]{1,0:T(8,128)}) custom-call(bf16[2048,256]{1,0:T(8,128)(2,1)} %bitcast.67, bf16[256,2048]{1,0:T(8,128)(2,1)} %get-tuple-element.71.w_ref, bf16[256,2048]{1,0:T(8,128)(2,1)} %bitcast.36, f32[1,2048]{1,0:T(1,128)} %bitcast.62, ...), custom_call_target="tpu_custom_call" | custom-call | flops 2147483648 | bytes 41943040 | tf_op jit(solution)/shard_map/scatter_attn/pallas_call | solution.py:938
  173.3 51.2 %gather_fc.1 = (bf16[2048,2048]{1,0:T(8,128)(2,1)}, bf16[2048,1024]{1,0:T(8,128)(2,1)}, bf16[2048,1024]{1,0:T(8,128)(2,1)}, bf16[1024,2048]{1,0:T(8,128)(2,1)}) custom-call(bf16[256,2048]{1,0:T(8,128)(2,1)} %get-tuple-element.72.own_ref, bf16[2048,1024]{1,0:T(8,128)(2,1)} %bitcast.56, f32[1,1024]{1,0:T(1,128)} %bitcast.51, ...), custom_call_target="tpu_custom_call" | custom-call | flops 17179869184 | bytes 41943040 | tf_op jit(solution)/shard_map/gather_fc/pallas_call | solution.py:806
  224.7 55.6 %scatter_fc.1 = (f32[256,2048]{1,0:T(8,128)}, bf16[256,2048]{1,0:T(8,128)(2,1)}, f32[4,2048]{1,0:T(4,128)}, f32[1,1024]{1,0:T(1,128)}, bf16[2048,1024]{1,0:T(8,128)(2,1)}) custom-call(bf16[2048,2048]{1,0:T(8,128)(2,1)} %get-tuple-element.69.cot_ref, bf16[2048,1024]{1,0:T(8,128)(2,1)} %get-tuple-element.74.slope_ref, ...), custom_call_target="tpu_custom_call" | custom-call | flops 25769803776 | bytes 41943040 | tf_op jit(solution)/shard_map/scatter_fc/pallas_call | solution.py:1073
  281.3 40.8 %gather_out.1 = (bf16[2048,256]{1,0:T(8,128)(2,1)}, bf16[256,2048]{1,0:T(8,128)(2,1)}) custom-call(bf16[256,2048]{1,0:T(8,128)(2,1)} %get-tuple-element.79.own_ref, bf16[256,2048]{1,0:T(8,128)(2,1)} %get-tuple-element.71.w_ref, bf16[2048,256]{1,0:T(8,128)(2,1)} %bitcast.68), custom_call_target="tpu_custom_call" | custom-call | flops 4294967296 | bytes 41943040 | tf_op jit(solution)/shard_map/gather_out/pallas_call | solution.py:884
  322.1 47.7 %attend_back_scatter_proj.1 = (bf16[8,2,128,256]{3,2,1,0:T(8,128)(2,1)}, bf16[8,2,128,256]{3,2,1,0:T(8,128)(2,1)}, f32[1,256]{1,0:T(1,128)}, f32[1,256]{1,0:T(1,...) custom-call(s32[2,4]{1,0:T(2,128)} %docs_ref.3, ...), custom_call_target="tpu_custom_call" | custom-call | flops 8589934592 | bytes 41943040 | tf_op jit(solution)/shard_map/attend_back_scatter_proj/pallas_call | solution.py:1449
  369.8 0.9 dynamic_update_slice.6
  370.7 68.6 %scatter_query.1 = (f32[256,2048]{1,0:T(8,128)}, f32[2,2048]{1,0:T(2,128)}, f32[64,2048]{1,0:T(8,128)}, bf16[64,2048]{1,0:T(8,128)(2,1)}, f32[64,256]{1,0:T(8,128)}) custom-call(bf16[2048,256]{1,0:T(8,128)(2,1)} %bitcast.69, bf16[2048,256]{1,0:T(8,128)(2,1)} %bitcast.70, bf16[2048,256]{1,0:T(8,128)(2,1)} %bitcast.61, ...), custom_call_target="tpu_custom_call" | custom-call | flops 4294967296 | bytes 41943040 | tf_op jit(solution)/shard_map/scatter_query/pallas_call | solution.py:1202
  439.3 0.9 fusion.2
  441.0 21.0 %last_exchange.1 = (f32[8,24,128]{2,1,0:T(8,128)}, bf16[64,8192]{1,0:T(8,128)(2,1)}) custom-call(f32[8,24,128]{2,1,0:T(8,128)} %bitcast.38, bf16[8,64,1024]{2,1,0:T(8,128)(2,1)} %reduce-scatter.5.cloned.1.call-done.fc_ref), custom_call_target="tpu_custom_call" | custom-call | tf_op jit(solution)/shard_map/last_exchange/pallas_call | solution.py:1277
  462.0 1.4 fusion
  463.4 1.4 slice.71
  464.8 1.2 slice.67
  466.0 2.7 convert_element_type.10
  468.7 0.8 convert_element_type.9
  469.5 1.6 convert_element_type.11
  471.1 1.3 copy.48
  472.4 1.3 copy.49
  474.4 0.8 copy.51
  (49 shorter events, 3.2 us)
Async XLA Ops:
  7.2 31.9 %copy-start.9 = (f32[128]{0:T(128)S(1)}, f32[128]{0:T(128)}, u32[]{:S(2)}) copy-start(f32[128]{0:T(128)} %param.27) | copy-start | bytes 1540
  7.2 166.1 %all-gather.3.cloned.1.call-start = ((), (), s32[]{:S(2)}) async-start(), calls=%async_computation.2 | async-start | bytes 5242880 | tf_op jit(solution)/shard_map/all_gather | solution.py:1508
  37.0 187.7 %all-gather.5.cloned.1.call-start = ((), (), s32[]{:S(2)}) async-start(), calls=%async_computation.3 | async-start | bytes 5242880 | tf_op jit(solution)/shard_map/all_gather | solution.py:1508
  37.7 284.4 %reduce-scatter.3.cloned.1.call-start = ((), (), s32[]{:S(2)}) async-start(), calls=%async_computation.4 | async-start | bytes 5242880 | tf_op jit(solution)/shard_map/reduce_scatter | solution.py:1512
  224.6 215.8 %reduce-scatter.5.cloned.1.call-start = ((), (), s32[]{:S(2)}) async-start(), calls=%async_computation.5 | async-start | bytes 5242880 | tf_op jit(solution)/shard_map/reduce_scatter | solution.py:1512
  280.3 0.7 copy-start.8
  281.3 40.8 %copy-start.7 = (f32[4,2048]{1,0:T(4,128)S(1)}, f32[4,2048]{1,0:T(4,128)}, u32[]{:S(2)}) copy-start(f32[4,2048]{1,0:T(4,128)} %get-tuple-element.101) | copy-start | bytes 98308
  370.7 69.5 %copy-start.10 = (f32[1,256]{1,0:T(1,128)S(1)}, f32[1,256]{1,0:T(1,128)}, u32[]{:S(2)}) copy-start(f32[1,256]{1,0:T(1,128)} %get-tuple-element.100) | copy-start | bytes 3076
  439.3 29.4 %copy-start.4 = (bf16[64,2048]{1,0:T(8,128)(2,1)S(1)}, bf16[64,2048]{1,0:T(8,128)(2,1)}, u32[]{:S(2)}) copy-start(bf16[64,2048]{1,0:T(8,128)(2,1)} %get-tuple-element.95) | copy-start | bytes 786436
  439.3 30.2 %copy-start.2 = (bf16[256,2048]{1,0:T(8,128)(2,1)S(1)}, bf16[256,2048]{1,0:T(8,128)(2,1)}, u32[]{:S(2)}) copy-start(bf16[256,2048]{1,0:T(8,128)(2,1)} %reduce-scatter.3.cloned.1.call-done) | copy-start | bytes 3145732
  440.3 0.6 copy-start.5
  441.0 30.1 %copy-start = (f32[256,2048]{1,0:T(8,128)S(1)}, f32[256,2048]{1,0:T(8,128)}, u32[]{:S(2)}) copy-start(f32[256,2048]{1,0:T(8,128)} %get-tuple-element.85) | copy-start | bytes 6291460
  468.7 3.7 copy-start.1
  471.1 2.6 copy-start.6
  471.1 3.3 copy-start.3
Sparse Core Ops, SparseCore 0:
  37.1 97.9 all-gather.2
  136.7 78.9 all-gather.4
  224.7 83.6 reduce-scatter.2
  310.7 79.5 reduce-scatter.4
